TPU v7x, 1024 devices: a whole 4x8x16 slice. The times are simulated.
1024 devices in a mesh: ctx: 128 (over x, z, core), head: 8 (over y).
Axes of the slice: x: 4, y: 8, z: 16, core: 2. Of those that a mesh axis runs over, the one named last changes fastest.
Arguments:
- queries: bfloat16 [16384, 6144], P('ctx', 'head'), may hold values from -6 to 6
- key_input: bfloat16 [16384, 6144], P('ctx', 'head'), may hold values from -6 to 6
- value_input: bfloat16 [16384, 6144], P('ctx', 'head'), may hold values from -6 to 6
- norm_gain: float32 [6144], P('head'), may hold values from 0.5 to 1.5
- cotangent: bfloat16 [16384, 6144], P('ctx', 'head'), may hold values from -6 to 6
Outputs:
- attended: bfloat16 [16384, 6144], P('ctx', 'head')
- grad_query: bfloat16 [16384, 6144], P('ctx', 'head')
- grad_key: bfloat16 [16384, 6144], P('ctx', 'head')
- grad_value: bfloat16 [16384, 6144], P('ctx', 'head')
All inputs are finite; a program needn't handle non-finite values.
Results may differ from a plain program's by a relative error of at most 0.0065.
Values sent between devices are 32-bit elements; how exact they have to be, the bound alone decides.
No kernel may reach another device: no remote copies, remote signals or barrier semaphores. Data moves between devices by JAX's collectives and lax.ppermute only.
A program may use at most 128 MiB of HBM per device.

v0:
```python
import jax
import jax.numpy as jnp
from jax import lax
from jax.sharding import PartitionSpec as P

HEAD_DIM = 96
D = 6144


epsilon = 1e-06


def prefix_2(part, axis, combine, identity):
    place = lax.axis_index(axis)
    gathered = lax.all_gather(part, axis)
    state = jnp.zeros_like(part) + jnp.asarray(identity, part.dtype)

    def one(turn, state):
        return combine(state, lax.dynamic_index_in_dim(gathered, turn, 0, False))

    return lax.fori_loop(0, place, one, state)


def add_states(earlier, later):
    return earlier + later


def silu_slope(x):
    sig = jax.nn.sigmoid(x)
    return sig * (1.0 + x * (1.0 - sig))


def per_device(queries, key_input, value_input, norm_gain, cotangent):
    tok_rows = queries.shape[0]
    heads_here = queries.shape[1] // HEAD_DIM
    shape3 = (tok_rows, heads_here, HEAD_DIM)
    q_float = queries.astype(jnp.float32)
    k_float = key_input.astype(jnp.float32)
    q_feat = jax.nn.silu(q_float).astype(jnp.bfloat16).reshape(shape3)
    k_feat = jax.nn.silu(k_float).astype(jnp.bfloat16).reshape(shape3)
    values = value_input.reshape(shape3)
    causal = jnp.arange(tok_rows)[:, None] >= jnp.arange(tok_rows)[None, :]
    local_state = jnp.einsum("shd,she->hde", k_feat, values, preferred_element_type=jnp.float32)
    empty = jnp.zeros_like(local_state)
    prefix = prefix_2(local_state, "ctx", add_states, empty)
    prefix_low = prefix.astype(jnp.bfloat16)
    scores = jnp.einsum("thd,shd->hts", q_feat, k_feat, preferred_element_type=jnp.float32)
    attn_low = jnp.where(causal[None], scores, 0.0).astype(jnp.bfloat16)
    raw = jnp.einsum("hts,shd->thd", attn_low, values, preferred_element_type=jnp.float32)
    raw = raw + jnp.einsum("thd,hde->the", q_feat, prefix_low, preferred_element_type=jnp.float32)
    raw = raw.reshape(tok_rows, heads_here * HEAD_DIM)
    upstream = cotangent.astype(jnp.float32) * norm_gain[None, :]
    square_part = jnp.sum(raw * raw, axis=1)
    cross_part = jnp.sum(upstream * raw, axis=1)
    square_total = lax.psum(square_part, "head")
    rms = jnp.sqrt(square_total / D + epsilon)
    attended = (raw / rms[:, None] * norm_gain[None, :]).astype(jnp.bfloat16)
    cross_total = lax.psum(cross_part, "head")
    d_raw = (upstream - raw * (cross_total / (D * rms * rms))[:, None]) / rms[:, None]
    d_raw = d_raw.astype(jnp.bfloat16).reshape(shape3)
    local_grad = jnp.einsum("thd,the->hde", q_feat, d_raw, preferred_element_type=jnp.float32)
    before = prefix_2(local_grad, "ctx", add_states, empty)
    whole_sum = lax.psum(local_grad, "ctx")
    later = whole_sum - before - local_grad
    later_low = later.astype(jnp.bfloat16)
    back = jnp.einsum("the,she->hts", d_raw, values, preferred_element_type=jnp.float32)
    back_low = jnp.where(causal[None], back, 0.0).astype(jnp.bfloat16)
    grad_qf = jnp.einsum("hts,shd->thd", back_low, k_feat, preferred_element_type=jnp.float32)
    grad_qf = grad_qf + jnp.einsum(
        "the,hde->thd", d_raw, prefix_low, preferred_element_type=jnp.float32
    )
    grad_kf = jnp.einsum("hts,thd->shd", back_low, q_feat, preferred_element_type=jnp.float32)
    grad_kf = grad_kf + jnp.einsum(
        "she,hde->shd", values, later_low, preferred_element_type=jnp.float32
    )
    grad_vf = jnp.einsum("hts,the->she", attn_low, d_raw, preferred_element_type=jnp.float32)
    grad_vf = grad_vf + jnp.einsum(
        "shd,hde->she", k_feat, later_low, preferred_element_type=jnp.float32
    )
    width_here = heads_here * HEAD_DIM
    grad_query = (grad_qf.reshape(tok_rows, width_here) * silu_slope(q_float)).astype(jnp.bfloat16)
    grad_key = (grad_kf.reshape(tok_rows, width_here) * silu_slope(k_float)).astype(jnp.bfloat16)
    grad_value = grad_vf.reshape(tok_rows, width_here).astype(jnp.bfloat16)
    return (attended, grad_query, grad_key, grad_value)


def solution(mesh):
    in_specs = (P("ctx", "head"), P("ctx", "head"), P("ctx", "head"), P("head"), P("ctx", "head"))
    out_specs = (P("ctx", "head"), P("ctx", "head"), P("ctx", "head"), P("ctx", "head"))
    return jax.shard_map(
        per_device, mesh=mesh, in_specs=in_specs, out_specs=out_specs, check_vma=False
    )
```

profile of v0, /device:TPU:1, one launch (start us, length us, event | category | flops | bytes accessed | tf_op | source)
XLA Modules:
  0.0 1025.5 jit_solution(14162914996569096159)
XLA Ops:
  7.2 0.0 all-gather.5.cloned.1.call-start
  7.2 1.1 copy.44
  8.3 0.1 fusion.15
  8.4 1.1 copy.45
  9.5 1.0 fusion.29
  10.5 0.0 all-gather.5.cloned.1.call-update
  10.5 0.0 all-gather.7.cloned.1.call-start
  10.6 1.1 copy.43
  11.7 1.1 copy.47
  12.8 0.1 fusion.7
  12.9 0.3 fusion.1
  13.2 0.3 convolution_bitcast_fusion.1
  13.5 261.6 %all-gather.5.cloned.1.call-done = f32[1024,96,96]{2,1,0:T(8,128)} async-done(((f32[8,96,96]{2,1,0:T(8,128)}), f32[1024,96,96]{2,1,0:T(8,128)}) %all-gather.5.cloned.1.call-update) | async-done | bytes 37748752 | tf_op jit(solution)/shard_map/all_gather | solution.py:15
  275.2 1.1 while.20
  275.2 1.1 bitcast_add_fusion.4
  276.3 0.3 multiply_reduce_fusion
  276.6 0.9 fusion.22
  277.5 13.2 %all-reduce = (f32[128]{0:T(128)S(1)}, f32[128]{0:T(128)S(1)}) all-reduce(f32[128]{0:T(128)S(1)} %get-tuple-element.86, f32[128]{0:T(128)S(1)} %fusion.22), channel_id=1, replica_groups=mesh['ctx'=128,'head'=8] {'head'}, use_global_device_ids=true, to_apply=%region_3.4 | all-reduce | flops 256 | bytes 2048 | tf_op jit(solution)/shard_map/psum | solution.py:55
  290.7 0.9 fusion.25
  291.6 1.0 fusion.32
  292.6 0.0 all-gather.7.cloned.1.call-update
  292.6 0.0 all-reduce.3.cloned.1.call-start
  292.7 0.3 fusion.2
  293.0 0.3 fusion.30
  293.2 0.2 convolution_add_fusion.2
  293.4 0.2 fusion.11
  293.6 0.8 copy.50
  294.4 0.8 copy.49
  295.3 0.2 fusion.33
  295.5 0.2 fusion.31
  295.7 0.0 all-reduce.3.cloned.1.call-update
  295.7 381.3 %all-gather.7.cloned.1.call-done = f32[1024,96,96]{2,1,0:T(8,128)} async-done(((f32[8,96,96]{2,1,0:T(8,128)}), f32[1024,96,96]{2,1,0:T(8,128)}) %all-gather.7.cloned.1.call-update) | async-done | bytes 37748752 | tf_op jit(solution)/shard_map/all_gather | solution.py:15
  677.0 1.1 while.21
  677.0 1.1 bitcast_add_fusion.5
  678.1 337.4 %all-reduce.3.cloned.1.call-done = f32[8,96,96]{2,1,0:T(8,128)} async-done(((f32[8,96,96]{2,1,0:T(8,128)}), f32[8,96,96]{2,1,0:T(8,128)}) %all-reduce.3.cloned.1.call-update) | async-done | bytes 294928 | tf_op jit(solution)/shard_map/psum | solution.py:63
  1015.5 1.2 subtract_convert_fusion
  1016.7 0.3 fusion.3
  1017.0 0.8 copy.52
  1017.8 0.2 convolution_add_fusion.1
  1018.0 0.2 fusion.19
  1018.2 0.8 copy.51
  (4 shorter events, 0.1 us)
Async XLA Ops:
  7.2 268.0 %all-gather.5.cloned.1.call-start = ((), (), s32[]{:S(2)}) async-start(), calls=%async_computation.1 | async-start | bytes 50724864 | tf_op jit(solution)/shard_map/all_gather | solution.py:15
  10.5 666.4 %all-gather.7.cloned.1.call-start = ((), (), s32[]{:S(2)}) async-start(), calls=%async_computation.2 | async-start | bytes 50724864 | tf_op jit(solution)/shard_map/all_gather | solution.py:15
  292.6 722.9 %all-reduce.3.cloned.1.call-start = ((), (), s32[]{:S(2)}) async-start(), calls=%async_computation | async-start | bytes 786432 | tf_op jit(solution)/shard_map/psum | solution.py:63
Sparse Core Ops, SparseCore 0:
  12.3 262.7 all-gather.4
  292.7 384.1 all-gather.6
  680.4 335.0 all-reduce.2
where the time goes:
time: 1040 us; the launch traced here: 1030 us
  waiting for transfers between devices  980 us (94%)
  between operations  13.9 us (1%)
  blocking collectives  13.2 us (1%)
    all_gather x2, waiting for transfers between devices, prefix_2(): gathered = lax.all_gather(part, axis)  643 us
    psum x1, waiting for transfers between devices, per_device(): whole_sum = lax.psum(local_grad, 'ctx')  337 us
  transfers between devices with their start and end apart: 3, of which 3 were waited for; matrix products, arithmetic and copies ran while one was open for 1% of the time, Pallas kernels for 0%

commit v1 on v0

--- a/solution.py
+++ b/solution.py
@@ -1,28 +1,57 @@
 import jax
 import jax.numpy as jnp
 from jax import lax
+from jax.experimental import pallas as pl
 from jax.sharding import PartitionSpec as P
 
 HEAD_DIM = 96
 D = 6144
-
+CHIPS = 64
+CORES = 2
 
 epsilon = 1e-06
 
 
-def prefix_2(part, axis, combine, identity):
-    place = lax.axis_index(axis)
-    gathered = lax.all_gather(part, axis)
-    state = jnp.zeros_like(part) + jnp.asarray(identity, part.dtype)
-
-    def one(turn, state):
-        return combine(state, lax.dynamic_index_in_dim(gathered, turn, 0, False))
-
-    return lax.fori_loop(0, place, one, state)
+def swap_cores(x):
+    pairs = [(i, i ^ 1) for i in range(CHIPS * CORES)]
+    return lax.ppermute(x, "ctx", pairs)
 
 
-def add_states(earlier, later):
-    return earlier + later
+def across_chips(x):
+    groups = [[chip * CORES + core for chip in range(CHIPS)] for core in range(CORES)]
+    return lax.all_to_all(x, "ctx", 0, 0, axis_index_groups=groups)
+
+
+def rounded(here_ref, there_ref, out_ref):
+    core = lax.axis_index("ctx") % CORES
+    here, there = here_ref[...], there_ref[...]
+    out_ref[0] = jnp.where(core == 0, here, there).astype(jnp.bfloat16)
+    out_ref[1] = jnp.where(core == 0, there, here).astype(jnp.bfloat16)
+
+
+def exclusive(state, backward):
+    core = lax.axis_index("ctx") % CORES
+    halves = state.reshape(CORES, CHIPS, -1)
+    mine = lax.dynamic_index_in_dim(halves, core, 0, False)
+    theirs = lax.dynamic_index_in_dim(halves, 1 - core, 0, False)
+    received = swap_cores(theirs)
+    pieces = across_chips((mine + received)[:, None, :])[:, 0, :]
+    order = jnp.arange(CHIPS)
+    if backward:
+        before = order[:, None] < order[None, :]
+        first = core == 1
+    else:
+        before = order[:, None] > order[None, :]
+        first = core == 0
+    summed = jnp.dot(before.astype(jnp.float32), pieces, precision=lax.Precision.HIGHEST)
+    chip = across_chips(summed[:, None, :])[:, 0, :]
+    zero = jnp.zeros_like(mine)
+    here = chip + jnp.where(first, zero, received)
+    there = swap_cores(chip + jnp.where(first, mine, zero))
+    low = pl.pallas_call(
+        rounded, out_shape=jax.ShapeDtypeStruct((CORES,) + here.shape, jnp.bfloat16)
+    )(here, there)
+    return low.reshape(state.shape)
 
 
 def silu_slope(x):
@@ -41,28 +70,23 @@
     values = value_input.reshape(shape3)
     causal = jnp.arange(tok_rows)[:, None] >= jnp.arange(tok_rows)[None, :]
     local_state = jnp.einsum("shd,she->hde", k_feat, values, preferred_element_type=jnp.float32)
-    empty = jnp.zeros_like(local_state)
-    prefix = prefix_2(local_state, "ctx", add_states, empty)
-    prefix_low = prefix.astype(jnp.bfloat16)
+    prefix_low = exclusive(local_state, False)
     scores = jnp.einsum("thd,shd->hts", q_feat, k_feat, preferred_element_type=jnp.float32)
     attn_low = jnp.where(causal[None], scores, 0.0).astype(jnp.bfloat16)
     raw = jnp.einsum("hts,shd->thd", attn_low, values, preferred_element_type=jnp.float32)
     raw = raw + jnp.einsum("thd,hde->the", q_feat, prefix_low, preferred_element_type=jnp.float32)
     raw = raw.reshape(tok_rows, heads_here * HEAD_DIM)
     upstream = cotangent.astype(jnp.float32) * norm_gain[None, :]
-    square_part = jnp.sum(raw * raw, axis=1)
-    cross_part = jnp.sum(upstream * raw, axis=1)
-    square_total = lax.psum(square_part, "head")
+    parts = jnp.stack([jnp.sum(raw * raw, axis=1), jnp.sum(upstream * raw, axis=1)])
+    parts = jnp.broadcast_to(parts[None], (8,) + parts.shape)
+    totals = jnp.sum(lax.all_to_all(parts, "head", 0, 0), axis=0)
+    square_total, cross_total = totals[0], totals[1]
     rms = jnp.sqrt(square_total / D + epsilon)
     attended = (raw / rms[:, None] * norm_gain[None, :]).astype(jnp.bfloat16)
-    cross_total = lax.psum(cross_part, "head")
     d_raw = (upstream - raw * (cross_total / (D * rms * rms))[:, None]) / rms[:, None]
     d_raw = d_raw.astype(jnp.bfloat16).reshape(shape3)
     local_grad = jnp.einsum("thd,the->hde", q_feat, d_raw, preferred_element_type=jnp.float32)
-    before = prefix_2(local_grad, "ctx", add_states, empty)
-    whole_sum = lax.psum(local_grad, "ctx")
-    later = whole_sum - before - local_grad
-    later_low = later.astype(jnp.bfloat16)
+    later_low = exclusive(local_grad, True)
     back = jnp.einsum("the,she->hts", d_raw, values, preferred_element_type=jnp.float32)
     back_low = jnp.where(causal[None], back, 0.0).astype(jnp.bfloat16)
     grad_qf = jnp.einsum("hts,shd->thd", back_low, k_feat, preferred_element_type=jnp.float32)

time: 1040 us -> 159 us (0.15); the launches traced: 1030 us -> 159 us
  waiting for transfers between devices: 980 us -> 59.7 us
  starting transfers between devices: 0.12 us -> 60.4 us
  between operations: 13.9 us -> 0.95 us
    all_gather x2 -> x0, waiting for transfers between devices: 643 us -> none  [prefix_2(): gathered = lax.all_gather(part, axis)]
    psum x1 -> x0, waiting for transfers between devices: 337 us -> none  [per_device(): whole_sum = lax.psum(local_grad, 'ctx')]
    all_to_all x0 -> x4, waiting for transfers between devices: none -> 56.2 us  [across_chips(): return lax.all_to_all(x, 'ctx', 0, 0, axis_index_groups=groups)]
    ppermute x0 -> x4, starting transfers between devices: none -> 30.9 us  [swap_cores(): return lax.ppermute(x, 'ctx', pairs)]
    all_to_all x0 -> x4, starting transfers between devices: none -> 29.5 us  [across_chips(): return lax.all_to_all(x, 'ctx', 0, 0, axis_index_groups=groups)]
    psum x1 -> x0, blocking collectives: 13.2 us -> none  [per_device(): square_total = lax.psum(square_part, 'head')]
    all_to_all x0 -> x1, blocking collectives: none -> 13.2 us  [per_device(): totals = jnp.sum(lax.all_to_all(parts, 'head', 0, 0), axis=0)]
  transfers between devices with their start and end apart: 3 -> 8, of which waited for: 3 -> 8; matrix products, arithmetic and copies ran while one was open for 1% -> 3% of each run, Pallas kernels for 0% -> 0%
where the time goes in v1:
time: 159 us
  starting transfers between devices  60.4 us (38%)
  waiting for transfers between devices  59.7 us (38%)
  local copies, waits for them, and re-layouts  14.3 us (9%)
  blocking collectives  13.2 us (8%)
  Pallas kernels  3.39 us (2%)
  matrix products  3.38 us (2%)
  other arithmetic  3.37 us (2%)
    all_to_all x4, waiting for transfers between devices, across_chips(): return lax.all_to_all(x, 'ctx', 0, 0, axis_index_groups=groups)  56.2 us
    ppermute x4, starting transfers between devices, swap_cores(): return lax.ppermute(x, 'ctx', pairs)  30.9 us
    all_to_all x4, starting transfers between devices, across_chips(): return lax.all_to_all(x, 'ctx', 0, 0, axis_index_groups=groups)  29.5 us
    all_to_all x1, blocking collectives, per_device(): totals = jnp.sum(lax.all_to_all(parts, 'head', 0, 0), axis=0)  13.2 us
    unnamed x20, local copies, waits for them, and re-layouts  8.13 us
    ppermute x4, waiting for transfers between devices, swap_cores(): return lax.ppermute(x, 'ctx', pairs)  3.52 us
    pallas_call x2, Pallas kernels, exclusive(): pl.pallas_call(rounded, out_shape=jax.ShapeDtypeStruct((CORES,) + here.sh...  3.39 us
  transfers between devices with their start and end apart: 8, of which 8 were waited for; matrix products, arithmetic and copies ran while one was open for 3% of the time, Pallas kernels for 0%

profile of v1, /device:TPU:1, one launch (start us, length us, event | category | flops | bytes accessed | tf_op | source)
XLA Modules:
  0.0 158.6 jit_solution(8272459393126397335)
XLA Ops:
  0.6 1.1 copy.72
  1.7 0.0 copy-start
  1.7 0.1 fusion.15
  1.9 0.8 copy-done
  2.7 0.2 copy.73
  2.8 0.2 fusion.33
  3.1 0.2 reshape.82
  3.3 16.1 %collective-permute-start = (f32[64,576]{1,0:T(8,128)S(1)}, f32[64,576]{1,0:T(8,128)S(1)}, u32[]{:S(2)}, u32[]{:S(2)}) collective-permute-start(f32[64,576]{1,0:T(8,128)S(1)} %dynamic-slice_bitcast_fusion.1), channel_id=1, source_target_pairs={{0,8},{8,0},{16,24},{24,16},{32,40},{40,32},{48,56},{56,48},{64,72... | collective-permute-start | bytes 442376 | tf_op jit(solution)/shard_map/ppermute | solution.py:17
  19.4 1.0 collective-permute-done
  20.4 0.8 copy.74
  21.2 9.4 %all-to-all-start = ((f32[64,1,576]{2,1,0:T(1,128)}), f32[64,1,576]{2,1,0:T(1,128)S(1)}, u32[]{:S(2)}, u32[]{:S(2)}) async-start(f32[64,1,576]{2,1,0:T(1,128)} %copy.74), calls=%async_computation | async-start | bytes 327680 | tf_op jit(solution)/shard_map/all_to_all | solution.py:22
  30.7 0.0 copy-start.2
  30.7 0.2 copy.71
  30.8 0.8 copy-done.2
  31.6 0.2 copy.77
  31.8 14.7 %all-to-all-done = f32[64,1,576]{2,1,0:T(1,128)S(1)} async-done(((f32[64,1,576]{2,1,0:T(1,128)}), f32[64,1,576]{2,1,0:T(1,128)S(1)}, u32[]{:S(2)}, u32[]{:S(2)}) %all-to-all-start) | async-done | bytes 147488 | tf_op jit(solution)/shard_map/all_to_all | solution.py:22
  46.4 0.2 convolution_bitcast_fusion.3
  46.7 0.8 copy.75
  47.5 7.0 %all-to-all-start.1 = ((f32[64,1,576]{2,1,0:T(1,128)}), f32[64,1,576]{2,1,0:T(1,128)S(1)}, u32[]{:S(2)}, u32[]{:S(2)}) async-start(f32[64,1,576]{2,1,0:T(1,128)} %copy.75), calls=%async_computation.1 | async-start | bytes 327680 | tf_op jit(solution)/shard_map/all_to_all | solution.py:22
  54.5 0.1 fusion.7
  54.7 0.3 fusion.1
  55.0 14.3 %all-to-all-done.1 = f32[64,1,576]{2,1,0:T(1,128)S(1)} async-done(((f32[64,1,576]{2,1,0:T(1,128)}), f32[64,1,576]{2,1,0:T(1,128)S(1)}, u32[]{:S(2)}, u32[]{:S(2)}) %all-to-all-start.1) | async-done | bytes 147488 | tf_op jit(solution)/shard_map/all_to_all | solution.py:22
  69.2 0.7 bitcast_add_fusion.2
  69.9 5.4 %collective-permute-start.1 = (f32[64,576]{1,0:T(8,128)S(1)}, f32[64,576]{1,0:T(8,128)S(1)}, u32[]{:S(2)}, u32[]{:S(2)}) collective-permute-start(f32[64,576]{1,0:T(8,128)S(1)} %get-tuple-element.28), channel_id=1, source_target_pairs={{0,8},{8,0},{16,24},{24,16},{32,40},{40,32},{48,56},{56,48},{64,72... | collective-permute-start | bytes 442376 | tf_op jit(solution)/shard_map/ppermute | solution.py:17
  75.3 0.3 convolution_bitcast_fusion.1
  75.6 0.7 collective-permute-done.1.there_ref
  76.3 0.7 copy-done.4
  77.0 1.7 %shard_map.84 = bf16[2,64,576]{2,1,0:T(8,128)(2,1)} custom-call(f32[64,576]{1,0:T(8,128)} %get-tuple-element.29.here_ref, f32[64,576]{1,0:T(8,128)} %copy-done.4), custom_call_target="tpu_custom_call" | custom-call | tf_op jit(solution)/shard_map/pallas_call | solution.py:51
  78.7 1.2 reshape.83
  79.9 0.3 multiply_reduce_fusion
  80.3 0.4 copy-done.5
  80.6 0.2 fusion.20
  80.8 13.2 %all_to_all.25 = f32[8,2,128]{2,1,0:T(2,128)S(1)} all-to-all(f32[8,2,128]{2,1,0:T(2,128)S(1)} %broadcast_in_dim.53), channel_id=1, replica_groups=mesh['ctx'=128,'head'=8] {'head'}, dimensions={0} | all-to-all | bytes 16384 | tf_op jit(solution)/shard_map/all_to_all | solution.py:82
  94.1 0.2 fusion.25
  94.3 0.2 fusion.36
  94.5 0.2 reshape.87
  94.7 3.7 %collective-permute-start.2 = (f32[64,576]{1,0:T(8,128)S(1)}, f32[64,576]{1,0:T(8,128)S(1)}, u32[]{:S(2)}, u32[]{:S(2)}) collective-permute-start(f32[64,576]{1,0:T(8,128)S(1)} %dynamic-slice_bitcast_fusion), channel_id=1, source_target_pairs={{0,8},{8,0},{16,24},{24,16},{32,40},{40,32},{48,56},{56,48},{64,72... | collective-permute-start | bytes 442376 | tf_op jit(solution)/shard_map/ppermute | solution.py:17
  98.4 1.0 collective-permute-done.2
  99.5 0.8 copy.79
  100.3 5.8 %all-to-all-start.3 = ((f32[64,1,576]{2,1,0:T(1,128)}), f32[64,1,576]{2,1,0:T(1,128)S(1)}, u32[]{:S(2)}, u32[]{:S(2)}) async-start(f32[64,1,576]{2,1,0:T(1,128)} %copy.79), calls=%async_computation.3 | async-start | bytes 327680 | tf_op jit(solution)/shard_map/all_to_all | solution.py:22
  106.1 0.3 fusion.2
  106.4 0.3 fusion.34
  106.6 15.2 %all-to-all-done.3 = f32[64,1,576]{2,1,0:T(1,128)S(1)} async-done(((f32[64,1,576]{2,1,0:T(1,128)}), f32[64,1,576]{2,1,0:T(1,128)S(1)}, u32[]{:S(2)}, u32[]{:S(2)}) %all-to-all-start.3) | async-done | bytes 147488 | tf_op jit(solution)/shard_map/all_to_all | solution.py:22
  121.8 0.2 convolution_bitcast_fusion.2
  122.1 0.8 copy.80
  122.9 7.2 %all-to-all-start.4 = ((f32[64,1,576]{2,1,0:T(1,128)}), f32[64,1,576]{2,1,0:T(1,128)}, u32[]{:S(2)}, u32[]{:S(2)}) async-start(f32[64,1,576]{2,1,0:T(1,128)} %copy.80), calls=%async_computation.4 | async-start | bytes 327680 | tf_op jit(solution)/shard_map/all_to_all | solution.py:22
  130.2 0.2 convolution_add_fusion.2
  130.4 0.8 copy.82
  131.2 0.2 fusion.11
  131.4 0.8 copy.83
  132.2 0.2 fusion.35
  132.4 12.0 %all-to-all-done.4 = f32[64,1,576]{2,1,0:T(1,128)} async-done(((f32[64,1,576]{2,1,0:T(1,128)}), f32[64,1,576]{2,1,0:T(1,128)}, u32[]{:S(2)}, u32[]{:S(2)}) %all-to-all-start.4) | async-done | bytes 147488 | tf_op jit(solution)/shard_map/all_to_all | solution.py:22
  144.4 1.6 %bitcast_add_fusion = (f32[64,576]{1,0:T(8,128)S(1)}, f32[64,576]{1,0:T(8,128)}) fusion(f32[64,1,576]{2,1,0:T(1,128)} %all-to-all-done.4, f32[2,64,576]{2,1,0:T(8,128)S(1)} %reshape.87, s32[]{:T(128)S(6)} %select_n.49, pred[]{:T(512)S(6)} %eq.10, f32[64,576]{1,0:T(8,128)S(1)} %collective-permute-done.2), kind=kLoop, calls=%fused_computation.46 | loop fusion | flops 147456 | bytes 737285 | tf_op jit(solution)/shard_map/add | solution.py:50
  146.0 5.7 %collective-permute-start.3 = (f32[64,576]{1,0:T(8,128)S(1)}, f32[64,576]{1,0:T(8,128)S(1)}, u32[]{:S(2)}, u32[]{:S(2)}) collective-permute-start(f32[64,576]{1,0:T(8,128)S(1)} %get-tuple-element.26), channel_id=1, source_target_pairs={{0,8},{8,0},{16,24},{24,16},{32,40},{40,32},{48,56},{56,48},{64,72... | collective-permute-start | bytes 442376 | tf_op jit(solution)/shard_map/ppermute | solution.py:17
  151.8 0.2 fusion.37
  152.0 0.8 collective-permute-done.3.there_ref
  152.8 0.7 copy-done.3
  153.4 1.7 %shard_map.85 = bf16[2,64,576]{2,1,0:T(8,128)(2,1)} custom-call(f32[64,576]{1,0:T(8,128)} %get-tuple-element.27.here_ref, f32[64,576]{1,0:T(8,128)} %copy-done.3), custom_call_target="tpu_custom_call" | custom-call | tf_op jit(solution)/shard_map/pallas_call | solution.py:51
  155.1 1.2 reshape.88
  156.4 0.2 convolution_add_fusion.1
  156.6 0.2 fusion.19
  156.7 0.8 copy.84
  157.6 0.3 fusion.3
  157.8 0.8 copy.85
  (15 shorter events, 0.2 us)
Async XLA Ops:
  1.7 0.9 copy-start
  3.3 17.1 %collective-permute-start = (f32[64,576]{1,0:T(8,128)S(1)}, f32[64,576]{1,0:T(8,128)S(1)}, u32[]{:S(2)}, u32[]{:S(2)}) collective-permute-start(f32[64,576]{1,0:T(8,128)S(1)} %dynamic-slice_bitcast_fusion.1), channel_id=1, source_target_pairs={{0,8},{8,0},{16,24},{24,16},{32,40},{40,32},{48,56},{56,48},{64,72... | collective-permute-start | bytes 442376 | tf_op jit(solution)/shard_map/ppermute | solution.py:17
  21.2 9.5 %copy-start.1 = (bf16[128,768]{1,0:T(8,128)(2,1)S(1)}, bf16[128,768]{1,0:T(8,128)(2,1)}, u32[]{:S(2)}) copy-start(bf16[128,768]{1,0:T(8,128)(2,1)} %param.5) | copy-start | bytes 589828
  21.2 25.2 %all-to-all-start = ((f32[64,1,576]{2,1,0:T(1,128)}), f32[64,1,576]{2,1,0:T(1,128)S(1)}, u32[]{:S(2)}, u32[]{:S(2)}) async-start(f32[64,1,576]{2,1,0:T(1,128)} %copy.74), calls=%async_computation | async-start | bytes 327680 | tf_op jit(solution)/shard_map/all_to_all | solution.py:22
  30.7 0.9 copy-start.2
  47.5 21.7 %all-to-all-start.1 = ((f32[64,1,576]{2,1,0:T(1,128)}), f32[64,1,576]{2,1,0:T(1,128)S(1)}, u32[]{:S(2)}, u32[]{:S(2)}) async-start(f32[64,1,576]{2,1,0:T(1,128)} %copy.75), calls=%async_computation.1 | async-start | bytes 327680 | tf_op jit(solution)/shard_map/all_to_all | solution.py:22
  69.9 6.4 %collective-permute-start.1 = (f32[64,576]{1,0:T(8,128)S(1)}, f32[64,576]{1,0:T(8,128)S(1)}, u32[]{:S(2)}, u32[]{:S(2)}) collective-permute-start(f32[64,576]{1,0:T(8,128)S(1)} %get-tuple-element.28), channel_id=1, source_target_pairs={{0,8},{8,0},{16,24},{24,16},{32,40},{40,32},{48,56},{56,48},{64,72... | collective-permute-start | bytes 442376 | tf_op jit(solution)/shard_map/ppermute | solution.py:17
  76.3 0.7 copy-start.4
  79.9 0.7 copy-start.5
  94.7 4.7 %collective-permute-start.2 = (f32[64,576]{1,0:T(8,128)S(1)}, f32[64,576]{1,0:T(8,128)S(1)}, u32[]{:S(2)}, u32[]{:S(2)}) collective-permute-start(f32[64,576]{1,0:T(8,128)S(1)} %dynamic-slice_bitcast_fusion), channel_id=1, source_target_pairs={{0,8},{8,0},{16,24},{24,16},{32,40},{40,32},{48,56},{56,48},{64,72... | collective-permute-start | bytes 442376 | tf_op jit(solution)/shard_map/ppermute | solution.py:17
  100.3 21.5 %all-to-all-start.3 = ((f32[64,1,576]{2,1,0:T(1,128)}), f32[64,1,576]{2,1,0:T(1,128)S(1)}, u32[]{:S(2)}, u32[]{:S(2)}) async-start(f32[64,1,576]{2,1,0:T(1,128)} %copy.79), calls=%async_computation.3 | async-start | bytes 327680 | tf_op jit(solution)/shard_map/all_to_all | solution.py:22
  122.9 21.5 %all-to-all-start.4 = ((f32[64,1,576]{2,1,0:T(1,128)}), f32[64,1,576]{2,1,0:T(1,128)}, u32[]{:S(2)}, u32[]{:S(2)}) async-start(f32[64,1,576]{2,1,0:T(1,128)} %copy.80), calls=%async_computation.4 | async-start | bytes 327680 | tf_op jit(solution)/shard_map/all_to_all | solution.py:22
  146.0 6.7 %collective-permute-start.3 = (f32[64,576]{1,0:T(8,128)S(1)}, f32[64,576]{1,0:T(8,128)S(1)}, u32[]{:S(2)}, u32[]{:S(2)}) collective-permute-start(f32[64,576]{1,0:T(8,128)S(1)} %get-tuple-element.26), channel_id=1, source_target_pairs={{0,8},{8,0},{16,24},{24,16},{32,40},{40,32},{48,56},{56,48},{64,72... | collective-permute-start | bytes 442376 | tf_op jit(solution)/shard_map/ppermute | solution.py:17
  152.8 0.7 copy-start.3

commit v2 on v0

v2 whole, which is shorter than its diff:
```python
import jax
import jax.numpy as jnp
from jax import lax
from jax.experimental import pallas as pl
from jax.experimental.pallas import tpu as pltpu
from jax.sharding import PartitionSpec as P

HEAD_DIM = 96
D = 6144
TOK = 128
LANES = 128
HALF_HEADS = 4
HALF = HALF_HEADS * HEAD_DIM
CHIPS = 64
CORES = 2
PIECE = 640

epsilon = 1e-06
F32 = jnp.float32
BF16 = jnp.bfloat16
VMEM = pl.BlockSpec(memory_space=pltpu.VMEM)
NN = (((1,), (0,)), ((), ()))
NT = (((1,), (1,)), ((), ()))
TN = (((0,), (0,)), ((), ()))


def mm(a, b, dims):
    return lax.dot_general(a, b, dims, preferred_element_type=F32)


def half(g):
    return slice(g * HALF, (g + 1) * HALF)


def head_masks(rows):
    lane = lax.broadcasted_iota(jnp.int32, (rows, HALF), 1)
    return [(lane >= h * HEAD_DIM) & (lane < (h + 1) * HEAD_DIM) for h in range(HALF_HEADS)]


def spread(x):
    return jnp.concatenate([x * m.astype(BF16) for m in head_masks(x.shape[0])], axis=0)


def diagonal(x):
    rows = x.shape[0] // HALF_HEADS
    masks = head_masks(rows)
    out = x[:rows]
    for h in range(1, HALF_HEADS):
        out = jnp.where(masks[h], x[h * rows : (h + 1) * rows], out)
    return out


def to_pieces(state):
    rest = state[64:96]
    tail = rest[:, 256:384]
    return jnp.concatenate(
        [
            state[0:64],
            jnp.concatenate([rest[:, 0:128], rest[:, 128:256]], axis=0),
            jnp.concatenate([tail, pltpu.roll(tail, 64, 1)], axis=0),
        ],
        axis=1,
    )


def from_pieces(pieces):
    low = lax.broadcasted_iota(jnp.int32, (32, LANES), 1) < 64
    tail = jnp.where(low, pieces[0:32, 512:640], pltpu.roll(pieces[32:64, 512:640], 64, 1))
    rest = jnp.concatenate([pieces[0:32, 384:512], pieces[32:64, 384:512], tail], axis=1)
    return jnp.concatenate([pieces[:, 0:384], rest], axis=0)


def silu_low(x):
    x = x.astype(F32)
    return (x * jax.nn.sigmoid(x)).astype(BF16)


def silu_slope(x):
    x = x.astype(F32)
    sig = jax.nn.sigmoid(x)
    return sig * (1.0 + x * (1.0 - sig))


def causal4():
    row = lax.broadcasted_iota(jnp.int32, (TOK, TOK), 0)
    col = lax.broadcasted_iota(jnp.int32, (TOK, TOK), 1)
    keep = jnp.where(row >= col, 1.0, 0.0)
    return jnp.concatenate([keep] * HALF_HEADS, axis=1) > 0.5


def by_head(x):
    return jnp.concatenate([x[:, h * TOK : (h + 1) * TOK] for h in range(HALF_HEADS)], axis=0)


def store_states(first, second, mine_ref, theirs_ref):
    low = (lax.axis_index("ctx") % CORES) == 0
    first, second = to_pieces(first), to_pieces(second)
    mine_ref[:, 0, :] = jnp.where(low, first, second)
    theirs_ref[:, 0, :] = jnp.where(low, second, first)


def load_states(here_ref, there_ref):
    low = (lax.axis_index("ctx") % CORES) == 0
    here, there = here_ref[:, 0, :], there_ref[:, 0, :]
    pair = jnp.where(low, here, there), jnp.where(low, there, here)
    return [from_pieces(p).astype(BF16) for p in pair]


def state_kernel(k_ref, v_ref, mine_ref, theirs_ref):
    states = [
        diagonal(mm(silu_low(k_ref[:, half(g)]), v_ref[:, half(g)], TN)) for g in range(CORES)
    ]
    store_states(*states, mine_ref, theirs_ref)


def intra_kernel(q_ref, k_ref, v_ref, attn_ref, intra_ref):
    keep = causal4()
    for g in range(CORES):
        q_feat, k_feat = silu_low(q_ref[:, half(g)]), silu_low(k_ref[:, half(g)])
        attn = jnp.where(keep, mm(q_feat, spread(k_feat), NT), 0.0).astype(BF16)
        attn_ref[g] = attn
        intra_ref[:, half(g)] = mm(attn, spread(v_ref[:, half(g)]), NN)


def scan_kernel(backward, pieces_ref, out_ref):
    row = lax.broadcasted_iota(jnp.int32, (CHIPS, CHIPS), 0)
    col = lax.broadcasted_iota(jnp.int32, (CHIPS, CHIPS), 1)
    before = jnp.where(row < col if backward else row > col, 1.0, 0.0)
    out_ref[:, 0, :] = lax.dot_general(
        before, pieces_ref[:, 0, :], NN, precision=lax.Precision.HIGHEST, preferred_element_type=F32
    )


def lane_sums(x):
    part = x[:, 0:LANES]
    for i in range(1, x.shape[1] // LANES):
        part = part + x[:, i * LANES : (i + 1) * LANES]
    return jnp.sum(part.T, axis=0, keepdims=True)


def raw_kernel(q_ref, c_ref, gain_ref, intra_ref, here_ref, there_ref, raw_ref, low_ref, parts_ref):
    for g, state in enumerate(load_states(here_ref, there_ref)):
        low_ref[g] = state
        raw_ref[:, half(g)] = intra_ref[:, half(g)] + mm(
            silu_low(q_ref[:, half(g)]), spread(state), NN
        )
    raw = raw_ref[...]
    upstream = c_ref[...].astype(F32) * gain_ref[...]
    sums = jnp.concatenate([lane_sums(raw * raw), lane_sums(upstream * raw)], axis=0)
    parts_ref[...] = jnp.broadcast_to(sums[None], parts_ref.shape)


def grad_state_kernel(
    q_ref, c_ref, gain_ref, raw_ref, parts_ref, attended_ref, d_raw_ref, mine_ref, theirs_ref
):
    totals = jnp.sum(parts_ref[...], axis=0)
    square = jnp.broadcast_to(totals[0:1], (TOK, LANES)).T
    cross = jnp.broadcast_to(totals[1:2], (TOK, LANES)).T
    mean = square * (1.0 / D) + epsilon
    inverse = lax.rsqrt(mean)
    pull = cross / (D * mean)
    wide = 3
    inverse, pull = (jnp.concatenate([x] * wide, axis=1) for x in (inverse, pull))
    states = []
    for g in range(CORES):
        raw, gain = raw_ref[:, half(g)], gain_ref[:, half(g)]
        attended_ref[:, half(g)] = (raw * inverse * gain).astype(BF16)
        d_raw = ((c_ref[:, half(g)].astype(F32) * gain - raw * pull) * inverse).astype(BF16)
        d_raw_ref[:, half(g)] = d_raw
        states.append(diagonal(mm(silu_low(q_ref[:, half(g)]), d_raw, TN)))
    store_states(*states, mine_ref, theirs_ref)


def back_kernel(
    q_ref, k_ref, v_ref, d_raw_ref, attn_ref, low_ref, grad_q_ref, grad_kf_ref, grad_vf_ref
):
    keep = causal4()
    for g in range(CORES):
        q, d_raw = q_ref[:, half(g)], d_raw_ref[:, half(g)]
        q_feat, k_feat = silu_low(q), silu_low(k_ref[:, half(g)])
        back = jnp.where(keep, mm(d_raw, spread(v_ref[:, half(g)]), NT), 0.0).astype(BF16)
        grad_qf = mm(back, spread(k_feat), NN) + mm(d_raw, spread(low_ref[g]), NT)
        grad_q_ref[:, half(g)] = (grad_qf * silu_slope(q)).astype(BF16)
        grad_kf_ref[:, half(g)] = mm(by_head(back), spread(q_feat), TN)
        grad_vf_ref[:, half(g)] = mm(by_head(attn_ref[g]), spread(d_raw), TN)


def last_kernel(k_ref, v_ref, grad_kf_ref, grad_vf_ref, here_ref, there_ref, grad_k_ref, grad_v_ref):
    for g, state in enumerate(load_states(here_ref, there_ref)):
        k = k_ref[:, half(g)]
        later = spread(state)
        grad_kf = grad_kf_ref[:, half(g)] + mm(v_ref[:, half(g)], later, NT)
        grad_k_ref[:, half(g)] = (grad_kf * silu_slope(k)).astype(BF16)
        grad_vf = grad_vf_ref[:, half(g)] + mm(silu_low(k), later, NN)
        grad_v_ref[:, half(g)] = grad_vf.astype(BF16)


def call(kernel, outs, *args, flops=0):
    return pl.pallas_call(
        kernel,
        out_shape=[jax.ShapeDtypeStruct(shape, kind) for shape, kind in outs],
        in_specs=[VMEM] * len(args),
        out_specs=[VMEM] * len(outs),
        compiler_params=pltpu.CompilerParams(vmem_limit_bytes=32 * 1024 * 1024),
        cost_estimate=pl.CostEstimate(flops=flops, bytes_accessed=1_000_000, transcendentals=0),
    )(*args)


def swap_cores(x):
    pairs = [(i, i ^ 1) for i in range(CHIPS * CORES)]
    return lax.ppermute(x, "ctx", pairs)


def across_chips(x):
    groups = [[chip * CORES + core for chip in range(CHIPS)] for core in range(CORES)]
    return lax.all_to_all(x, "ctx", 0, 0, axis_index_groups=groups)


PIECES = ((CHIPS, 1, PIECE), F32)
WIDE = ((TOK, CORES * HALF), F32)
WIDE_LOW = ((TOK, CORES * HALF), BF16)
ATTN = ((CORES, TOK, HALF_HEADS * TOK), BF16)
STATE_LOW = ((CORES, HEAD_DIM, HALF), BF16)


def exclusive(mine, theirs, backward):
    core = lax.axis_index("ctx") % CORES
    mine_goes = core == (1 if backward else 0)
    received = swap_cores(theirs)
    pieces = across_chips(mine + received)

    def kernel(pieces_ref, out_ref):
        scan_kernel(backward, pieces_ref, out_ref)

    (summed,) = call(kernel, [PIECES], pieces)
    chip = across_chips(summed)
    there = swap_cores(chip + jnp.where(mine_goes, mine, 0.0))
    here = chip + jnp.where(mine_goes, 0.0, received)
    return here, there


def per_device(queries, key_input, value_input, norm_gain, cotangent):
    n_head = lax.axis_size("head")
    gain = norm_gain.reshape(1, -1)
    mine, theirs = call(state_kernel, [PIECES, PIECES], key_input, value_input)
    attn, intra = call(
        intra_kernel, [ATTN, WIDE], queries, key_input, value_input, flops=200_000_000
    )
    here, there = exclusive(mine, theirs, False)
    raw, low, parts = call(
        raw_kernel,
        [WIDE, STATE_LOW, ((n_head, 2, TOK), F32)],
        queries, cotangent, gain, intra, here, there,
    )
    parts = lax.all_to_all(parts, "head", 0, 0)
    attended, d_raw, mine, theirs = call(
        grad_state_kernel,
        [WIDE_LOW, WIDE_LOW, PIECES, PIECES],
        queries, cotangent, gain, raw, parts,
    )
    grad_query, grad_kf, grad_vf = call(
        back_kernel,
        [WIDE_LOW, WIDE, WIDE],
        queries, key_input, value_input, d_raw, attn, low,
        flops=500_000_000,
    )
    here, there = exclusive(mine, theirs, True)
    grad_key, grad_value = call(
        last_kernel,
        [WIDE_LOW, WIDE_LOW],
        key_input, value_input, grad_kf, grad_vf, here, there,
    )
    return (attended, grad_query, grad_key, grad_value)


def solution(mesh):
    in_specs = (P("ctx", "head"), P("ctx", "head"), P("ctx", "head"), P("head"), P("ctx", "head"))
    out_specs = (P("ctx", "head"), P("ctx", "head"), P("ctx", "head"), P("ctx", "head"))
    return jax.shard_map(
        per_device, mesh=mesh, in_specs=in_specs, out_specs=out_specs, check_vma=False
    )
```

time: 1040 us -> 147 us (0.14); the launches traced: 1030 us -> 147 us
  waiting for transfers between devices: 980 us -> 31.2 us
  blocking collectives: 13.2 us -> 59.4 us
  starting transfers between devices: 0.12 us -> 44.9 us
  between operations: 13.9 us -> 0.82 us
    all_gather x2 -> x0, waiting for transfers between devices: 643 us -> none  [prefix_2(): gathered = lax.all_gather(part, axis)]
    psum x1 -> x0, waiting for transfers between devices: 337 us -> none  [per_device(): whole_sum = lax.psum(local_grad, 'ctx')]
    all_to_all x0 -> x3, blocking collectives: none -> 59.4 us  [the longest x2 46.2 us: across_chips(): return lax.all_to_all(x, 'ctx', 0, 0, axis_index_groups=groups)]
    ppermute x0 -> x4, starting transfers between devices: none -> 30.9 us  [swap_cores(): return lax.ppermute(x, 'ctx', pairs)]
    all_to_all x0 -> x2, waiting for transfers between devices: none -> 29 us  [across_chips(): return lax.all_to_all(x, 'ctx', 0, 0, axis_index_groups=groups)]
    all_to_all x0 -> x2, starting transfers between devices: none -> 14 us  [across_chips(): return lax.all_to_all(x, 'ctx', 0, 0, axis_index_groups=groups)]
    psum x1 -> x0, blocking collectives: 13.2 us -> none  [per_device(): square_total = lax.psum(square_part, 'head')]
  transfers between devices with their start and end apart: 3 -> 6, of which waited for: 3 -> 5; matrix products, arithmetic and copies ran while one was open for 1% -> 0% of each run, Pallas kernels for 0% -> 2%
where the time goes in v2:
time: 147 us
  blocking collectives  59.4 us (40%)
  starting transfers between devices  44.9 us (31%)
  waiting for transfers between devices  31.2 us (21%)
  Pallas kernels  7.44 us (5%)
  local copies, waits for them, and re-layouts  1.88 us (1%)
    all_to_all x2, blocking collectives, across_chips(): return lax.all_to_all(x, 'ctx', 0, 0, axis_index_groups=groups)  46.2 us
    ppermute x4, starting transfers between devices, swap_cores(): return lax.ppermute(x, 'ctx', pairs)  30.9 us
    all_to_all x2, waiting for transfers between devices, across_chips(): return lax.all_to_all(x, 'ctx', 0, 0, axis_index_groups=groups)  29 us
    all_to_all x2, starting transfers between devices, across_chips(): return lax.all_to_all(x, 'ctx', 0, 0, axis_index_groups=groups)  14 us
    all_to_all x1, blocking collectives, per_device(): parts = lax.all_to_all(parts, 'head', 0, 0)  13.2 us
    pallas_call x8, Pallas kernels, call(): pl.pallas_call(kernel, out_shape=[jax.ShapeDtypeStruct(shape, kind) for s...  7.44 us
  transfers between devices with their start and end apart: 6, of which 5 were waited for; matrix products, arithmetic and copies ran while one was open for 0% of the time, Pallas kernels for 2%

profile of v2, /device:TPU:1, one launch (start us, length us, event | category | flops | bytes accessed | tf_op | source)
XLA Modules:
  0.0 146.7 jit_solution(4396504234678812753)
XLA Ops:
  0.6 0.0 copy-start.2
  0.6 0.9 copy-done.2
  1.6 0.0 copy-start.4
  1.6 0.9 copy-done.4
  2.5 0.5 shard_map.85
  3.0 16.1 %collective-permute-start = (f32[64,1,640]{2,1,0:T(1,128)S(1)}, f32[64,1,640]{2,1,0:T(1,128)S(1)}, u32[]{:S(2)}, u32[]{:S(2)}) collective-permute-start(f32[64,1,640]{2,1,0:T(1,128)S(1)} %get-tuple-element.22), channel_id=1, source_target_pairs={{0,8},{8,0},{16,24},{24,16},{32,40},{40,32},{48,56},{56,48},{64,72... | collective-permute-start | bytes 491528 | tf_op jit(solution)/shard_map/ppermute | solution.py:211
  19.0 1.0 collective-permute-done
  20.0 0.2 add.23
  20.2 24.9 %all_to_all.25.pieces_ref = f32[64,1,640]{2,1,0:T(1,128)S(1)} all-to-all(f32[64,1,640]{2,1,0:T(1,128)S(1)} %add.23), channel_id=1, replica_groups={{0,16,32,48,64,80,96,112,128,144,160,176,192,208,224,240,256,272,288,30..., dimensions={0} | all-to-all | bytes 327680 | tf_op jit(solution)/shard_map/all_to_all | solution.py:216
  45.1 1.0 shard_map.86
  46.1 7.0 %all-to-all-start.1 = ((f32[64,1,640]{2,1,0:T(1,128)}), f32[64,1,640]{2,1,0:T(1,128)S(1)}, u32[]{:S(2)}, u32[]{:S(2)}) async-start(f32[64,1,640]{2,1,0:T(1,128)} %shard_map.86), calls=%async_computation.1 | async-start | bytes 327680 | tf_op jit(solution)/shard_map/all_to_all | solution.py:216
  53.1 0.0 copy-start.1
  53.1 0.0 copy-start.3
  53.1 0.0 copy-start.5
  53.1 14.3 %all-to-all-done.1 = f32[64,1,640]{2,1,0:T(1,128)S(1)} async-done(((f32[64,1,640]{2,1,0:T(1,128)}), f32[64,1,640]{2,1,0:T(1,128)S(1)}, u32[]{:S(2)}, u32[]{:S(2)}) %all-to-all-start.1) | async-done | bytes 163872 | tf_op jit(solution)/shard_map/all_to_all | solution.py:216
  67.5 0.0 copy-start.6
  67.5 0.3 fusion.1
  67.8 5.7 %collective-permute-start.1 = (f32[64,1,640]{2,1,0:T(1,128)S(1)}, f32[64,1,640]{2,1,0:T(1,128)S(1)}, u32[]{:S(2)}, u32[]{:S(2)}) collective-permute-start(f32[64,1,640]{2,1,0:T(1,128)S(1)} %get-tuple-element.38), channel_id=1, source_target_pairs={{0,8},{8,0},{16,24},{24,16},{32,40},{40,32},{48,56},{56,48},{64,72... | collective-permute-start | bytes 491528 | tf_op jit(solution)/shard_map/ppermute | solution.py:211
  73.6 0.0 copy-done.6
  73.6 0.0 copy-done.1
  73.6 0.0 copy-done.3
  73.6 0.0 copy-done.5
  73.6 0.0 copy-start
  73.6 0.8 shard_map.84
  74.4 0.2 collective-permute-done.1.there_ref
  74.6 0.0 copy-done
  74.6 0.5 shard_map.87
  75.1 13.2 %all_to_all.26.parts_ref = f32[8,2,128]{2,1,0:T(2,128)S(1)} all-to-all(f32[8,2,128]{2,1,0:T(2,128)S(1)} %get-tuple-element.24), channel_id=1, replica_groups=mesh['ctx'=128,'head'=8] {'head'}, dimensions={0} | all-to-all | bytes 16384 | tf_op jit(solution)/shard_map/all_to_all | solution.py:255
  88.3 0.9 shard_map.88
  89.2 3.7 %collective-permute-start.2 = (f32[64,1,640]{2,1,0:T(1,128)S(1)}, f32[64,1,640]{2,1,0:T(1,128)S(1)}, u32[]{:S(2)}, u32[]{:S(2)}) collective-permute-start(f32[64,1,640]{2,1,0:T(1,128)S(1)} %get-tuple-element.33), channel_id=1, source_target_pairs={{0,8},{8,0},{16,24},{24,16},{32,40},{40,32},{48,56},{56,48},{64,72... | collective-permute-start | bytes 491528 | tf_op jit(solution)/shard_map/ppermute | solution.py:211
  92.9 1.0 collective-permute-done.2
  93.9 0.2 add.27
  94.1 21.3 %all_to_all.27.pieces_ref = f32[64,1,640]{2,1,0:T(1,128)S(1)} all-to-all(f32[64,1,640]{2,1,0:T(1,128)S(1)} %add.27), channel_id=1, replica_groups={{0,16,32,48,64,80,96,112,128,144,160,176,192,208,224,240,256,272,288,30..., dimensions={0} | all-to-all | bytes 327680 | tf_op jit(solution)/shard_map/all_to_all | solution.py:216
  115.4 1.0 shard_map.90
  116.4 7.0 %all-to-all-start.4 = ((f32[64,1,640]{2,1,0:T(1,128)}), f32[64,1,640]{2,1,0:T(1,128)S(1)}, u32[]{:S(2)}, u32[]{:S(2)}) async-start(f32[64,1,640]{2,1,0:T(1,128)} %shard_map.90), calls=%async_computation.4 | async-start | bytes 327680 | tf_op jit(solution)/shard_map/all_to_all | solution.py:216
  123.4 14.7 %all-to-all-done.4 = f32[64,1,640]{2,1,0:T(1,128)S(1)} async-done(((f32[64,1,640]{2,1,0:T(1,128)}), f32[64,1,640]{2,1,0:T(1,128)S(1)}, u32[]{:S(2)}, u32[]{:S(2)}) %all-to-all-start.4) | async-done | bytes 163872 | tf_op jit(solution)/shard_map/all_to_all | solution.py:216
  138.1 0.3 fusion.3
  138.5 5.4 %collective-permute-start.3 = (f32[64,1,640]{2,1,0:T(1,128)S(1)}, f32[64,1,640]{2,1,0:T(1,128)S(1)}, u32[]{:S(2)}, u32[]{:S(2)}) collective-permute-start(f32[64,1,640]{2,1,0:T(1,128)S(1)} %get-tuple-element.36), channel_id=1, source_target_pairs={{0,8},{8,0},{16,24},{24,16},{32,40},{40,32},{48,56},{56,48},{64,72... | collective-permute-start | bytes 491528 | tf_op jit(solution)/shard_map/ppermute | solution.py:211
  143.9 1.6 %shard_map.89 = (bf16[128,768]{1,0:T(8,128)(2,1)}, f32[128,768]{1,0:T(8,128)S(1)}, f32[128,768]{1,0:T(8,128)S(1)}) custom-call(bf16[128,768]{1,0:T(8,128)(2,1)S(1)} %copy-done.1, bf16[128,768]{1,0:T(8,128)(2,1)S(1)} %copy-done.3, bf16[128,768]{1,0:T(8,128)(2,1)S(1)} %copy-done.5, bf16[128,768]{1,0:T(8,128)(2,1)S(1)} %get-tuple-element.26.d_raw_ref, ...), custom_call_target="tpu_custom_call" | custom-call | flops 500000000 | bytes 1000000 | tf_op jit(solution)/shard_map/pallas_call | solution.py:199
  145.5 0.0 collective-permute-done.3.there_ref
  145.5 1.2 shard_map.91
  (1 shorter events, 0.0 us)
Async XLA Ops:
  0.6 0.9 copy-start.2
  1.6 0.9 copy-start.4
  3.0 17.1 %collective-permute-start = (f32[64,1,640]{2,1,0:T(1,128)S(1)}, f32[64,1,640]{2,1,0:T(1,128)S(1)}, u32[]{:S(2)}, u32[]{:S(2)}) collective-permute-start(f32[64,1,640]{2,1,0:T(1,128)S(1)} %get-tuple-element.22), channel_id=1, source_target_pairs={{0,8},{8,0},{16,24},{24,16},{32,40},{40,32},{48,56},{56,48},{64,72... | collective-permute-start | bytes 491528 | tf_op jit(solution)/shard_map/ppermute | solution.py:211
  46.1 21.4 %all-to-all-start.1 = ((f32[64,1,640]{2,1,0:T(1,128)}), f32[64,1,640]{2,1,0:T(1,128)S(1)}, u32[]{:S(2)}, u32[]{:S(2)}) async-start(f32[64,1,640]{2,1,0:T(1,128)} %shard_map.86), calls=%async_computation.1 | async-start | bytes 327680 | tf_op jit(solution)/shard_map/all_to_all | solution.py:216
  53.1 20.5 %copy-start.1 = (bf16[128,768]{1,0:T(8,128)(2,1)S(1)}, bf16[128,768]{1,0:T(8,128)(2,1)}, u32[]{:S(2)}) copy-start(bf16[128,768]{1,0:T(8,128)(2,1)} %q_ref.7) | copy-start | bytes 589828
  53.1 20.5 %copy-start.3 = (bf16[128,768]{1,0:T(8,128)(2,1)S(1)}, bf16[128,768]{1,0:T(8,128)(2,1)}, u32[]{:S(2)}) copy-start(bf16[128,768]{1,0:T(8,128)(2,1)} %k_ref.7) | copy-start | bytes 589828
  53.1 20.5 %copy-start.5 = (bf16[128,768]{1,0:T(8,128)(2,1)S(1)}, bf16[128,768]{1,0:T(8,128)(2,1)}, u32[]{:S(2)}) copy-start(bf16[128,768]{1,0:T(8,128)(2,1)} %v_ref.7) | copy-start | bytes 589828
  67.5 6.1 %copy-start.6 = (f32[768]{0:T(1024)S(1)}, f32[768]{0:T(1024)}, u32[]{:S(2)}) copy-start(f32[768]{0:T(1024)} %param.8) | copy-start | bytes 9220
  67.8 6.8 %collective-permute-start.1 = (f32[64,1,640]{2,1,0:T(1,128)S(1)}, f32[64,1,640]{2,1,0:T(1,128)S(1)}, u32[]{:S(2)}, u32[]{:S(2)}) collective-permute-start(f32[64,1,640]{2,1,0:T(1,128)S(1)} %get-tuple-element.38), channel_id=1, source_target_pairs={{0,8},{8,0},{16,24},{24,16},{32,40},{40,32},{48,56},{56,48},{64,72... | collective-permute-start | bytes 491528 | tf_op jit(solution)/shard_map/ppermute | solution.py:211
  73.6 1.0 copy-start
  89.2 4.7 %collective-permute-start.2 = (f32[64,1,640]{2,1,0:T(1,128)S(1)}, f32[64,1,640]{2,1,0:T(1,128)S(1)}, u32[]{:S(2)}, u32[]{:S(2)}) collective-permute-start(f32[64,1,640]{2,1,0:T(1,128)S(1)} %get-tuple-element.33), channel_id=1, source_target_pairs={{0,8},{8,0},{16,24},{24,16},{32,40},{40,32},{48,56},{56,48},{64,72... | collective-permute-start | bytes 491528 | tf_op jit(solution)/shard_map/ppermute | solution.py:211
  116.4 21.7 %all-to-all-start.4 = ((f32[64,1,640]{2,1,0:T(1,128)}), f32[64,1,640]{2,1,0:T(1,128)S(1)}, u32[]{:S(2)}, u32[]{:S(2)}) async-start(f32[64,1,640]{2,1,0:T(1,128)} %shard_map.90), calls=%async_computation.4 | async-start | bytes 327680 | tf_op jit(solution)/shard_map/all_to_all | solution.py:216
  138.5 7.0 %collective-permute-start.3 = (f32[64,1,640]{2,1,0:T(1,128)S(1)}, f32[64,1,640]{2,1,0:T(1,128)S(1)}, u32[]{:S(2)}, u32[]{:S(2)}) collective-permute-start(f32[64,1,640]{2,1,0:T(1,128)S(1)} %get-tuple-element.36), channel_id=1, source_target_pairs={{0,8},{8,0},{16,24},{24,16},{32,40},{40,32},{48,56},{56,48},{64,72... | collective-permute-start | bytes 491528 | tf_op jit(solution)/shard_map/ppermute | solution.py:211

commit v3 on v2

v3 whole, which is shorter than its diff:
```python
import jax
import jax.numpy as jnp
from jax import lax
from jax.experimental import pallas as pl
from jax.experimental.pallas import tpu as pltpu
from jax.sharding import PartitionSpec as P

HEAD_DIM = 96
D = 6144
TOK = 128
LANES = 128
HALF_HEADS = 4
HALF = HALF_HEADS * HEAD_DIM
CHIPS = 64
CORES = 2
PIECE = 640

epsilon = 1e-06
F32 = jnp.float32
BF16 = jnp.bfloat16
VMEM = pl.BlockSpec(memory_space=pltpu.VMEM)
NN = (((1,), (0,)), ((), ()))
NT = (((1,), (1,)), ((), ()))
TN = (((0,), (0,)), ((), ()))


def mm(a, b, dims):
    return lax.dot_general(a, b, dims, preferred_element_type=F32)


def half(g):
    return slice(g * HALF, (g + 1) * HALF)


def head_masks(rows):
    lane = lax.broadcasted_iota(jnp.int32, (rows, HALF), 1)
    return [(lane >= h * HEAD_DIM) & (lane < (h + 1) * HEAD_DIM) for h in range(HALF_HEADS)]


def spread(x):
    return jnp.concatenate([x * m.astype(BF16) for m in head_masks(x.shape[0])], axis=0)


def diagonal(x):
    rows = x.shape[0] // HALF_HEADS
    masks = head_masks(rows)
    out = x[:rows]
    for h in range(1, HALF_HEADS):
        out = jnp.where(masks[h], x[h * rows : (h + 1) * rows], out)
    return out


def to_pieces(state):
    rest = state[64:96]
    tail = rest[:, 256:384]
    return jnp.concatenate(
        [
            state[0:64],
            jnp.concatenate([rest[:, 0:128], rest[:, 128:256]], axis=0),
            jnp.concatenate([tail, pltpu.roll(tail, 64, 1)], axis=0),
        ],
        axis=1,
    )


def from_pieces(pieces):
    low = lax.broadcasted_iota(jnp.int32, (32, LANES), 1) < 64
    tail = jnp.where(low, pieces[0:32, 512:640], pltpu.roll(pieces[32:64, 512:640], 64, 1))
    rest = jnp.concatenate([pieces[0:32, 384:512], pieces[32:64, 384:512], tail], axis=1)
    return jnp.concatenate([pieces[:, 0:384], rest], axis=0)


def silu_low(x):
    x = x.astype(F32)
    return (x * jax.nn.sigmoid(x)).astype(BF16)


def silu_slope(x):
    x = x.astype(F32)
    sig = jax.nn.sigmoid(x)
    return sig * (1.0 + x * (1.0 - sig))


def causal4():
    row = lax.broadcasted_iota(jnp.int32, (TOK, TOK), 0)
    col = lax.broadcasted_iota(jnp.int32, (TOK, TOK), 1)
    keep = jnp.where(row >= col, 1.0, 0.0)
    return jnp.concatenate([keep] * HALF_HEADS, axis=1) > 0.5


def by_head(x):
    return jnp.concatenate([x[:, h * TOK : (h + 1) * TOK] for h in range(HALF_HEADS)], axis=0)


def core_index():
    return lax.axis_index("ctx") % CORES


def pick(own, x):
    first = (core_index() == 0) == own
    return jnp.where(first, x[:, half(0)], x[:, half(1)])


def in_order(own, other):
    first = core_index() == 0
    return jnp.where(first, own, other), jnp.where(first, other, own)


def state_kernel(k_ref, v_ref, mine_ref, theirs_ref):
    first, second = (
        to_pieces(diagonal(mm(silu_low(k_ref[:, half(g)]), v_ref[:, half(g)], TN)))
        for g in range(CORES)
    )
    low = core_index() == 0
    mine_ref[:, 0, :] = jnp.where(low, first, second)
    theirs_ref[:, 0, :] = jnp.where(low, second, first)


def send_kernel(q_ref, k_ref, v_ref, c_ref, out_ref):
    for i, ref in enumerate((q_ref, k_ref, v_ref, c_ref)):
        out_ref[i] = pick(False, ref[...]).astype(F32)


def attention(q_feat, k_feat):
    return jnp.where(causal4(), mm(q_feat, spread(k_feat), NT), 0.0).astype(BF16)


def intra_kernel(q_ref, k_ref, v_ref, got_ref, intra_ref):
    mine = [pick(True, ref[...]) for ref in (q_ref, k_ref, v_ref)]
    others = [got_ref[i].astype(BF16) for i in range(3)]
    for i, (q, k, v) in enumerate((mine, others)):
        intra_ref[i] = mm(attention(silu_low(q), silu_low(k)), spread(v), NN)


def scan_kernel(backward, pieces_ref, out_ref):
    row = lax.broadcasted_iota(jnp.int32, (CHIPS, CHIPS), 0)
    col = lax.broadcasted_iota(jnp.int32, (CHIPS, CHIPS), 1)
    before = jnp.where(row < col if backward else row > col, 1.0, 0.0)
    out_ref[:, 0, :] = lax.dot_general(
        before, pieces_ref[:, 0, :], NN, precision=lax.Precision.HIGHEST, preferred_element_type=F32
    )


def lane_sums(x):
    part = x[:, 0:LANES]
    for i in range(1, x.shape[1] // LANES):
        part = part + x[:, i * LANES : (i + 1) * LANES]
    return jnp.sum(part.T, axis=0, keepdims=True)


def raw_kernel(
    q_ref, c_ref, gain_ref, got_ref, intra_ref, chip_ref, mine_ref, received_ref,
    raw_ref, low_ref, give_ref, parts_ref,
):
    core = core_index()
    chip = chip_ref[:, 0, :]
    own = from_pieces(chip + jnp.where(core == 1, received_ref[:, 0, :], 0.0))
    other = from_pieces(chip + jnp.where(core == 0, mine_ref[:, 0, :], 0.0))
    low_ref[...] = own.astype(BF16)
    give_ref[TOK:, :] = other
    gain = pick(True, gain_ref[...])
    q, c = pick(True, q_ref[...]), pick(True, c_ref[...])
    sums = []
    for i, (q, c, state) in enumerate(
        ((q, c, own), (got_ref[0].astype(BF16), got_ref[3], other))
    ):
        raw = intra_ref[i] + mm(silu_low(q), spread(state.astype(BF16)), NN)
        raw_ref[i] = raw
        upstream = c.astype(F32) * gain
        sums.append(jnp.concatenate([lane_sums(raw * raw), lane_sums(upstream * raw)], axis=0))
    give_ref[0:TOK, :] = raw_ref[1]
    sums = jnp.concatenate(in_order(*sums), axis=0)
    parts_ref[...] = jnp.broadcast_to(sums[None], parts_ref.shape)


def scales(totals):
    square = jnp.broadcast_to(totals[0:1], (TOK, LANES)).T
    cross = jnp.broadcast_to(totals[1:2], (TOK, LANES)).T
    mean = square * (1.0 / D) + epsilon
    pair = lax.rsqrt(mean), cross / (D * mean)
    return [jnp.concatenate([x] * (HALF // LANES), axis=1) for x in pair]


def gradient(c, gain, raw, inverse, pull):
    return ((c.astype(F32) * gain - raw * pull) * inverse).astype(BF16)


def own_and_other(parts_ref):
    totals = jnp.sum(parts_ref[...], axis=0)
    return in_order(totals[0:2], totals[2:4])


def grad_state_kernel(
    q_ref, c_ref, gain_ref, got_ref, raw_ref, parts_ref, sum_ref, here_ref, there_ref
):
    core = core_index()
    gain = pick(True, gain_ref[...])
    q, c = pick(True, q_ref[...]), pick(True, c_ref[...])
    states = []
    for i, (q, c, totals) in enumerate(
        zip((q, got_ref[0].astype(BF16)), (c, got_ref[3]), own_and_other(parts_ref))
    ):
        d_raw = gradient(c, gain, raw_ref[i], *scales(totals))
        states.append(to_pieces(diagonal(mm(silu_low(q), d_raw, TN))))
    sum_ref[:, 0, :] = states[0] + states[1]
    here_ref[:, 0, :] = jnp.where(core == 0, states[1], 0.0)
    there_ref[:, 0, :] = jnp.where(core == 1, states[0], 0.0)


def back_kernel(
    q_ref, k_ref, v_ref, c_ref, gain_ref, raw_ref, low_ref, got_ref, parts_ref,
    attended_ref, grad_q_ref, grad_kf_ref, grad_vf_ref,
):
    keep = causal4()
    inverse, pull = scales(own_and_other(parts_ref)[0])
    raws = in_order(raw_ref[0], got_ref[0:TOK])
    lows = in_order(low_ref[...].astype(F32), got_ref[TOK:])
    for g in range(CORES):
        q, raw, gain = q_ref[:, half(g)], raws[g], gain_ref[:, half(g)]
        q_feat, k_feat = silu_low(q), silu_low(k_ref[:, half(g)])
        attended_ref[:, half(g)] = (raw * inverse * gain).astype(BF16)
        d_raw = gradient(c_ref[:, half(g)], gain, raw, inverse, pull)
        back = jnp.where(keep, mm(d_raw, spread(v_ref[:, half(g)]), NT), 0.0).astype(BF16)
        grad_qf = mm(back, spread(k_feat), NN) + mm(d_raw, spread(lows[g].astype(BF16)), NT)
        grad_q_ref[:, half(g)] = (grad_qf * silu_slope(q)).astype(BF16)
        grad_kf_ref[:, half(g)] = mm(by_head(back), spread(q_feat), TN)
        grad_vf_ref[:, half(g)] = mm(by_head(attention(q_feat, k_feat)), spread(d_raw), TN)


def last_kernel(
    k_ref, v_ref, grad_kf_ref, grad_vf_ref, chip_ref, here_ref, there_ref, grad_k_ref, grad_v_ref
):
    states = in_order(chip_ref[:, 0, :] + here_ref[:, 0, :], there_ref[:, 0, :])
    for g, state in enumerate(states):
        k = k_ref[:, half(g)]
        later = spread(from_pieces(state).astype(BF16))
        grad_kf = grad_kf_ref[:, half(g)] + mm(v_ref[:, half(g)], later, NT)
        grad_k_ref[:, half(g)] = (grad_kf * silu_slope(k)).astype(BF16)
        grad_vf = grad_vf_ref[:, half(g)] + mm(silu_low(k), later, NN)
        grad_v_ref[:, half(g)] = grad_vf.astype(BF16)


def call(kernel, outs, *args, flops=0):
    return pl.pallas_call(
        kernel,
        out_shape=[jax.ShapeDtypeStruct(shape, kind) for shape, kind in outs],
        in_specs=[VMEM] * len(args),
        out_specs=[VMEM] * len(outs),
        compiler_params=pltpu.CompilerParams(vmem_limit_bytes=32 * 1024 * 1024),
        cost_estimate=pl.CostEstimate(flops=flops, bytes_accessed=1_000_000, transcendentals=0),
    )(*args)


def swap_cores(x):
    pairs = [(i, i ^ 1) for i in range(CHIPS * CORES)]
    return lax.ppermute(x, "ctx", pairs)


def across_chips(x):
    groups = [[chip * CORES + core for chip in range(CHIPS)] for core in range(CORES)]
    return lax.all_to_all(x, "ctx", 0, 0, axis_index_groups=groups)


def over_heads(x):
    size = CORES * lax.axis_size("head")
    groups = [[chip * size + i for i in range(size)] for chip in range(CHIPS)]
    return lax.all_to_all(x, ("ctx", "head"), 0, 0, axis_index_groups=groups)


PIECES = ((CHIPS, 1, PIECE), F32)
WIDE = ((TOK, CORES * HALF), F32)
WIDE_LOW = ((TOK, CORES * HALF), BF16)
BLOCKS = ((CORES, TOK, HALF), F32)


def scan(pieces, backward):
    def kernel(pieces_ref, out_ref):
        scan_kernel(backward, pieces_ref, out_ref)

    (summed,) = call(kernel, [PIECES], across_chips(pieces))
    return across_chips(summed)


def per_device(queries, key_input, value_input, norm_gain, cotangent):
    sharers = CORES * lax.axis_size("head")
    gain = norm_gain.reshape(1, -1)
    mine, theirs = call(state_kernel, [PIECES, PIECES], key_input, value_input)
    received = swap_cores(theirs)
    (given,) = call(
        send_kernel, [((4, TOK, HALF), F32)], queries, key_input, value_input, cotangent
    )
    got = swap_cores(given)
    (intra,) = call(
        intra_kernel, [BLOCKS], queries, key_input, value_input, got, flops=200_000_000
    )
    chip = scan(mine + received, False)
    raw, low, give, parts = call(
        raw_kernel,
        [BLOCKS, ((HEAD_DIM, HALF), BF16), ((TOK + HEAD_DIM, HALF), F32), ((sharers, 4, TOK), F32)],
        queries, cotangent, gain, got, intra, chip, mine, received,
    )
    parts = over_heads(parts)
    total, here, there = call(
        grad_state_kernel,
        [PIECES, PIECES, PIECES],
        queries, cotangent, gain, got, raw, parts,
    )
    attended, grad_query, grad_kf, grad_vf = call(
        back_kernel,
        [WIDE_LOW, WIDE_LOW, WIDE, WIDE],
        queries, key_input, value_input, cotangent, gain, raw, low, swap_cores(give), parts,
        flops=500_000_000,
    )
    chip = scan(total, True)
    grad_key, grad_value = call(
        last_kernel,
        [WIDE_LOW, WIDE_LOW],
        key_input, value_input, grad_kf, grad_vf, chip, here, swap_cores(chip + there),
    )
    return (attended, grad_query, grad_key, grad_value)


def solution(mesh):
    in_specs = (P("ctx", "head"), P("ctx", "head"), P("ctx", "head"), P("head"), P("ctx", "head"))
    out_specs = (P("ctx", "head"), P("ctx", "head"), P("ctx", "head"), P("ctx", "head"))
    return jax.shard_map(
        per_device, mesh=mesh, in_specs=in_specs, out_specs=out_specs, check_vma=False
    )
```

time: 147 us -> 141 us (0.959)
  blocking collectives: 59.4 us -> 38.1 us
  waiting for transfers between devices: 31.2 us -> 38.6 us
  starting transfers between devices: 44.9 us -> 52.2 us
    all_to_all x2 -> x1, blocking collectives: 46.2 us -> 20.6 us  [across_chips(): return lax.all_to_all(x, 'ctx', 0, 0, axis_index_groups=groups)]
    all_to_all x2 -> x3, starting transfers between devices: 14 us -> 24 us  [across_chips(): return lax.all_to_all(x, 'ctx', 0, 0, axis_index_groups=groups)]
    all_to_all x2 -> x3, waiting for transfers between devices: 29 us -> 37.6 us  [across_chips(): return lax.all_to_all(x, 'ctx', 0, 0, axis_index_groups=groups)]
    all_to_all x1, blocking collectives: 13.2 us -> 17.4 us  [over_heads(): return lax.all_to_all(x, ('ctx', 'head'), 0, 0, axis_index_groups=groups)]
    ppermute x4, starting transfers between devices: 30.9 us -> 28.2 us  [swap_cores(): return lax.ppermute(x, 'ctx', pairs)]
    pallas_call x8 -> x9, Pallas kernels: 7.44 us -> 7.66 us  [call(): pl.pallas_call(kernel, out_shape=[jax.ShapeDtypeStruct(shape, kind) for s...]
  transfers between devices with their start and end apart: 6 -> 7, of which waited for: 5 -> 4; matrix products, arithmetic and copies ran while one was open for 0% -> 0% of each run, Pallas kernels for 2% -> 3%
where the time goes in v3:
time: 141 us; the launch traced here: 140 us
  starting transfers between devices  52.2 us (37%)
  waiting for transfers between devices  38.6 us (27%)
  blocking collectives  38.1 us (27%)
  Pallas kernels  7.66 us (5%)
  local copies, waits for them, and re-layouts  1.88 us (1%)
    all_to_all x3, waiting for transfers between devices, across_chips(): return lax.all_to_all(x, 'ctx', 0, 0, axis_index_groups=groups)  37.6 us
    ppermute x4, starting transfers between devices, swap_cores(): return lax.ppermute(x, 'ctx', pairs)  28.2 us
    all_to_all x3, starting transfers between devices, across_chips(): return lax.all_to_all(x, 'ctx', 0, 0, axis_index_groups=groups)  24 us
    all_to_all x1, blocking collectives, across_chips(): return lax.all_to_all(x, 'ctx', 0, 0, axis_index_groups=groups)  20.6 us
    all_to_all x1, blocking collectives, over_heads(): return lax.all_to_all(x, ('ctx', 'head'), 0, 0, axis_index_groups=groups)  17.4 us
    pallas_call x9, Pallas kernels, call(): pl.pallas_call(kernel, out_shape=[jax.ShapeDtypeStruct(shape, kind) for s...  7.66 us
  transfers between devices with their start and end apart: 7, of which 4 were waited for; matrix products, arithmetic and copies ran while one was open for 0% of the time, Pallas kernels for 3%

profile of v3, /device:TPU:1, one launch (start us, length us, event | category | flops | bytes accessed | tf_op | source)
XLA Modules:
  0.0 140.3 jit_solution(113332805112013947)
XLA Ops:
  0.6 0.0 copy-start
  0.6 0.9 copy-done
  1.6 0.0 copy-start.2
  1.6 0.9 copy-done.2
  2.5 0.5 shard_map.86
  3.0 16.1 %collective-permute-start.1 = (f32[64,1,640]{2,1,0:T(1,128)S(1)}, f32[64,1,640]{2,1,0:T(1,128)S(1)}, u32[]{:S(2)}, u32[]{:S(2)}) collective-permute-start(f32[64,1,640]{2,1,0:T(1,128)S(1)} %get-tuple-element.20), channel_id=1, source_target_pairs={{0,8},{8,0},{16,24},{24,16},{32,40},{40,32},{48,56},{56,48},{64,72... | collective-permute-start | bytes 491528 | tf_op jit(solution)/shard_map/ppermute | solution.py:256
  19.0 1.0 collective-permute-done.1.received_ref
  20.0 0.0 copy-start.3
  20.0 0.0 copy-start.4
  20.0 0.0 copy-start.5
  20.0 0.8 add.6
  20.9 0.0 copy-start.1
  20.9 9.4 %all-to-all-start = ((f32[64,1,640]{2,1,0:T(1,128)}), f32[64,1,640]{2,1,0:T(1,128)S(1)}, u32[]{:S(2)}, u32[]{:S(2)}) async-start(f32[64,1,640]{2,1,0:T(1,128)} %add.6), calls=%async_computation | async-start | bytes 327680 | tf_op jit(solution)/shard_map/all_to_all | solution.py:261
  30.3 0.0 copy-done.3
  30.3 0.0 copy-done.4
  30.3 0.0 copy-done.5
  30.4 0.0 copy-done.1
  30.4 0.1 shard_map.84
  30.5 2.6 %collective-permute-start = (f32[4,128,384]{2,1,0:T(8,128)S(1)}, f32[4,128,384]{2,1,0:T(8,128)S(1)}, u32[]{:S(2)}, u32[]{:S(2)}) collective-permute-start(f32[4,128,384]{2,1,0:T(8,128)S(1)} %shard_map.84), channel_id=1, source_target_pairs={{0,8},{8,0},{16,24},{24,16},{32,40},{40,32},{48,56},{56,48},{64,72... | collective-permute-start | bytes 2359304 | tf_op jit(solution)/shard_map/ppermute | solution.py:256
  33.0 13.1 %all-to-all-done.pieces_ref = f32[64,1,640]{2,1,0:T(1,128)S(1)} async-done(((f32[64,1,640]{2,1,0:T(1,128)}), f32[64,1,640]{2,1,0:T(1,128)S(1)}, u32[]{:S(2)}, u32[]{:S(2)}) %all-to-all-start) | async-done | bytes 163872 | tf_op jit(solution)/shard_map/all_to_all | solution.py:261
  46.1 1.0 shard_map.87
  47.1 0.0 copy-start.8
  47.1 7.2 %all-to-all-start.1 = ((f32[64,1,640]{2,1,0:T(1,128)}), f32[64,1,640]{2,1,0:T(1,128)S(1)}, u32[]{:S(2)}, u32[]{:S(2)}) async-start(f32[64,1,640]{2,1,0:T(1,128)} %shard_map.87), calls=%async_computation.1 | async-start | bytes 327680 | tf_op jit(solution)/shard_map/all_to_all | solution.py:261
  54.2 0.0 copy-done.8
  54.3 0.0 collective-permute-done.got_ref
  54.3 0.8 shard_map.85.intra_ref
  55.1 13.9 %all-to-all-done.1.chip_ref = f32[64,1,640]{2,1,0:T(1,128)S(1)} async-done(((f32[64,1,640]{2,1,0:T(1,128)}), f32[64,1,640]{2,1,0:T(1,128)S(1)}, u32[]{:S(2)}, u32[]{:S(2)}) %all-to-all-start.1) | async-done | bytes 163872 | tf_op jit(solution)/shard_map/all_to_all | solution.py:261
  69.0 0.5 shard_map.88
  69.5 0.0 copy-start.6
  69.5 17.4 %all_to_all.25.parts_ref = f32[16,4,128]{2,1,0:T(4,128)S(1)} all-to-all(f32[16,4,128]{2,1,0:T(4,128)S(1)} %get-tuple-element.24), channel_id=1, replica_groups={{0,1,2,3,4,5,6,7,8,9,10,11,12,13,14,15},{16,17,18,19,20,21,22,23,24,25,..., dimensions={0} | all-to-all | bytes 65536 | tf_op jit(solution)/shard_map/all_to_all | solution.py:267
  86.9 0.5 shard_map.90
  87.5 0.0 copy-done.6
  87.5 20.6 %all_to_all.26.pieces_ref = f32[64,1,640]{2,1,0:T(1,128)S(1)} all-to-all(f32[64,1,640]{2,1,0:T(1,128)S(1)} %get-tuple-element.29), channel_id=1, replica_groups={{0,16,32,48,64,80,96,112,128,144,160,176,192,208,224,240,256,272,288,30..., dimensions={0} | all-to-all | bytes 327680 | tf_op jit(solution)/shard_map/all_to_all | solution.py:261
  108.1 1.0 shard_map.91
  109.1 7.4 %all-to-all-start.4 = ((f32[64,1,640]{2,1,0:T(1,128)}), f32[64,1,640]{2,1,0:T(1,128)S(1)}, u32[]{:S(2)}, u32[]{:S(2)}) async-start(f32[64,1,640]{2,1,0:T(1,128)} %shard_map.91), calls=%async_computation.4 | async-start | bytes 327680 | tf_op jit(solution)/shard_map/all_to_all | solution.py:261
  116.6 3.6 %collective-permute-start.2 = (f32[224,384]{1,0:T(8,128)S(1)}, f32[224,384]{1,0:T(8,128)S(1)}, u32[]{:S(2)}, u32[]{:S(2)}) collective-permute-start(f32[224,384]{1,0:T(8,128)S(1)} %get-tuple-element.23), channel_id=1, source_target_pairs={{0,8},{8,0},{16,24},{24,16},{32,40},{40,32},{48,56},{56,48},{64,72... | collective-permute-start | bytes 1032200 | tf_op jit(solution)/shard_map/ppermute | solution.py:256
  120.2 10.7 %all-to-all-done.4.chip_ref = f32[64,1,640]{2,1,0:T(1,128)S(1)} async-done(((f32[64,1,640]{2,1,0:T(1,128)}), f32[64,1,640]{2,1,0:T(1,128)S(1)}, u32[]{:S(2)}, u32[]{:S(2)}) %all-to-all-start.4) | async-done | bytes 163872 | tf_op jit(solution)/shard_map/all_to_all | solution.py:261
  130.9 0.0 copy-start.7
  130.9 0.2 add.7
  131.1 5.9 %collective-permute-start.3 = (f32[64,1,640]{2,1,0:T(1,128)S(1)}, f32[64,1,640]{2,1,0:T(1,128)S(1)}, u32[]{:S(2)}, u32[]{:S(2)}) collective-permute-start(f32[64,1,640]{2,1,0:T(1,128)S(1)} %add.7), channel_id=1, source_target_pairs={{0,8},{8,0},{16,24},{24,16},{32,40},{40,32},{48,56},{56,48},{64,72... | collective-permute-start | bytes 491528 | tf_op jit(solution)/shard_map/ppermute | solution.py:256
  137.0 0.0 collective-permute-done.2.got_ref
  137.0 0.0 copy-done.7
  137.0 2.1 %shard_map.89 = (bf16[128,768]{1,0:T(8,128)(2,1)}, bf16[128,768]{1,0:T(8,128)(2,1)}, f32[128,768]{1,0:T(8,128)S(1)}, f32[128,768]{1,0:T(8,128)S(1)}) custom-call(bf16[128,768]{1,0:T(8,128)(2,1)S(1)} %copy-done.4, bf16[128,768]{1,0:T(8,128)(2,1)S(1)} %copy-done.1, bf16[128,768]{1,0:T(8,128)(2,1)S(1)} %copy-done.3, bf16[128,768]{1,0:T(8,128)(2,1)S(1)} %copy-done.5, ...), custom_call_target="tpu_custom_call" | custom-call | flops 500000000 | bytes 1000000 | tf_op jit(solution)/shard_map/pallas_call | solution.py:244
  139.1 0.0 collective-permute-done.3.there_ref
  139.1 1.2 shard_map.92
  (1 shorter events, 0.0 us)
Async XLA Ops:
  0.6 0.9 copy-start
  1.6 0.9 copy-start.2
  3.0 17.1 %collective-permute-start.1 = (f32[64,1,640]{2,1,0:T(1,128)S(1)}, f32[64,1,640]{2,1,0:T(1,128)S(1)}, u32[]{:S(2)}, u32[]{:S(2)}) collective-permute-start(f32[64,1,640]{2,1,0:T(1,128)S(1)} %get-tuple-element.20), channel_id=1, source_target_pairs={{0,8},{8,0},{16,24},{24,16},{32,40},{40,32},{48,56},{56,48},{64,72... | collective-permute-start | bytes 491528 | tf_op jit(solution)/shard_map/ppermute | solution.py:256
  20.0 10.3 %copy-start.3 = (bf16[128,768]{1,0:T(8,128)(2,1)S(1)}, bf16[128,768]{1,0:T(8,128)(2,1)}, u32[]{:S(2)}) copy-start(bf16[128,768]{1,0:T(8,128)(2,1)} %v_ref.9) | copy-start | bytes 589828
  20.0 10.3 %copy-start.4 = (bf16[128,768]{1,0:T(8,128)(2,1)S(1)}, bf16[128,768]{1,0:T(8,128)(2,1)}, u32[]{:S(2)}) copy-start(bf16[128,768]{1,0:T(8,128)(2,1)} %q_ref.9) | copy-start | bytes 589828
  20.0 10.3 %copy-start.5 = (bf16[128,768]{1,0:T(8,128)(2,1)S(1)}, bf16[128,768]{1,0:T(8,128)(2,1)}, u32[]{:S(2)}) copy-start(bf16[128,768]{1,0:T(8,128)(2,1)} %c_ref.7) | copy-start | bytes 589828
  20.9 9.5 %copy-start.1 = (bf16[128,768]{1,0:T(8,128)(2,1)S(1)}, bf16[128,768]{1,0:T(8,128)(2,1)}, u32[]{:S(2)}) copy-start(bf16[128,768]{1,0:T(8,128)(2,1)} %k_ref.9) | copy-start | bytes 589828
  20.9 25.2 %all-to-all-start = ((f32[64,1,640]{2,1,0:T(1,128)}), f32[64,1,640]{2,1,0:T(1,128)S(1)}, u32[]{:S(2)}, u32[]{:S(2)}) async-start(f32[64,1,640]{2,1,0:T(1,128)} %add.6), calls=%async_computation | async-start | bytes 327680 | tf_op jit(solution)/shard_map/all_to_all | solution.py:261
  30.5 23.8 %collective-permute-start = (f32[4,128,384]{2,1,0:T(8,128)S(1)}, f32[4,128,384]{2,1,0:T(8,128)S(1)}, u32[]{:S(2)}, u32[]{:S(2)}) collective-permute-start(f32[4,128,384]{2,1,0:T(8,128)S(1)} %shard_map.84), channel_id=1, source_target_pairs={{0,8},{8,0},{16,24},{24,16},{32,40},{40,32},{48,56},{56,48},{64,72... | collective-permute-start | bytes 2359304 | tf_op jit(solution)/shard_map/ppermute | solution.py:256
  47.1 7.2 %copy-start.8 = (f32[768]{0:T(1024)S(1)}, f32[768]{0:T(1024)}, u32[]{:S(2)}) copy-start(f32[768]{0:T(1024)} %param.8) | copy-start | bytes 9220
  47.1 21.9 %all-to-all-start.1 = ((f32[64,1,640]{2,1,0:T(1,128)}), f32[64,1,640]{2,1,0:T(1,128)S(1)}, u32[]{:S(2)}, u32[]{:S(2)}) async-start(f32[64,1,640]{2,1,0:T(1,128)} %shard_map.87), calls=%async_computation.1 | async-start | bytes 327680 | tf_op jit(solution)/shard_map/all_to_all | solution.py:261
  69.5 18.0 %copy-start.6 = (bf16[96,384]{1,0:T(8,128)(2,1)}, bf16[96,384]{1,0:T(8,128)(2,1)S(1)}, u32[]{:S(2)}) copy-start(bf16[96,384]{1,0:T(8,128)(2,1)S(1)} %get-tuple-element.22.low_ref) | copy-start | bytes 221188
  109.1 21.8 %all-to-all-start.4 = ((f32[64,1,640]{2,1,0:T(1,128)}), f32[64,1,640]{2,1,0:T(1,128)S(1)}, u32[]{:S(2)}, u32[]{:S(2)}) async-start(f32[64,1,640]{2,1,0:T(1,128)} %shard_map.91), calls=%async_computation.4 | async-start | bytes 327680 | tf_op jit(solution)/shard_map/all_to_all | solution.py:261
  116.6 20.4 %collective-permute-start.2 = (f32[224,384]{1,0:T(8,128)S(1)}, f32[224,384]{1,0:T(8,128)S(1)}, u32[]{:S(2)}, u32[]{:S(2)}) collective-permute-start(f32[224,384]{1,0:T(8,128)S(1)} %get-tuple-element.23), channel_id=1, source_target_pairs={{0,8},{8,0},{16,24},{24,16},{32,40},{40,32},{48,56},{56,48},{64,72... | collective-permute-start | bytes 1032200 | tf_op jit(solution)/shard_map/ppermute | solution.py:256
  130.9 6.1 %copy-start.7 = (bf16[96,384]{1,0:T(8,128)(2,1)S(1)}, bf16[96,384]{1,0:T(8,128)(2,1)}, u32[]{:S(2)}) copy-start(bf16[96,384]{1,0:T(8,128)(2,1)} %copy-done.6) | copy-start | bytes 221188
  131.1 8.0 %collective-permute-start.3 = (f32[64,1,640]{2,1,0:T(1,128)S(1)}, f32[64,1,640]{2,1,0:T(1,128)S(1)}, u32[]{:S(2)}, u32[]{:S(2)}) collective-permute-start(f32[64,1,640]{2,1,0:T(1,128)S(1)} %add.7), channel_id=1, source_target_pairs={{0,8},{8,0},{16,24},{24,16},{32,40},{40,32},{48,56},{56,48},{64,72... | collective-permute-start | bytes 491528 | tf_op jit(solution)/shard_map/ppermute | solution.py:256

commit v4 on v3

v4 whole, which is shorter than its diff:
```python
import jax
import jax.numpy as jnp
from jax import lax
from jax.experimental import pallas as pl
from jax.experimental.pallas import tpu as pltpu
from jax.sharding import PartitionSpec as P

HEAD_DIM = 96
D = 6144
TOK = 128
LANES = 128
HALF_HEADS = 4
HALF = HALF_HEADS * HEAD_DIM
CHIPS = 64
CORES = 2
PIECE = 640

epsilon = 1e-06
F32 = jnp.float32
BF16 = jnp.bfloat16
VMEM = pl.BlockSpec(memory_space=pltpu.VMEM)
NN = (((1,), (0,)), ((), ()))
NT = (((1,), (1,)), ((), ()))
TN = (((0,), (0,)), ((), ()))


def mm(a, b, dims):
    return lax.dot_general(a, b, dims, preferred_element_type=F32)


def half(g):
    return slice(g * HALF, (g + 1) * HALF)


def head_masks(rows):
    lane = lax.broadcasted_iota(jnp.int32, (rows, HALF), 1)
    return [(lane >= h * HEAD_DIM) & (lane < (h + 1) * HEAD_DIM) for h in range(HALF_HEADS)]


def spread(x):
    return jnp.concatenate([x * m.astype(BF16) for m in head_masks(x.shape[0])], axis=0)


def diagonal(x):
    rows = x.shape[0] // HALF_HEADS
    masks = head_masks(rows)
    out = x[:rows]
    for h in range(1, HALF_HEADS):
        out = jnp.where(masks[h], x[h * rows : (h + 1) * rows], out)
    return out


def to_pieces(state):
    rest = state[64:96]
    tail = rest[:, 256:384]
    return jnp.concatenate(
        [
            state[0:64],
            jnp.concatenate([rest[:, 0:128], rest[:, 128:256]], axis=0),
            jnp.concatenate([tail, pltpu.roll(tail, 64, 1)], axis=0),
        ],
        axis=1,
    )


def from_pieces(pieces):
    low = lax.broadcasted_iota(jnp.int32, (32, LANES), 1) < 64
    tail = jnp.where(low, pieces[0:32, 512:640], pltpu.roll(pieces[32:64, 512:640], 64, 1))
    rest = jnp.concatenate([pieces[0:32, 384:512], pieces[32:64, 384:512], tail], axis=1)
    return jnp.concatenate([pieces[:, 0:384], rest], axis=0)


def silu_low(x):
    x = x.astype(F32)
    return (x * jax.nn.sigmoid(x)).astype(BF16)


def silu_slope(x):
    x = x.astype(F32)
    sig = jax.nn.sigmoid(x)
    return sig * (1.0 + x * (1.0 - sig))


def causal4():
    row = lax.broadcasted_iota(jnp.int32, (TOK, TOK), 0)
    col = lax.broadcasted_iota(jnp.int32, (TOK, TOK), 1)
    keep = jnp.where(row >= col, 1.0, 0.0)
    return jnp.concatenate([keep] * HALF_HEADS, axis=1) > 0.5


def by_head(x):
    return jnp.concatenate([x[:, h * TOK : (h + 1) * TOK] for h in range(HALF_HEADS)], axis=0)


def core_index():
    return lax.axis_index("ctx") % CORES


def pick(own, x):
    first = (core_index() == 0) == own
    return jnp.where(first, x[:, half(0)], x[:, half(1)])


def in_order(own, other):
    first = core_index() == 0
    return jnp.where(first, own, other), jnp.where(first, other, own)


def state_kernel(k_hbm, v_hbm, mine_ref, theirs_ref, k_ref, v_ref, sems):
    copies = []
    for g in range(CORES):
        pair = []
        for i, (source, target) in enumerate(((k_hbm, k_ref), (v_hbm, v_ref))):
            copy = pltpu.make_async_copy(
                source.at[:, pl.ds(g * HALF, HALF)], target.at[g], sems.at[2 * g + i]
            )
            copy.start()
            pair.append(copy)
        copies.append(pair)
    states = []
    for g in range(CORES):
        for copy in copies[g]:
            copy.wait()
        states.append(to_pieces(diagonal(mm(silu_low(k_ref[g]), v_ref[g], TN))))
    low = core_index() == 0
    mine_ref[:, 0, :] = jnp.where(low, states[0], states[1])
    theirs_ref[:, 0, :] = jnp.where(low, states[1], states[0])


def send_kernel(after_ref, q_ref, k_ref, v_ref, c_ref, out_ref):
    for i, ref in enumerate((q_ref, k_ref, v_ref, c_ref)):
        out_ref[i] = pick(False, ref[...]).astype(F32)


def attention(q_feat, k_feat):
    return jnp.where(causal4(), mm(q_feat, spread(k_feat), NT), 0.0).astype(BF16)


def intra_kernel(
    q_ref, k_ref, v_ref, c_ref, gain_ref, got_ref, mine_ref, received_ref,
    intra_ref, q_feat_ref, upstream_ref, extra_ref,
):
    core = core_index()
    gain = pick(True, gain_ref[...])
    mine = [pick(True, ref[...]) for ref in (q_ref, k_ref, v_ref, c_ref)]
    others = [got_ref[i].astype(BF16) for i in range(4)]
    for i, (q, k, v, c) in enumerate((mine, others)):
        q_feat = silu_low(q)
        q_feat_ref[i] = q_feat
        upstream_ref[i] = c.astype(F32) * gain
        intra_ref[i] = mm(attention(q_feat, silu_low(k)), spread(v), NN)
    extra_ref[0] = from_pieces(jnp.where(core == 1, received_ref[:, 0, :], 0.0))
    extra_ref[1] = from_pieces(jnp.where(core == 0, mine_ref[:, 0, :], 0.0))


def scan_kernel(backward, pieces_ref, after_ref, out_ref, done_ref):
    row = lax.broadcasted_iota(jnp.int32, (CHIPS, CHIPS), 0)
    col = lax.broadcasted_iota(jnp.int32, (CHIPS, CHIPS), 1)
    before = jnp.where(row < col if backward else row > col, 1.0, 0.0).astype(BF16)
    rest = pieces_ref[:, 0, :]
    terms = []
    for _ in range(3):
        term = rest.astype(BF16)
        rest = rest - term.astype(F32)
        terms.append(term)
    out_ref[:, 0, :] = mm(
        jnp.concatenate([before] * 3, axis=1), jnp.concatenate(terms, axis=0), NN
    )
    done_ref[...] = jnp.zeros_like(done_ref)


def lane_sums(x):
    part = x[:, 0:LANES]
    for i in range(1, x.shape[1] // LANES):
        part = part + x[:, i * LANES : (i + 1) * LANES]
    return jnp.sum(part.T, axis=0, keepdims=True)


def raw_kernel(q_feat_ref, upstream_ref, intra_ref, extra_ref, chip_ref, raw_ref, prefix_ref, parts_ref):
    chip = from_pieces(chip_ref[:, 0, :])
    sums = []
    for i in range(CORES):
        state = (chip + extra_ref[i]).astype(BF16)
        prefix_ref[i] = state
        raw = intra_ref[i] + mm(q_feat_ref[i], spread(state), NN)
        raw_ref[i] = raw
        sums.append(
            jnp.concatenate([lane_sums(raw * raw), lane_sums(upstream_ref[i] * raw)], axis=0)
        )
    sums = jnp.concatenate(in_order(*sums), axis=0)
    parts_ref[...] = jnp.broadcast_to(sums[None], parts_ref.shape)


def scales(totals):
    square = jnp.broadcast_to(totals[0:1], (TOK, LANES)).T
    cross = jnp.broadcast_to(totals[1:2], (TOK, LANES)).T
    mean = square * (1.0 / D) + epsilon
    pair = lax.rsqrt(mean), cross / (D * mean)
    return [jnp.concatenate([x] * (HALF // LANES), axis=1) for x in pair]


def gradient(upstream, raw, inverse, pull):
    return ((upstream - raw * pull) * inverse).astype(BF16)


def own_and_other(parts_ref):
    totals = jnp.sum(parts_ref[...], axis=0)
    return in_order(totals[0:2], totals[2:4])


def grad_state_kernel(
    q_feat_ref, upstream_ref, raw_ref, prefix_ref, parts_ref,
    sum_ref, here_ref, there_ref, give_ref,
):
    core = core_index()
    states = []
    for i, totals in enumerate(own_and_other(parts_ref)):
        d_raw = gradient(upstream_ref[i], raw_ref[i], *scales(totals))
        states.append(diagonal(mm(q_feat_ref[i], d_raw, TN)))
    own, other = states
    sum_ref[:, 0, :] = to_pieces(own + other)
    here_ref[...] = jnp.where(core == 0, other, 0.0)
    there_ref[:, 0, :] = to_pieces(jnp.where(core == 1, own, 0.0))
    give_ref[0:TOK, :] = raw_ref[1]
    give_ref[TOK:, :] = prefix_ref[1].astype(F32)


def back_kernel(
    q_ref, k_ref, v_ref, c_ref, gain_ref, raw_ref, prefix_ref, got_ref, parts_ref,
    attended_ref, grad_q_ref, grad_kf_ref, grad_vf_ref, k_feat_ref, slope_ref, done_ref,
):
    keep = causal4()
    inverse, pull = scales(own_and_other(parts_ref)[0])
    raws = in_order(raw_ref[0], got_ref[0:TOK])
    prefixes = in_order(prefix_ref[0].astype(F32), got_ref[TOK:])
    for g in range(CORES):
        q, k, raw, gain = q_ref[:, half(g)], k_ref[:, half(g)], raws[g], gain_ref[:, half(g)]
        q_feat, k_feat = silu_low(q), silu_low(k)
        k_feat_ref[:, half(g)] = k_feat
        slope_ref[:, half(g)] = silu_slope(k)
        attended_ref[:, half(g)] = (raw * inverse * gain).astype(BF16)
        d_raw = gradient(c_ref[:, half(g)].astype(F32) * gain, raw, inverse, pull)
        back = jnp.where(keep, mm(d_raw, spread(v_ref[:, half(g)]), NT), 0.0).astype(BF16)
        grad_qf = mm(back, spread(k_feat), NN) + mm(d_raw, spread(prefixes[g].astype(BF16)), NT)
        grad_q_ref[:, half(g)] = (grad_qf * silu_slope(q)).astype(BF16)
        grad_kf_ref[:, half(g)] = mm(by_head(back), spread(q_feat), TN)
        grad_vf_ref[:, half(g)] = mm(by_head(attention(q_feat, k_feat)), spread(d_raw), TN)
    done_ref[...] = jnp.zeros_like(done_ref)


def finished(own, refs, later):
    v, k_feat, slope, grad_kf, grad_vf = (pick(own, ref[...]) for ref in refs)
    later = spread(later.astype(BF16))
    grad_k = (grad_kf + mm(v, later, NT)) * slope
    return grad_k.astype(BF16), (grad_vf + mm(k_feat, later, NN)).astype(BF16)


def own_kernel(
    v_ref, k_feat_ref, slope_ref, grad_kf_ref, grad_vf_ref, chip_ref, here_ref, grad_k_ref, grad_v_ref
):
    refs = v_ref, k_feat_ref, slope_ref, grad_kf_ref, grad_vf_ref
    later = from_pieces(chip_ref[:, 0, :]) + here_ref[...]
    grad_k_ref[...], grad_v_ref[...] = finished(True, refs, later)


def last_kernel(
    v_ref, k_feat_ref, slope_ref, grad_kf_ref, grad_vf_ref, there_ref, own_k_ref, own_v_ref,
    grad_k_hbm, grad_v_hbm, k_ref, other_ref, sems,
):
    core = core_index()
    own = pl.ds(pl.multiple_of(core * HALF, HALF), HALF)
    other = pl.ds(pl.multiple_of((1 - core) * HALF, HALF), HALF)
    copies = [
        pltpu.make_async_copy(own_k_ref, grad_k_hbm.at[:, own], sems.at[0]),
        pltpu.make_async_copy(own_v_ref, grad_v_hbm.at[:, own], sems.at[1]),
        pltpu.make_async_copy(k_ref, grad_k_hbm.at[:, other], sems.at[2]),
        pltpu.make_async_copy(other_ref, grad_v_hbm.at[:, other], sems.at[3]),
    ]
    copies[0].start()
    copies[1].start()
    refs = v_ref, k_feat_ref, slope_ref, grad_kf_ref, grad_vf_ref
    k_ref[...], other_ref[...] = finished(False, refs, from_pieces(there_ref[:, 0, :]))
    copies[2].start()
    copies[3].start()
    for copy in copies:
        copy.wait()


def call(kernel, outs, *args, flops=0, in_hbm=False, out_hbm=False, scratch=(), room=32):
    in_space, out_space = (
        pl.BlockSpec(memory_space=pltpu.HBM) if far else VMEM for far in (in_hbm, out_hbm)
    )
    return pl.pallas_call(
        kernel,
        out_shape=[jax.ShapeDtypeStruct(shape, kind) for shape, kind in outs],
        in_specs=[in_space] * len(args),
        out_specs=[out_space] * len(outs),
        scratch_shapes=list(scratch),
        compiler_params=pltpu.CompilerParams(vmem_limit_bytes=room * 1024 * 1024),
        cost_estimate=pl.CostEstimate(flops=flops, bytes_accessed=1_000_000, transcendentals=0),
    )(*args)


def swap_cores(x):
    pairs = [(i, i ^ 1) for i in range(CHIPS * CORES)]
    return lax.ppermute(x, "ctx", pairs)


def across_chips(x):
    groups = [[chip * CORES + core for chip in range(CHIPS)] for core in range(CORES)]
    return lax.all_to_all(x, "ctx", 0, 0, axis_index_groups=groups)


def over_heads(x):
    size = CORES * lax.axis_size("head")
    groups = [[chip * size + i for i in range(size)] for chip in range(CHIPS)]
    return lax.all_to_all(x, ("ctx", "head"), 0, 0, axis_index_groups=groups)


PIECES = ((CHIPS, 1, PIECE), F32)
DONE = ((8, LANES), F32)
WIDE = ((TOK, CORES * HALF), F32)
WIDE_LOW = ((TOK, CORES * HALF), BF16)
HALF_LOW = ((TOK, HALF), BF16)
BLOCKS = ((CORES, TOK, HALF), F32)
BLOCKS_LOW = ((CORES, TOK, HALF), BF16)


def scan_sums(pieces, after, backward):
    def kernel(*refs):
        scan_kernel(backward, *refs)

    return call(kernel, [PIECES, DONE], pieces, after)


def per_device(queries, key_input, value_input, norm_gain, cotangent):
    sharers = CORES * lax.axis_size("head")
    gain = norm_gain.reshape(1, -1)
    load = [pltpu.VMEM((CORES, TOK, HALF), BF16)] * 2 + [pltpu.SemaphoreType.DMA((4,))]
    mine, theirs = call(
        state_kernel, [PIECES, PIECES], key_input, value_input, in_hbm=True, scratch=load, room=60
    )
    received = swap_cores(theirs)
    summed, done = scan_sums(across_chips(mine + received), jnp.zeros(*DONE), False)
    (given,) = call(
        send_kernel, [((4, TOK, HALF), F32)], done, queries, key_input, value_input, cotangent
    )
    got = swap_cores(given)
    intra, q_feat, upstream, extra = call(
        intra_kernel,
        [BLOCKS, BLOCKS_LOW, BLOCKS, ((CORES, HEAD_DIM, HALF), F32)],
        queries, key_input, value_input, cotangent, gain, got, mine, received,
        flops=200_000_000,
    )
    raw, prefix, parts = call(
        raw_kernel,
        [BLOCKS, ((CORES, HEAD_DIM, HALF), BF16), ((sharers, 4, TOK), F32)],
        q_feat, upstream, intra, extra, across_chips(summed),
    )
    parts = over_heads(parts)
    total, here, there, give = call(
        grad_state_kernel,
        [PIECES, ((HEAD_DIM, HALF), F32), PIECES, ((TOK + HEAD_DIM, HALF), F32)],
        q_feat, upstream, raw, prefix, parts,
    )
    attended, grad_query, grad_kf, grad_vf, k_feat, slope, done = call(
        back_kernel,
        [WIDE_LOW, WIDE_LOW, WIDE, WIDE, WIDE_LOW, WIDE, DONE],
        queries, key_input, value_input, cotangent, gain, raw, prefix, swap_cores(give), parts,
        flops=500_000_000,
    )
    summed, _ = scan_sums(across_chips(total), done, True)
    chip = across_chips(summed)
    there = swap_cores(chip + there)
    parts = value_input, k_feat, slope, grad_kf, grad_vf
    own = call(own_kernel, [HALF_LOW, HALF_LOW], *parts, chip, here, flops=50_000_000)
    store = [pltpu.VMEM((TOK, HALF), BF16)] * 2 + [pltpu.SemaphoreType.DMA((4,))]
    grad_key, grad_value = call(
        last_kernel, [WIDE_LOW, WIDE_LOW], *parts, there, *own, out_hbm=True, scratch=store
    )
    return (attended, grad_query, grad_key, grad_value)


def solution(mesh):
    in_specs = (P("ctx", "head"), P("ctx", "head"), P("ctx", "head"), P("head"), P("ctx", "head"))
    out_specs = (P("ctx", "head"), P("ctx", "head"), P("ctx", "head"), P("ctx", "head"))
    return jax.shard_map(
        per_device, mesh=mesh, in_specs=in_specs, out_specs=out_specs, check_vma=False
    )
```

time: 141 us -> 145 us (1.028)
  blocking collectives: 38.1 us -> 62.1 us
  waiting for transfers between devices: 38.6 us -> 26.7 us
  starting transfers between devices: 52.2 us -> 41.2 us
  Pallas kernels: 7.66 us -> 11 us
    all_to_all x1 -> x2, blocking collectives: 20.6 us -> 46.6 us  [across_chips(): return lax.all_to_all(x, 'ctx', 0, 0, axis_index_groups=groups)]
    all_to_all x3 -> x2, waiting for transfers between devices: 37.6 us -> 23.6 us  [across_chips(): return lax.all_to_all(x, 'ctx', 0, 0, axis_index_groups=groups)]
    all_to_all x3 -> x2, starting transfers between devices: 24 us -> 12.3 us  [across_chips(): return lax.all_to_all(x, 'ctx', 0, 0, axis_index_groups=groups)]
    pallas_call x9 -> x10, Pallas kernels: 7.66 us -> 11 us  [call(): pl.pallas_call(kernel, out_shape=[jax.ShapeDtypeStruct(shape, kind) for s...]
    ppermute x4, waiting for transfers between devices: 1.01 us -> 3.11 us  [swap_cores(): return lax.ppermute(x, 'ctx', pairs)]
    all_to_all x1, blocking collectives: 17.4 us -> 15.5 us  [over_heads(): return lax.all_to_all(x, ('ctx', 'head'), 0, 0, axis_index_groups=groups)]
  transfers between devices with their start and end apart: 7 -> 6, of which waited for: 4 -> 5; matrix products, arithmetic and copies ran while one was open for 0% -> 0% of each run, Pallas kernels for 3% -> 2%
where the time goes in v4:
time: 145 us
  blocking collectives  62.1 us (43%)
  starting transfers between devices  41.2 us (28%)
  waiting for transfers between devices  26.7 us (18%)
  Pallas kernels  11 us (8%)
  local copies, waits for them, and re-layouts  1.71 us (1%)
    all_to_all x2, blocking collectives, across_chips(): return lax.all_to_all(x, 'ctx', 0, 0, axis_index_groups=groups)  46.6 us
    ppermute x4, starting transfers between devices, swap_cores(): return lax.ppermute(x, 'ctx', pairs)  28.9 us
    all_to_all x2, waiting for transfers between devices, across_chips(): return lax.all_to_all(x, 'ctx', 0, 0, axis_index_groups=groups)  23.6 us
    all_to_all x1, blocking collectives, over_heads(): return lax.all_to_all(x, ('ctx', 'head'), 0, 0, axis_index_groups=groups)  15.5 us
    all_to_all x2, starting transfers between devices, across_chips(): return lax.all_to_all(x, 'ctx', 0, 0, axis_index_groups=groups)  12.3 us
    pallas_call x10, Pallas kernels, call(): pl.pallas_call(kernel, out_shape=[jax.ShapeDtypeStruct(shape, kind) for s...  11 us
    ppermute x4, waiting for transfers between devices, swap_cores(): return lax.ppermute(x, 'ctx', pairs)  3.11 us
  transfers between devices with their start and end apart: 6, of which 5 were waited for; matrix products, arithmetic and copies ran while one was open for 0% of the time, Pallas kernels for 2%

profile of v4, /device:TPU:1, one launch (start us, length us, event | category | flops | bytes accessed | tf_op | source)
XLA Modules:
  0.0 144.8 jit_solution(10999329489026464846)
XLA Ops:
  0.6 2.4 %shard_map.84 = (f32[64,1,640]{2,1,0:T(1,128)}, f32[64,1,640]{2,1,0:T(1,128)}) custom-call(bf16[128,768]{1,0:T(8,128)(2,1)} %k_ref.5, bf16[128,768]{1,0:T(8,128)(2,1)} %v_ref.9), custom_call_target="tpu_custom_call" | custom-call | bytes 1000000 | tf_op jit(solution)/shard_map/pallas_call | solution.py:293
  3.0 16.1 %collective-permute-start = (f32[64,1,640]{2,1,0:T(1,128)}, f32[64,1,640]{2,1,0:T(1,128)S(1)}, u32[]{:S(2)}, u32[]{:S(2)}) collective-permute-start(f32[64,1,640]{2,1,0:T(1,128)} %get-tuple-element.32), channel_id=1, source_target_pairs={{0,8},{8,0},{16,24},{24,16},{32,40},{40,32},{48,56},{56,48},{64,72... | collective-permute-start | bytes 491528 | tf_op jit(solution)/shard_map/ppermute | solution.py:306
  19.1 1.2 collective-permute-done.received_ref
  20.3 0.0 copy-start.2
  20.3 0.0 copy-start.3
  20.3 1.1 add.6
  21.4 0.0 copy-start
  21.4 0.0 copy-start.1
  21.4 25.0 %all_to_all.25.refs_0_ = f32[64,1,640]{2,1,0:T(1,128)S(1)} all-to-all(f32[64,1,640]{2,1,0:T(1,128)S(1)} %add.6), channel_id=1, replica_groups={{0,16,32,48,64,80,96,112,128,144,160,176,192,208,224,240,256,272,288,30..., dimensions={0} | all-to-all | bytes 327680 | tf_op jit(solution)/shard_map/all_to_all | solution.py:311
  46.5 1.6 %shard_map.85 = (f32[64,1,640]{2,1,0:T(1,128)}, f32[8,128]{1,0:T(8,128)S(1)}) custom-call(f32[64,1,640]{2,1,0:T(1,128)S(1)} %all_to_all.25.refs_0_, f32[8,128]{1,0:T(8,128)S(1)} %broadcast_in_dim.3.refs_1_), custom_call_target="tpu_custom_call" | custom-call | bytes 1000000 | tf_op jit(solution)/shard_map/pallas_call | solution.py:293
  48.1 0.0 copy-done.2
  48.1 0.0 copy-done.3
  48.1 0.0 copy-done
  48.1 0.0 copy-done.1
  48.1 0.1 shard_map.86
  48.2 4.0 %collective-permute-start.1 = (f32[4,128,384]{2,1,0:T(8,128)S(1)}, f32[4,128,384]{2,1,0:T(8,128)S(1)}, u32[]{:S(2)}, u32[]{:S(2)}) collective-permute-start(f32[4,128,384]{2,1,0:T(8,128)S(1)} %shard_map.86), channel_id=1, source_target_pairs={{0,8},{8,0},{16,24},{24,16},{32,40},{40,32},{48,56},{56,48},{64,72... | collective-permute-start | bytes 2359304 | tf_op jit(solution)/shard_map/ppermute | solution.py:306
  52.2 0.0 copy-start.7
  52.2 0.0 copy-start.4
  52.2 6.3 %all-to-all-start.1 = ((f32[64,1,640]{2,1,0:T(1,128)}), f32[64,1,640]{2,1,0:T(1,128)S(1)}, u32[]{:S(2)}, u32[]{:S(2)}) async-start(f32[64,1,640]{2,1,0:T(1,128)} %get-tuple-element.38), calls=%async_computation.1 | async-start | bytes 327680 | tf_op jit(solution)/shard_map/all_to_all | solution.py:311
  58.5 0.0 copy-done.7
  58.5 0.0 collective-permute-done.1.got_ref
  58.5 0.0 copy-done.4
  58.5 0.8 shard_map.87
  59.4 0.0 copy-start.5
  59.4 0.7 copy-done.5
  60.1 14.8 %all-to-all-done.1.chip_ref = f32[64,1,640]{2,1,0:T(1,128)S(1)} async-done(((f32[64,1,640]{2,1,0:T(1,128)}), f32[64,1,640]{2,1,0:T(1,128)S(1)}, u32[]{:S(2)}, u32[]{:S(2)}) %all-to-all-start.1) | async-done | bytes 163872 | tf_op jit(solution)/shard_map/all_to_all | solution.py:311
  74.9 0.0 copy-start.6
  74.9 1.0 copy-done.6
  75.8 0.4 shard_map.88
  76.3 15.5 %all_to_all.26.parts_ref = f32[16,4,128]{2,1,0:T(4,128)S(1)} all-to-all(f32[16,4,128]{2,1,0:T(4,128)S(1)} %get-tuple-element.41), channel_id=1, replica_groups={{0,1,2,3,4,5,6,7,8,9,10,11,12,13,14,15},{16,17,18,19,20,21,22,23,24,25,..., dimensions={0} | all-to-all | bytes 65536 | tf_op jit(solution)/shard_map/all_to_all | solution.py:317
  91.8 1.2 shard_map.89
  93.0 6.1 %all-to-all-start.3 = ((f32[64,1,640]{2,1,0:T(1,128)}), f32[64,1,640]{2,1,0:T(1,128)S(1)}, u32[]{:S(2)}, u32[]{:S(2)}) async-start(f32[64,1,640]{2,1,0:T(1,128)} %get-tuple-element.49), calls=%async_computation.3 | async-start | bytes 327680 | tf_op jit(solution)/shard_map/all_to_all | solution.py:311
  99.0 2.9 %collective-permute-start.2 = (f32[224,384]{1,0:T(8,128)S(1)}, f32[224,384]{1,0:T(8,128)S(1)}, u32[]{:S(2)}, u32[]{:S(2)}) collective-permute-start(f32[224,384]{1,0:T(8,128)S(1)} %get-tuple-element.42), channel_id=1, source_target_pairs={{0,8},{8,0},{16,24},{24,16},{32,40},{40,32},{48,56},{56,48},{64,72... | collective-permute-start | bytes 1032200 | tf_op jit(solution)/shard_map/ppermute | solution.py:306
  102.0 1.3 collective-permute-done.2.got_ref
  103.2 2.0 %shard_map.90 = (bf16[128,768]{1,0:T(8,128)(2,1)}, bf16[128,768]{1,0:T(8,128)(2,1)}, f32[128,768]{1,0:T(8,128)S(1)}, f32[128,768]{1,0:T(8,128)S(1)}, bf16[128,76...) custom-call(bf16[128,768]{1,0:T(8,128)(2,1)S(1)} %copy-done.2, bf16[128,768]{1,0:T(8,128)(2,1)S(1)} %copy-done.1, ...), custom_call_target="tpu_custom_call" | custom-call | flops 500000000 | bytes 1000000 | tf_op jit(solution)/shard_map/pallas_call | solution.py:293
  105.3 8.9 %all-to-all-done.3.refs_0_ = f32[64,1,640]{2,1,0:T(1,128)S(1)} async-done(((f32[64,1,640]{2,1,0:T(1,128)}), f32[64,1,640]{2,1,0:T(1,128)S(1)}, u32[]{:S(2)}, u32[]{:S(2)}) %all-to-all-start.3) | async-done | bytes 163872 | tf_op jit(solution)/shard_map/all_to_all | solution.py:311
  114.1 1.0 shard_map.91
  115.1 21.6 %all_to_all.27.chip_ref = f32[64,1,640]{2,1,0:T(1,128)S(1)} all-to-all(f32[64,1,640]{2,1,0:T(1,128)S(1)} %get-tuple-element.51), channel_id=1, replica_groups={{0,16,32,48,64,80,96,112,128,144,160,176,192,208,224,240,256,272,288,30..., dimensions={0} | all-to-all | bytes 327680 | tf_op jit(solution)/shard_map/all_to_all | solution.py:311
  136.7 0.2 add.7
  136.8 5.9 %collective-permute-start.3 = (f32[64,1,640]{2,1,0:T(1,128)S(1)}, f32[64,1,640]{2,1,0:T(1,128)S(1)}, u32[]{:S(2)}, u32[]{:S(2)}) collective-permute-start(f32[64,1,640]{2,1,0:T(1,128)S(1)} %add.7), channel_id=1, source_target_pairs={{0,8},{8,0},{16,24},{24,16},{32,40},{40,32},{48,56},{56,48},{64,72... | collective-permute-start | bytes 491528 | tf_op jit(solution)/shard_map/ppermute | solution.py:306
  142.7 0.4 shard_map.92
  143.1 0.6 collective-permute-done.3.there_ref
  143.7 1.1 shard_map.93
  (2 shorter events, 0.0 us)
Async XLA Ops:
  3.0 17.3 %collective-permute-start = (f32[64,1,640]{2,1,0:T(1,128)}, f32[64,1,640]{2,1,0:T(1,128)S(1)}, u32[]{:S(2)}, u32[]{:S(2)}) collective-permute-start(f32[64,1,640]{2,1,0:T(1,128)} %get-tuple-element.32), channel_id=1, source_target_pairs={{0,8},{8,0},{16,24},{24,16},{32,40},{40,32},{48,56},{56,48},{64,72... | collective-permute-start | bytes 491528 | tf_op jit(solution)/shard_map/ppermute | solution.py:306
  20.3 27.8 %copy-start.2 = (bf16[128,768]{1,0:T(8,128)(2,1)S(1)}, bf16[128,768]{1,0:T(8,128)(2,1)}, u32[]{:S(2)}) copy-start(bf16[128,768]{1,0:T(8,128)(2,1)} %q_ref.5) | copy-start | bytes 589828
  20.3 27.8 %copy-start.3 = (bf16[128,768]{1,0:T(8,128)(2,1)S(1)}, bf16[128,768]{1,0:T(8,128)(2,1)}, u32[]{:S(2)}) copy-start(bf16[128,768]{1,0:T(8,128)(2,1)} %c_ref.5) | copy-start | bytes 589828
  21.4 26.7 %copy-start = (bf16[128,768]{1,0:T(8,128)(2,1)S(1)}, bf16[128,768]{1,0:T(8,128)(2,1)}, u32[]{:S(2)}) copy-start(bf16[128,768]{1,0:T(8,128)(2,1)} %v_ref.9) | copy-start | bytes 589828
  21.4 26.7 %copy-start.1 = (bf16[128,768]{1,0:T(8,128)(2,1)S(1)}, bf16[128,768]{1,0:T(8,128)(2,1)}, u32[]{:S(2)}) copy-start(bf16[128,768]{1,0:T(8,128)(2,1)} %k_ref.5) | copy-start | bytes 589828
  48.2 10.3 %collective-permute-start.1 = (f32[4,128,384]{2,1,0:T(8,128)S(1)}, f32[4,128,384]{2,1,0:T(8,128)S(1)}, u32[]{:S(2)}, u32[]{:S(2)}) collective-permute-start(f32[4,128,384]{2,1,0:T(8,128)S(1)} %shard_map.86), channel_id=1, source_target_pairs={{0,8},{8,0},{16,24},{24,16},{32,40},{40,32},{48,56},{56,48},{64,72... | collective-permute-start | bytes 2359304 | tf_op jit(solution)/shard_map/ppermute | solution.py:306
  52.2 6.3 %copy-start.7 = (f32[768]{0:T(1024)S(1)}, f32[768]{0:T(1024)}, u32[]{:S(2)}) copy-start(f32[768]{0:T(1024)} %param.8) | copy-start | bytes 9220
  52.2 6.3 %copy-start.4 = (f32[64,1,640]{2,1,0:T(1,128)S(1)}, f32[64,1,640]{2,1,0:T(1,128)}, u32[]{:S(2)}) copy-start(f32[64,1,640]{2,1,0:T(1,128)} %get-tuple-element.31.mine_ref) | copy-start | bytes 491524
  52.2 22.6 %all-to-all-start.1 = ((f32[64,1,640]{2,1,0:T(1,128)}), f32[64,1,640]{2,1,0:T(1,128)S(1)}, u32[]{:S(2)}, u32[]{:S(2)}) async-start(f32[64,1,640]{2,1,0:T(1,128)} %get-tuple-element.38), calls=%async_computation.1 | async-start | bytes 327680 | tf_op jit(solution)/shard_map/all_to_all | solution.py:311
  59.4 0.7 copy-start.5
  74.9 1.0 copy-start.6
  93.0 21.2 %all-to-all-start.3 = ((f32[64,1,640]{2,1,0:T(1,128)}), f32[64,1,640]{2,1,0:T(1,128)S(1)}, u32[]{:S(2)}, u32[]{:S(2)}) async-start(f32[64,1,640]{2,1,0:T(1,128)} %get-tuple-element.49), calls=%async_computation.3 | async-start | bytes 327680 | tf_op jit(solution)/shard_map/all_to_all | solution.py:311
  99.0 4.2 %collective-permute-start.2 = (f32[224,384]{1,0:T(8,128)S(1)}, f32[224,384]{1,0:T(8,128)S(1)}, u32[]{:S(2)}, u32[]{:S(2)}) collective-permute-start(f32[224,384]{1,0:T(8,128)S(1)} %get-tuple-element.42), channel_id=1, source_target_pairs={{0,8},{8,0},{16,24},{24,16},{32,40},{40,32},{48,56},{56,48},{64,72... | collective-permute-start | bytes 1032200 | tf_op jit(solution)/shard_map/ppermute | solution.py:306
  136.8 6.9 %collective-permute-start.3 = (f32[64,1,640]{2,1,0:T(1,128)S(1)}, f32[64,1,640]{2,1,0:T(1,128)S(1)}, u32[]{:S(2)}, u32[]{:S(2)}) collective-permute-start(f32[64,1,640]{2,1,0:T(1,128)S(1)} %add.7), channel_id=1, source_target_pairs={{0,8},{8,0},{16,24},{24,16},{32,40},{40,32},{48,56},{56,48},{64,72... | collective-permute-start | bytes 491528 | tf_op jit(solution)/shard_map/ppermute | solution.py:306

commit v5 on v3

--- a/solution.py
+++ b/solution.py
@@ -106,9 +106,9 @@
     return jnp.where(first, own, other), jnp.where(first, other, own)
 
 
-def state_kernel(k_ref, v_ref, mine_ref, theirs_ref):
+def state_kernel(pair_ref, mine_ref, theirs_ref):
     first, second = (
-        to_pieces(diagonal(mm(silu_low(k_ref[:, half(g)]), v_ref[:, half(g)], TN)))
+        to_pieces(diagonal(mm(silu_low(pair_ref[0, :, half(g)]), pair_ref[1, :, half(g)], TN)))
         for g in range(CORES)
     )
     low = core_index() == 0
@@ -135,9 +135,15 @@
 def scan_kernel(backward, pieces_ref, out_ref):
     row = lax.broadcasted_iota(jnp.int32, (CHIPS, CHIPS), 0)
     col = lax.broadcasted_iota(jnp.int32, (CHIPS, CHIPS), 1)
-    before = jnp.where(row < col if backward else row > col, 1.0, 0.0)
-    out_ref[:, 0, :] = lax.dot_general(
-        before, pieces_ref[:, 0, :], NN, precision=lax.Precision.HIGHEST, preferred_element_type=F32
+    before = jnp.where(row < col if backward else row > col, 1.0, 0.0).astype(BF16)
+    rest = pieces_ref[:, 0, :]
+    terms = []
+    for _ in range(3):
+        term = rest.astype(BF16)
+        rest = rest - term.astype(F32)
+        terms.append(term)
+    out_ref[:, 0, :] = mm(
+        jnp.concatenate([before] * 3, axis=1), jnp.concatenate(terms, axis=0), NN
     )
 
 
@@ -191,9 +197,8 @@
 
 
 def grad_state_kernel(
-    q_ref, c_ref, gain_ref, got_ref, raw_ref, parts_ref, sum_ref, here_ref, there_ref
-):
-    core = core_index()
+    q_ref, c_ref, gain_ref, got_ref, raw_ref, parts_ref, sum_ref, own_ref, other_ref
+):
     gain = pick(True, gain_ref[...])
     q, c = pick(True, q_ref[...]), pick(True, c_ref[...])
     states = []
@@ -201,16 +206,18 @@
         zip((q, got_ref[0].astype(BF16)), (c, got_ref[3]), own_and_other(parts_ref))
     ):
         d_raw = gradient(c, gain, raw_ref[i], *scales(totals))
-        states.append(to_pieces(diagonal(mm(silu_low(q), d_raw, TN))))
-    sum_ref[:, 0, :] = states[0] + states[1]
-    here_ref[:, 0, :] = jnp.where(core == 0, states[1], 0.0)
-    there_ref[:, 0, :] = jnp.where(core == 1, states[0], 0.0)
+        states.append(diagonal(mm(silu_low(q), d_raw, TN)))
+    own_ref[...], other_ref[...] = states
+    sum_ref[:, 0, :] = to_pieces(states[0] + states[1])
 
 
 def back_kernel(
-    q_ref, k_ref, v_ref, c_ref, gain_ref, raw_ref, low_ref, got_ref, parts_ref,
-    attended_ref, grad_q_ref, grad_kf_ref, grad_vf_ref,
-):
+    q_ref, k_ref, v_ref, c_ref, gain_ref, raw_ref, low_ref, got_ref, parts_ref, own_ref, other_ref,
+    attended_ref, grad_q_ref, grad_kf_ref, grad_vf_ref, here_ref, there_ref,
+):
+    core = core_index()
+    here_ref[...] = jnp.where(core == 0, other_ref[...], 0.0)
+    there_ref[:, 0, :] = to_pieces(jnp.where(core == 1, own_ref[...], 0.0))
     keep = causal4()
     inverse, pull = scales(own_and_other(parts_ref)[0])
     raws = in_order(raw_ref[0], got_ref[0:TOK])
@@ -227,25 +234,52 @@
         grad_vf_ref[:, half(g)] = mm(by_head(attention(q_feat, k_feat)), spread(d_raw), TN)
 
 
+def finished(own, refs, later):
+    k, v, grad_kf, grad_vf = (pick(own, ref[...]) for ref in refs)
+    later = spread(later.astype(BF16))
+    grad_k = (grad_kf + mm(v, later, NT)) * silu_slope(k)
+    return grad_k.astype(BF16), (grad_vf + mm(silu_low(k), later, NN)).astype(BF16)
+
+
+def own_kernel(
+    k_ref, v_ref, grad_kf_ref, grad_vf_ref, chip_ref, here_ref, grad_k_ref, grad_v_ref
+):
+    later = from_pieces(chip_ref[:, 0, :]) + here_ref[...]
+    refs = k_ref, v_ref, grad_kf_ref, grad_vf_ref
+    grad_k_ref[...], grad_v_ref[...] = finished(True, refs, later)
+
+
 def last_kernel(
-    k_ref, v_ref, grad_kf_ref, grad_vf_ref, chip_ref, here_ref, there_ref, grad_k_ref, grad_v_ref
-):
-    states = in_order(chip_ref[:, 0, :] + here_ref[:, 0, :], there_ref[:, 0, :])
-    for g, state in enumerate(states):
-        k = k_ref[:, half(g)]
-        later = spread(from_pieces(state).astype(BF16))
-        grad_kf = grad_kf_ref[:, half(g)] + mm(v_ref[:, half(g)], later, NT)
-        grad_k_ref[:, half(g)] = (grad_kf * silu_slope(k)).astype(BF16)
-        grad_vf = grad_vf_ref[:, half(g)] + mm(silu_low(k), later, NN)
-        grad_v_ref[:, half(g)] = grad_vf.astype(BF16)
-
-
-def call(kernel, outs, *args, flops=0):
+    k_ref, v_ref, grad_kf_ref, grad_vf_ref, there_ref, own_k_ref, own_v_ref,
+    grad_k_hbm, grad_v_hbm, other_k_ref, other_v_ref, sems,
+):
+    core = core_index()
+    own = pl.ds(pl.multiple_of(core * HALF, HALF), HALF)
+    other = pl.ds(pl.multiple_of((1 - core) * HALF, HALF), HALF)
+    copies = [
+        pltpu.make_async_copy(own_k_ref, grad_k_hbm.at[:, own], sems.at[0]),
+        pltpu.make_async_copy(own_v_ref, grad_v_hbm.at[:, own], sems.at[1]),
+        pltpu.make_async_copy(other_k_ref, grad_k_hbm.at[:, other], sems.at[2]),
+        pltpu.make_async_copy(other_v_ref, grad_v_hbm.at[:, other], sems.at[3]),
+    ]
+    copies[0].start()
+    copies[1].start()
+    refs = k_ref, v_ref, grad_kf_ref, grad_vf_ref
+    later = from_pieces(there_ref[:, 0, :])
+    other_k_ref[...], other_v_ref[...] = finished(False, refs, later)
+    copies[2].start()
+    copies[3].start()
+    for copy in copies:
+        copy.wait()
+
+
+def call(kernel, outs, *args, flops=0, out_space=VMEM, scratch=()):
     return pl.pallas_call(
         kernel,
         out_shape=[jax.ShapeDtypeStruct(shape, kind) for shape, kind in outs],
         in_specs=[VMEM] * len(args),
-        out_specs=[VMEM] * len(outs),
+        out_specs=[out_space] * len(outs),
+        scratch_shapes=list(scratch),
         compiler_params=pltpu.CompilerParams(vmem_limit_bytes=32 * 1024 * 1024),
         cost_estimate=pl.CostEstimate(flops=flops, bytes_accessed=1_000_000, transcendentals=0),
     )(*args)
@@ -270,6 +304,8 @@
 PIECES = ((CHIPS, 1, PIECE), F32)
 WIDE = ((TOK, CORES * HALF), F32)
 WIDE_LOW = ((TOK, CORES * HALF), BF16)
+STATE = ((HEAD_DIM, HALF), F32)
+HALF_LOW = ((TOK, HALF), BF16)
 BLOCKS = ((CORES, TOK, HALF), F32)
 
 
@@ -284,7 +320,7 @@
 def per_device(queries, key_input, value_input, norm_gain, cotangent):
     sharers = CORES * lax.axis_size("head")
     gain = norm_gain.reshape(1, -1)
-    mine, theirs = call(state_kernel, [PIECES, PIECES], key_input, value_input)
+    mine, theirs = call(state_kernel, [PIECES, PIECES], jnp.stack([key_input, value_input]))
     received = swap_cores(theirs)
     (given,) = call(
         send_kernel, [((4, TOK, HALF), F32)], queries, key_input, value_input, cotangent
@@ -300,22 +336,29 @@
         queries, cotangent, gain, got, intra, chip, mine, received,
     )
     parts = over_heads(parts)
-    total, here, there = call(
+    total, own, other = call(
         grad_state_kernel,
-        [PIECES, PIECES, PIECES],
+        [PIECES, STATE, STATE],
         queries, cotangent, gain, got, raw, parts,
     )
-    attended, grad_query, grad_kf, grad_vf = call(
+    attended, grad_query, grad_kf, grad_vf, here, there = call(
         back_kernel,
-        [WIDE_LOW, WIDE_LOW, WIDE, WIDE],
+        [WIDE_LOW, WIDE_LOW, WIDE, WIDE, STATE, PIECES],
         queries, key_input, value_input, cotangent, gain, raw, low, swap_cores(give), parts,
+        own, other,
         flops=500_000_000,
     )
     chip = scan(total, True)
+    there = swap_cores(chip + there)
+    parts = key_input, value_input, grad_kf, grad_vf
+    own = call(own_kernel, [HALF_LOW, HALF_LOW], *parts, chip, here, flops=50_000_000)
+    store = [pltpu.VMEM(*HALF_LOW)] * 2 + [pltpu.SemaphoreType.DMA((4,))]
     grad_key, grad_value = call(
         last_kernel,
         [WIDE_LOW, WIDE_LOW],
-        key_input, value_input, grad_kf, grad_vf, chip, here, swap_cores(chip + there),
+        *parts, there, *own,
+        out_space=pl.BlockSpec(memory_space=pltpu.HBM),
+        scratch=store,
     )
     return (attended, grad_query, grad_key, grad_value)
 

time: 141 us -> 140 us (level)
  local copies, waits for them, and re-layouts: 1.88 us -> 0.02 us
  Pallas kernels: 7.66 us -> 9.49 us
  waiting for transfers between devices: 38.6 us -> 36.9 us
    all_to_all x3, waiting for transfers between devices: 37.6 us -> 34 us  [across_chips(): return lax.all_to_all(x, 'ctx', 0, 0, axis_index_groups=groups)]
    ppermute x4, waiting for transfers between devices: 1.01 us -> 2.89 us  [swap_cores(): return lax.ppermute(x, 'ctx', pairs)]
    unnamed x18 -> x10, local copies, waits for them, and re-layouts: 1.88 us -> 0.02 us
    pallas_call x9 -> x10, Pallas kernels: 7.66 us -> 9.49 us  [call(): pl.pallas_call(kernel, out_shape=[jax.ShapeDtypeStruct(shape, kind) for s...]
  transfers between devices with their start and end apart: 7 -> 7, of which waited for: 4 -> 6; matrix products, arithmetic and copies ran while one was open for 0% -> 0% of each run, Pallas kernels for 3% -> 4%
where the time goes in v5:
time: 140 us
  starting transfers between devices  52.2 us (37%)
  blocking collectives  38.1 us (27%)
  waiting for transfers between devices  36.9 us (26%)
  Pallas kernels  9.49 us (7%)
  other arithmetic  2.07 us (1%)
    all_to_all x3, waiting for transfers between devices, across_chips(): return lax.all_to_all(x, 'ctx', 0, 0, axis_index_groups=groups)  34 us
    ppermute x4, starting transfers between devices, swap_cores(): return lax.ppermute(x, 'ctx', pairs)  28.1 us
    all_to_all x3, starting transfers between devices, across_chips(): return lax.all_to_all(x, 'ctx', 0, 0, axis_index_groups=groups)  24 us
    all_to_all x1, blocking collectives, across_chips(): return lax.all_to_all(x, 'ctx', 0, 0, axis_index_groups=groups)  20.7 us
    all_to_all x1, blocking collectives, over_heads(): return lax.all_to_all(x, ('ctx', 'head'), 0, 0, axis_index_groups=groups)  17.5 us
    pallas_call x10, Pallas kernels, call(): pl.pallas_call(kernel, out_shape=[jax.ShapeDtypeStruct(shape, kind) for s...  9.49 us
    ppermute x4, waiting for transfers between devices, swap_cores(): return lax.ppermute(x, 'ctx', pairs)  2.89 us
  transfers between devices with their start and end apart: 7, of which 6 were waited for; matrix products, arithmetic and copies ran while one was open for 0% of the time, Pallas kernels for 4%

profile of v5, /device:TPU:1, one launch (start us, length us, event | category | flops | bytes accessed | tf_op | source)
XLA Modules:
  0.0 139.5 jit_solution(13231730850820715716)
XLA Ops:
  0.6 1.1 pad_maximum_fusion.pair_ref
  1.7 0.5 shard_map.86
  2.2 16.1 %collective-permute-start.1 = (f32[64,1,640]{2,1,0:T(1,128)S(1)}, f32[64,1,640]{2,1,0:T(1,128)S(1)}, u32[]{:S(2)}, u32[]{:S(2)}) collective-permute-start(f32[64,1,640]{2,1,0:T(1,128)S(1)} %get-tuple-element.24), channel_id=1, source_target_pairs={{0,8},{8,0},{16,24},{24,16},{32,40},{40,32},{48,56},{56,48},{64,72... | collective-permute-start | bytes 491528 | tf_op jit(solution)/shard_map/ppermute | solution.py:290
  18.2 1.0 collective-permute-done.1.received_ref
  19.2 0.0 copy-start.1
  19.2 0.0 copy-start.2
  19.3 0.0 copy-start.3
  19.3 0.8 add.6
  20.1 0.0 copy-start
  20.1 9.4 %all-to-all-start = ((f32[64,1,640]{2,1,0:T(1,128)}), f32[64,1,640]{2,1,0:T(1,128)S(1)}, u32[]{:S(2)}, u32[]{:S(2)}) async-start(f32[64,1,640]{2,1,0:T(1,128)} %add.6), calls=%async_computation | async-start | bytes 327680 | tf_op jit(solution)/shard_map/all_to_all | solution.py:295
  29.5 0.0 copy-done.1
  29.5 0.0 copy-done.2
  29.6 0.0 copy-done.3
  29.6 0.0 copy-done
  29.6 0.1 shard_map.84
  29.7 2.6 %collective-permute-start = (f32[4,128,384]{2,1,0:T(8,128)S(1)}, f32[4,128,384]{2,1,0:T(8,128)S(1)}, u32[]{:S(2)}, u32[]{:S(2)}) collective-permute-start(f32[4,128,384]{2,1,0:T(8,128)S(1)} %shard_map.84), channel_id=1, source_target_pairs={{0,8},{8,0},{16,24},{24,16},{32,40},{40,32},{48,56},{56,48},{64,72... | collective-permute-start | bytes 2359304 | tf_op jit(solution)/shard_map/ppermute | solution.py:290
  32.2 13.1 %all-to-all-done.pieces_ref = f32[64,1,640]{2,1,0:T(1,128)S(1)} async-done(((f32[64,1,640]{2,1,0:T(1,128)}), f32[64,1,640]{2,1,0:T(1,128)S(1)}, u32[]{:S(2)}, u32[]{:S(2)}) %all-to-all-start) | async-done | bytes 163872 | tf_op jit(solution)/shard_map/all_to_all | solution.py:295
  45.3 1.6 %shard_map.87 = f32[64,1,640]{2,1,0:T(1,128)} custom-call(f32[64,1,640]{2,1,0:T(1,128)S(1)} %all-to-all-done.pieces_ref), custom_call_target="tpu_custom_call" | custom-call | bytes 1000000 | tf_op jit(solution)/shard_map/pallas_call | solution.py:277
  46.9 0.0 copy-start.4
  47.0 7.1 %all-to-all-start.1 = ((f32[64,1,640]{2,1,0:T(1,128)}), f32[64,1,640]{2,1,0:T(1,128)S(1)}, u32[]{:S(2)}, u32[]{:S(2)}) async-start(f32[64,1,640]{2,1,0:T(1,128)} %shard_map.87), calls=%async_computation.1 | async-start | bytes 327680 | tf_op jit(solution)/shard_map/all_to_all | solution.py:295
  54.1 0.0 copy-done.4
  54.1 0.0 collective-permute-done.got_ref
  54.1 0.8 shard_map.85.intra_ref
  54.9 13.9 %all-to-all-done.1.chip_ref = f32[64,1,640]{2,1,0:T(1,128)S(1)} async-done(((f32[64,1,640]{2,1,0:T(1,128)}), f32[64,1,640]{2,1,0:T(1,128)S(1)}, u32[]{:S(2)}, u32[]{:S(2)}) %all-to-all-start.1) | async-done | bytes 163872 | tf_op jit(solution)/shard_map/all_to_all | solution.py:295
  68.8 0.5 shard_map.88
  69.3 17.5 %all_to_all.25.parts_ref = f32[16,4,128]{2,1,0:T(4,128)S(1)} all-to-all(f32[16,4,128]{2,1,0:T(4,128)S(1)} %get-tuple-element.28), channel_id=1, replica_groups={{0,1,2,3,4,5,6,7,8,9,10,11,12,13,14,15},{16,17,18,19,20,21,22,23,24,25,..., dimensions={0} | all-to-all | bytes 65536 | tf_op jit(solution)/shard_map/all_to_all | solution.py:301
  86.8 0.5 shard_map.89
  87.3 20.7 %all_to_all.26.pieces_ref = f32[64,1,640]{2,1,0:T(1,128)S(1)} all-to-all(f32[64,1,640]{2,1,0:T(1,128)S(1)} %get-tuple-element.35), channel_id=1, replica_groups={{0,16,32,48,64,80,96,112,128,144,160,176,192,208,224,240,256,272,288,30..., dimensions={0} | all-to-all | bytes 327680 | tf_op jit(solution)/shard_map/all_to_all | solution.py:295
  108.0 1.6 %shard_map.91 = f32[64,1,640]{2,1,0:T(1,128)} custom-call(f32[64,1,640]{2,1,0:T(1,128)S(1)} %all_to_all.26.pieces_ref), custom_call_target="tpu_custom_call" | custom-call | bytes 1000000 | tf_op jit(solution)/shard_map/pallas_call | solution.py:277
  109.6 7.4 %all-to-all-start.4 = ((f32[64,1,640]{2,1,0:T(1,128)}), f32[64,1,640]{2,1,0:T(1,128)S(1)}, u32[]{:S(2)}, u32[]{:S(2)}) async-start(f32[64,1,640]{2,1,0:T(1,128)} %shard_map.91), calls=%async_computation.4 | async-start | bytes 327680 | tf_op jit(solution)/shard_map/all_to_all | solution.py:295
  117.0 3.6 %collective-permute-start.2 = (f32[224,384]{1,0:T(8,128)S(1)}, f32[224,384]{1,0:T(8,128)S(1)}, u32[]{:S(2)}, u32[]{:S(2)}) collective-permute-start(f32[224,384]{1,0:T(8,128)S(1)} %get-tuple-element.27), channel_id=1, source_target_pairs={{0,8},{8,0},{16,24},{24,16},{32,40},{40,32},{48,56},{56,48},{64,72... | collective-permute-start | bytes 1032200 | tf_op jit(solution)/shard_map/ppermute | solution.py:290
  120.7 1.3 collective-permute-done.2.got_ref
  122.0 2.4 %shard_map.90 = (bf16[128,768]{1,0:T(8,128)(2,1)}, bf16[128,768]{1,0:T(8,128)(2,1)}, f32[128,768]{1,0:T(8,128)S(1)}, f32[128,768]{1,0:T(8,128)S(1)}, f32[96,384]{1,0:T(8,128)S(1)}, /*index=5*/f32[64,1,640]{2,1,0:T(1,128)S(1)}) custom-call(bf16[128,768]{1,0:T(8,128)(2,1)S(1)} %copy-done.2, bf16[128,768]{1,0:T(8,128)(2,1)S(1)} %copy-done, ...), custom_call_target="tpu_custom_call" | custom-call | flops 500000000 | bytes 1000000 | tf_op jit(solution)/shard_map/pallas_call | solution.py:277
  124.4 7.0 %all-to-all-done.4.chip_ref = f32[64,1,640]{2,1,0:T(1,128)S(1)} async-done(((f32[64,1,640]{2,1,0:T(1,128)}), f32[64,1,640]{2,1,0:T(1,128)S(1)}, u32[]{:S(2)}, u32[]{:S(2)}) %all-to-all-start.4) | async-done | bytes 163872 | tf_op jit(solution)/shard_map/all_to_all | solution.py:295
  131.4 0.2 add.7
  131.6 5.9 %collective-permute-start.3 = (f32[64,1,640]{2,1,0:T(1,128)S(1)}, f32[64,1,640]{2,1,0:T(1,128)S(1)}, u32[]{:S(2)}, u32[]{:S(2)}) collective-permute-start(f32[64,1,640]{2,1,0:T(1,128)S(1)} %add.7), channel_id=1, source_target_pairs={{0,8},{8,0},{16,24},{24,16},{32,40},{40,32},{48,56},{56,48},{64,72... | collective-permute-start | bytes 491528 | tf_op jit(solution)/shard_map/ppermute | solution.py:290
  137.4 0.4 shard_map.92
  137.8 0.6 collective-permute-done.3.there_ref
  138.5 1.1 shard_map.93
  (1 shorter events, 0.0 us)
Async XLA Ops:
  2.2 17.1 %collective-permute-start.1 = (f32[64,1,640]{2,1,0:T(1,128)S(1)}, f32[64,1,640]{2,1,0:T(1,128)S(1)}, u32[]{:S(2)}, u32[]{:S(2)}) collective-permute-start(f32[64,1,640]{2,1,0:T(1,128)S(1)} %get-tuple-element.24), channel_id=1, source_target_pairs={{0,8},{8,0},{16,24},{24,16},{32,40},{40,32},{48,56},{56,48},{64,72... | collective-permute-start | bytes 491528 | tf_op jit(solution)/shard_map/ppermute | solution.py:290
  19.2 10.3 %copy-start.1 = (bf16[128,768]{1,0:T(8,128)(2,1)S(1)}, bf16[128,768]{1,0:T(8,128)(2,1)}, u32[]{:S(2)}) copy-start(bf16[128,768]{1,0:T(8,128)(2,1)} %v_ref.9) | copy-start | bytes 589828
  19.2 10.3 %copy-start.2 = (bf16[128,768]{1,0:T(8,128)(2,1)S(1)}, bf16[128,768]{1,0:T(8,128)(2,1)}, u32[]{:S(2)}) copy-start(bf16[128,768]{1,0:T(8,128)(2,1)} %q_ref.9) | copy-start | bytes 589828
  19.3 10.3 %copy-start.3 = (bf16[128,768]{1,0:T(8,128)(2,1)S(1)}, bf16[128,768]{1,0:T(8,128)(2,1)}, u32[]{:S(2)}) copy-start(bf16[128,768]{1,0:T(8,128)(2,1)} %c_ref.7) | copy-start | bytes 589828
  20.1 9.5 %copy-start = (bf16[128,768]{1,0:T(8,128)(2,1)S(1)}, bf16[128,768]{1,0:T(8,128)(2,1)}, u32[]{:S(2)}) copy-start(bf16[128,768]{1,0:T(8,128)(2,1)} %k_ref.9) | copy-start | bytes 589828
  20.1 25.2 %all-to-all-start = ((f32[64,1,640]{2,1,0:T(1,128)}), f32[64,1,640]{2,1,0:T(1,128)S(1)}, u32[]{:S(2)}, u32[]{:S(2)}) async-start(f32[64,1,640]{2,1,0:T(1,128)} %add.6), calls=%async_computation | async-start | bytes 327680 | tf_op jit(solution)/shard_map/all_to_all | solution.py:295
  29.7 24.5 %collective-permute-start = (f32[4,128,384]{2,1,0:T(8,128)S(1)}, f32[4,128,384]{2,1,0:T(8,128)S(1)}, u32[]{:S(2)}, u32[]{:S(2)}) collective-permute-start(f32[4,128,384]{2,1,0:T(8,128)S(1)} %shard_map.84), channel_id=1, source_target_pairs={{0,8},{8,0},{16,24},{24,16},{32,40},{40,32},{48,56},{56,48},{64,72... | collective-permute-start | bytes 2359304 | tf_op jit(solution)/shard_map/ppermute | solution.py:290
  46.9 7.2 %copy-start.4 = (f32[768]{0:T(1024)S(1)}, f32[768]{0:T(1024)}, u32[]{:S(2)}) copy-start(f32[768]{0:T(1024)} %param.8) | copy-start | bytes 9220
  47.0 21.9 %all-to-all-start.1 = ((f32[64,1,640]{2,1,0:T(1,128)}), f32[64,1,640]{2,1,0:T(1,128)S(1)}, u32[]{:S(2)}, u32[]{:S(2)}) async-start(f32[64,1,640]{2,1,0:T(1,128)} %shard_map.87), calls=%async_computation.1 | async-start | bytes 327680 | tf_op jit(solution)/shard_map/all_to_all | solution.py:295
  109.6 21.8 %all-to-all-start.4 = ((f32[64,1,640]{2,1,0:T(1,128)}), f32[64,1,640]{2,1,0:T(1,128)S(1)}, u32[]{:S(2)}, u32[]{:S(2)}) async-start(f32[64,1,640]{2,1,0:T(1,128)} %shard_map.91), calls=%async_computation.4 | async-start | bytes 327680 | tf_op jit(solution)/shard_map/all_to_all | solution.py:295
  117.0 4.9 %collective-permute-start.2 = (f32[224,384]{1,0:T(8,128)S(1)}, f32[224,384]{1,0:T(8,128)S(1)}, u32[]{:S(2)}, u32[]{:S(2)}) collective-permute-start(f32[224,384]{1,0:T(8,128)S(1)} %get-tuple-element.27), channel_id=1, source_target_pairs={{0,8},{8,0},{16,24},{24,16},{32,40},{40,32},{48,56},{56,48},{64,72... | collective-permute-start | bytes 1032200 | tf_op jit(solution)/shard_map/ppermute | solution.py:290
  131.6 6.9 %collective-permute-start.3 = (f32[64,1,640]{2,1,0:T(1,128)S(1)}, f32[64,1,640]{2,1,0:T(1,128)S(1)}, u32[]{:S(2)}, u32[]{:S(2)}) collective-permute-start(f32[64,1,640]{2,1,0:T(1,128)S(1)} %add.7), channel_id=1, source_target_pairs={{0,8},{8,0},{16,24},{24,16},{32,40},{40,32},{48,56},{56,48},{64,72... | collective-permute-start | bytes 491528 | tf_op jit(solution)/shard_map/ppermute | solution.py:290

commit v6 on v5

--- a/solution.py
+++ b/solution.py
@@ -133,18 +133,11 @@
 
 
 def scan_kernel(backward, pieces_ref, out_ref):
-    row = lax.broadcasted_iota(jnp.int32, (CHIPS, CHIPS), 0)
-    col = lax.broadcasted_iota(jnp.int32, (CHIPS, CHIPS), 1)
-    before = jnp.where(row < col if backward else row > col, 1.0, 0.0).astype(BF16)
-    rest = pieces_ref[:, 0, :]
-    terms = []
-    for _ in range(3):
-        term = rest.astype(BF16)
-        rest = rest - term.astype(F32)
-        terms.append(term)
-    out_ref[:, 0, :] = mm(
-        jnp.concatenate([before] * 3, axis=1), jnp.concatenate(terms, axis=0), NN
-    )
+    total = jnp.zeros((1, PIECE), F32)
+    for i in range(CHIPS):
+        chip = CHIPS - 1 - i if backward else i
+        out_ref[chip] = total
+        total = total + pieces_ref[chip]
 
 
 def lane_sums(x):

time: 140 us -> 138 us (0.986)
  Pallas kernels: 9.49 us -> 7.66 us
    pallas_call x10, Pallas kernels: 9.49 us -> 7.66 us  [call(): pl.pallas_call(kernel, out_shape=[jax.ShapeDtypeStruct(shape, kind) for s...]
  transfers between devices with their start and end apart: 7 -> 7, of which waited for: 6 -> 6; matrix products, arithmetic and copies ran while one was open for 0% -> 0% of each run, Pallas kernels for 4% -> 3%
where the time goes in v6:
time: 138 us
  starting transfers between devices  52.2 us (38%)
  blocking collectives  38.1 us (28%)
  waiting for transfers between devices  36.9 us (27%)
  Pallas kernels  7.66 us (6%)
  other arithmetic  2.07 us (1%)
    all_to_all x3, waiting for transfers between devices, across_chips(): return lax.all_to_all(x, 'ctx', 0, 0, axis_index_groups=groups)  34 us
    ppermute x4, starting transfers between devices, swap_cores(): return lax.ppermute(x, 'ctx', pairs)  28.1 us
    all_to_all x3, starting transfers between devices, across_chips(): return lax.all_to_all(x, 'ctx', 0, 0, axis_index_groups=groups)  24 us
    all_to_all x1, blocking collectives, across_chips(): return lax.all_to_all(x, 'ctx', 0, 0, axis_index_groups=groups)  20.7 us
    all_to_all x1, blocking collectives, over_heads(): return lax.all_to_all(x, ('ctx', 'head'), 0, 0, axis_index_groups=groups)  17.5 us
    pallas_call x10, Pallas kernels, call(): pl.pallas_call(kernel, out_shape=[jax.ShapeDtypeStruct(shape, kind) for s...  7.66 us
    ppermute x4, waiting for transfers between devices, swap_cores(): return lax.ppermute(x, 'ctx', pairs)  2.9 us
  transfers between devices with their start and end apart: 7, of which 6 were waited for; matrix products, arithmetic and copies ran while one was open for 0% of the time, Pallas kernels for 3%

profile of v6, /device:TPU:1, one launch (start us, length us, event | category | flops | bytes accessed | tf_op | source)
XLA Modules:
  0.0 137.7 jit_solution(7656842182438750358)
XLA Ops:
  0.6 1.1 pad_maximum_fusion.pair_ref
  1.7 0.5 shard_map.86
  2.2 16.1 %collective-permute-start.1 = (f32[64,1,640]{2,1,0:T(1,128)S(1)}, f32[64,1,640]{2,1,0:T(1,128)S(1)}, u32[]{:S(2)}, u32[]{:S(2)}) collective-permute-start(f32[64,1,640]{2,1,0:T(1,128)S(1)} %get-tuple-element.24), channel_id=1, source_target_pairs={{0,8},{8,0},{16,24},{24,16},{32,40},{40,32},{48,56},{56,48},{64,72... | collective-permute-start | bytes 491528 | tf_op jit(solution)/shard_map/ppermute | solution.py:283
  18.2 1.0 collective-permute-done.1.received_ref
  19.2 0.0 copy-start.1
  19.2 0.0 copy-start.2
  19.3 0.0 copy-start.3
  19.3 0.8 add.6
  20.1 0.0 copy-start
  20.1 9.4 %all-to-all-start = ((f32[64,1,640]{2,1,0:T(1,128)}), f32[64,1,640]{2,1,0:T(1,128)S(1)}, u32[]{:S(2)}, u32[]{:S(2)}) async-start(f32[64,1,640]{2,1,0:T(1,128)} %add.6), calls=%async_computation | async-start | bytes 327680 | tf_op jit(solution)/shard_map/all_to_all | solution.py:288
  29.5 0.0 copy-done.1
  29.5 0.0 copy-done.2
  29.6 0.0 copy-done.3
  29.6 0.0 copy-done
  29.6 0.1 shard_map.84
  29.7 2.6 %collective-permute-start = (f32[4,128,384]{2,1,0:T(8,128)S(1)}, f32[4,128,384]{2,1,0:T(8,128)S(1)}, u32[]{:S(2)}, u32[]{:S(2)}) collective-permute-start(f32[4,128,384]{2,1,0:T(8,128)S(1)} %shard_map.84), channel_id=1, source_target_pairs={{0,8},{8,0},{16,24},{24,16},{32,40},{40,32},{48,56},{56,48},{64,72... | collective-permute-start | bytes 2359304 | tf_op jit(solution)/shard_map/ppermute | solution.py:283
  32.2 13.1 %all-to-all-done.pieces_ref = f32[64,1,640]{2,1,0:T(1,128)S(1)} async-done(((f32[64,1,640]{2,1,0:T(1,128)}), f32[64,1,640]{2,1,0:T(1,128)S(1)}, u32[]{:S(2)}, u32[]{:S(2)}) %all-to-all-start) | async-done | bytes 163872 | tf_op jit(solution)/shard_map/all_to_all | solution.py:288
  45.3 0.7 shard_map.87
  46.0 0.0 copy-start.4
  46.0 7.1 %all-to-all-start.1 = ((f32[64,1,640]{2,1,0:T(1,128)}), f32[64,1,640]{2,1,0:T(1,128)S(1)}, u32[]{:S(2)}, u32[]{:S(2)}) async-start(f32[64,1,640]{2,1,0:T(1,128)} %shard_map.87), calls=%async_computation.1 | async-start | bytes 327680 | tf_op jit(solution)/shard_map/all_to_all | solution.py:288
  53.2 0.0 copy-done.4
  53.2 0.0 collective-permute-done.got_ref
  53.2 0.8 shard_map.85.intra_ref
  54.0 13.9 %all-to-all-done.1.chip_ref = f32[64,1,640]{2,1,0:T(1,128)S(1)} async-done(((f32[64,1,640]{2,1,0:T(1,128)}), f32[64,1,640]{2,1,0:T(1,128)S(1)}, u32[]{:S(2)}, u32[]{:S(2)}) %all-to-all-start.1) | async-done | bytes 163872 | tf_op jit(solution)/shard_map/all_to_all | solution.py:288
  67.9 0.5 shard_map.88
  68.4 17.5 %all_to_all.25.parts_ref = f32[16,4,128]{2,1,0:T(4,128)S(1)} all-to-all(f32[16,4,128]{2,1,0:T(4,128)S(1)} %get-tuple-element.28), channel_id=1, replica_groups={{0,1,2,3,4,5,6,7,8,9,10,11,12,13,14,15},{16,17,18,19,20,21,22,23,24,25,..., dimensions={0} | all-to-all | bytes 65536 | tf_op jit(solution)/shard_map/all_to_all | solution.py:294
  85.9 0.5 shard_map.89
  86.4 20.7 %all_to_all.26.pieces_ref = f32[64,1,640]{2,1,0:T(1,128)S(1)} all-to-all(f32[64,1,640]{2,1,0:T(1,128)S(1)} %get-tuple-element.35), channel_id=1, replica_groups={{0,16,32,48,64,80,96,112,128,144,160,176,192,208,224,240,256,272,288,30..., dimensions={0} | all-to-all | bytes 327680 | tf_op jit(solution)/shard_map/all_to_all | solution.py:288
  107.0 0.7 shard_map.91
  107.8 7.4 %all-to-all-start.4 = ((f32[64,1,640]{2,1,0:T(1,128)}), f32[64,1,640]{2,1,0:T(1,128)S(1)}, u32[]{:S(2)}, u32[]{:S(2)}) async-start(f32[64,1,640]{2,1,0:T(1,128)} %shard_map.91), calls=%async_computation.4 | async-start | bytes 327680 | tf_op jit(solution)/shard_map/all_to_all | solution.py:288
  115.2 3.6 %collective-permute-start.2 = (f32[224,384]{1,0:T(8,128)S(1)}, f32[224,384]{1,0:T(8,128)S(1)}, u32[]{:S(2)}, u32[]{:S(2)}) collective-permute-start(f32[224,384]{1,0:T(8,128)S(1)} %get-tuple-element.27), channel_id=1, source_target_pairs={{0,8},{8,0},{16,24},{24,16},{32,40},{40,32},{48,56},{56,48},{64,72... | collective-permute-start | bytes 1032200 | tf_op jit(solution)/shard_map/ppermute | solution.py:283
  118.9 1.3 collective-permute-done.2.got_ref
  120.1 2.4 %shard_map.90 = (bf16[128,768]{1,0:T(8,128)(2,1)}, bf16[128,768]{1,0:T(8,128)(2,1)}, f32[128,768]{1,0:T(8,128)S(1)}, f32[128,768]{1,0:T(8,128)S(1)}, f32[96,384]{1,0:T(8,128)S(1)}, /*index=5*/f32[64,1,640]{2,1,0:T(1,128)S(1)}) custom-call(bf16[128,768]{1,0:T(8,128)(2,1)S(1)} %copy-done.2, bf16[128,768]{1,0:T(8,128)(2,1)S(1)} %copy-done, ...), custom_call_target="tpu_custom_call" | custom-call | flops 500000000 | bytes 1000000 | tf_op jit(solution)/shard_map/pallas_call | solution.py:270
  122.5 7.0 %all-to-all-done.4.chip_ref = f32[64,1,640]{2,1,0:T(1,128)S(1)} async-done(((f32[64,1,640]{2,1,0:T(1,128)}), f32[64,1,640]{2,1,0:T(1,128)S(1)}, u32[]{:S(2)}, u32[]{:S(2)}) %all-to-all-start.4) | async-done | bytes 163872 | tf_op jit(solution)/shard_map/all_to_all | solution.py:288
  129.6 0.2 add.7
  129.7 5.9 %collective-permute-start.3 = (f32[64,1,640]{2,1,0:T(1,128)S(1)}, f32[64,1,640]{2,1,0:T(1,128)S(1)}, u32[]{:S(2)}, u32[]{:S(2)}) collective-permute-start(f32[64,1,640]{2,1,0:T(1,128)S(1)} %add.7), channel_id=1, source_target_pairs={{0,8},{8,0},{16,24},{24,16},{32,40},{40,32},{48,56},{56,48},{64,72... | collective-permute-start | bytes 491528 | tf_op jit(solution)/shard_map/ppermute | solution.py:283
  135.6 0.4 shard_map.92
  136.0 0.6 collective-permute-done.3.there_ref
  136.6 1.1 shard_map.93
  (1 shorter events, 0.0 us)
Async XLA Ops:
  2.2 17.1 %collective-permute-start.1 = (f32[64,1,640]{2,1,0:T(1,128)S(1)}, f32[64,1,640]{2,1,0:T(1,128)S(1)}, u32[]{:S(2)}, u32[]{:S(2)}) collective-permute-start(f32[64,1,640]{2,1,0:T(1,128)S(1)} %get-tuple-element.24), channel_id=1, source_target_pairs={{0,8},{8,0},{16,24},{24,16},{32,40},{40,32},{48,56},{56,48},{64,72... | collective-permute-start | bytes 491528 | tf_op jit(solution)/shard_map/ppermute | solution.py:283
  19.2 10.3 %copy-start.1 = (bf16[128,768]{1,0:T(8,128)(2,1)S(1)}, bf16[128,768]{1,0:T(8,128)(2,1)}, u32[]{:S(2)}) copy-start(bf16[128,768]{1,0:T(8,128)(2,1)} %v_ref.9) | copy-start | bytes 589828
  19.2 10.3 %copy-start.2 = (bf16[128,768]{1,0:T(8,128)(2,1)S(1)}, bf16[128,768]{1,0:T(8,128)(2,1)}, u32[]{:S(2)}) copy-start(bf16[128,768]{1,0:T(8,128)(2,1)} %q_ref.9) | copy-start | bytes 589828
  19.3 10.3 %copy-start.3 = (bf16[128,768]{1,0:T(8,128)(2,1)S(1)}, bf16[128,768]{1,0:T(8,128)(2,1)}, u32[]{:S(2)}) copy-start(bf16[128,768]{1,0:T(8,128)(2,1)} %c_ref.7) | copy-start | bytes 589828
  20.1 9.5 %copy-start = (bf16[128,768]{1,0:T(8,128)(2,1)S(1)}, bf16[128,768]{1,0:T(8,128)(2,1)}, u32[]{:S(2)}) copy-start(bf16[128,768]{1,0:T(8,128)(2,1)} %k_ref.9) | copy-start | bytes 589828
  20.1 25.2 %all-to-all-start = ((f32[64,1,640]{2,1,0:T(1,128)}), f32[64,1,640]{2,1,0:T(1,128)S(1)}, u32[]{:S(2)}, u32[]{:S(2)}) async-start(f32[64,1,640]{2,1,0:T(1,128)} %add.6), calls=%async_computation | async-start | bytes 327680 | tf_op jit(solution)/shard_map/all_to_all | solution.py:288
  29.7 23.6 %collective-permute-start = (f32[4,128,384]{2,1,0:T(8,128)S(1)}, f32[4,128,384]{2,1,0:T(8,128)S(1)}, u32[]{:S(2)}, u32[]{:S(2)}) collective-permute-start(f32[4,128,384]{2,1,0:T(8,128)S(1)} %shard_map.84), channel_id=1, source_target_pairs={{0,8},{8,0},{16,24},{24,16},{32,40},{40,32},{48,56},{56,48},{64,72... | collective-permute-start | bytes 2359304 | tf_op jit(solution)/shard_map/ppermute | solution.py:283
  46.0 7.2 %copy-start.4 = (f32[768]{0:T(1024)S(1)}, f32[768]{0:T(1024)}, u32[]{:S(2)}) copy-start(f32[768]{0:T(1024)} %param.8) | copy-start | bytes 9220
  46.0 21.9 %all-to-all-start.1 = ((f32[64,1,640]{2,1,0:T(1,128)}), f32[64,1,640]{2,1,0:T(1,128)S(1)}, u32[]{:S(2)}, u32[]{:S(2)}) async-start(f32[64,1,640]{2,1,0:T(1,128)} %shard_map.87), calls=%async_computation.1 | async-start | bytes 327680 | tf_op jit(solution)/shard_map/all_to_all | solution.py:288
  107.8 21.8 %all-to-all-start.4 = ((f32[64,1,640]{2,1,0:T(1,128)}), f32[64,1,640]{2,1,0:T(1,128)S(1)}, u32[]{:S(2)}, u32[]{:S(2)}) async-start(f32[64,1,640]{2,1,0:T(1,128)} %shard_map.91), calls=%async_computation.4 | async-start | bytes 327680 | tf_op jit(solution)/shard_map/all_to_all | solution.py:288
  115.2 4.9 %collective-permute-start.2 = (f32[224,384]{1,0:T(8,128)S(1)}, f32[224,384]{1,0:T(8,128)S(1)}, u32[]{:S(2)}, u32[]{:S(2)}) collective-permute-start(f32[224,384]{1,0:T(8,128)S(1)} %get-tuple-element.27), channel_id=1, source_target_pairs={{0,8},{8,0},{16,24},{24,16},{32,40},{40,32},{48,56},{56,48},{64,72... | collective-permute-start | bytes 1032200 | tf_op jit(solution)/shard_map/ppermute | solution.py:283
  129.7 6.9 %collective-permute-start.3 = (f32[64,1,640]{2,1,0:T(1,128)S(1)}, f32[64,1,640]{2,1,0:T(1,128)S(1)}, u32[]{:S(2)}, u32[]{:S(2)}) collective-permute-start(f32[64,1,640]{2,1,0:T(1,128)S(1)} %add.7), channel_id=1, source_target_pairs={{0,8},{8,0},{16,24},{24,16},{32,40},{40,32},{48,56},{56,48},{64,72... | collective-permute-start | bytes 491528 | tf_op jit(solution)/shard_map/ppermute | solution.py:283

commit v7 on v6

--- a/solution.py
+++ b/solution.py
@@ -125,14 +125,16 @@
     return jnp.where(causal4(), mm(q_feat, spread(k_feat), NT), 0.0).astype(BF16)
 
 
-def intra_kernel(q_ref, k_ref, v_ref, got_ref, intra_ref):
+def intra_kernel(q_ref, k_ref, v_ref, got_ref, intra_ref, done_ref):
+    done_ref[...] = jnp.zeros_like(done_ref)
     mine = [pick(True, ref[...]) for ref in (q_ref, k_ref, v_ref)]
     others = [got_ref[i].astype(BF16) for i in range(3)]
     for i, (q, k, v) in enumerate((mine, others)):
         intra_ref[i] = mm(attention(silu_low(q), silu_low(k)), spread(v), NN)
 
 
-def scan_kernel(backward, pieces_ref, out_ref):
+def scan_kernel(backward, pieces_ref, *refs):
+    out_ref = refs[-1]
     total = jnp.zeros((1, PIECE), F32)
     for i in range(CHIPS):
         chip = CHIPS - 1 - i if backward else i
@@ -206,7 +208,7 @@
 
 def back_kernel(
     q_ref, k_ref, v_ref, c_ref, gain_ref, raw_ref, low_ref, got_ref, parts_ref, own_ref, other_ref,
-    attended_ref, grad_q_ref, grad_kf_ref, grad_vf_ref, here_ref, there_ref,
+    attended_ref, grad_q_ref, grad_kf_ref, grad_vf_ref, k_feat_ref, slope_ref, here_ref, there_ref,
 ):
     core = core_index()
     here_ref[...] = jnp.where(core == 0, other_ref[...], 0.0)
@@ -218,6 +220,8 @@
     for g in range(CORES):
         q, raw, gain = q_ref[:, half(g)], raws[g], gain_ref[:, half(g)]
         q_feat, k_feat = silu_low(q), silu_low(k_ref[:, half(g)])
+        k_feat_ref[:, half(g)] = k_feat
+        slope_ref[:, half(g)] = silu_slope(k_ref[:, half(g)])
         attended_ref[:, half(g)] = (raw * inverse * gain).astype(BF16)
         d_raw = gradient(c_ref[:, half(g)], gain, raw, inverse, pull)
         back = jnp.where(keep, mm(d_raw, spread(v_ref[:, half(g)]), NT), 0.0).astype(BF16)
@@ -227,23 +231,26 @@
         grad_vf_ref[:, half(g)] = mm(by_head(attention(q_feat, k_feat)), spread(d_raw), TN)
 
 
-def finished(own, refs, later):
-    k, v, grad_kf, grad_vf = (pick(own, ref[...]) for ref in refs)
-    later = spread(later.astype(BF16))
-    grad_k = (grad_kf + mm(v, later, NT)) * silu_slope(k)
-    return grad_k.astype(BF16), (grad_vf + mm(silu_low(k), later, NN)).astype(BF16)
+def key_gradient(own, v_ref, slope_ref, grad_kf_ref, later):
+    v, slope, grad_kf = (pick(own, ref[...]) for ref in (v_ref, slope_ref, grad_kf_ref))
+    return ((grad_kf + mm(v, later, NT)) * slope).astype(BF16)
+
+
+def value_gradient(own, k_feat_ref, grad_vf_ref, later):
+    k_feat, grad_vf = pick(own, k_feat_ref[...]), pick(own, grad_vf_ref[...])
+    return (grad_vf + mm(k_feat, later, NN)).astype(BF16)
 
 
 def own_kernel(
-    k_ref, v_ref, grad_kf_ref, grad_vf_ref, chip_ref, here_ref, grad_k_ref, grad_v_ref
-):
-    later = from_pieces(chip_ref[:, 0, :]) + here_ref[...]
-    refs = k_ref, v_ref, grad_kf_ref, grad_vf_ref
-    grad_k_ref[...], grad_v_ref[...] = finished(True, refs, later)
+    v_ref, k_feat_ref, slope_ref, grad_kf_ref, grad_vf_ref, chip_ref, here_ref, grad_k_ref, grad_v_ref
+):
+    later = spread((from_pieces(chip_ref[:, 0, :]) + here_ref[...]).astype(BF16))
+    grad_k_ref[...] = key_gradient(True, v_ref, slope_ref, grad_kf_ref, later)
+    grad_v_ref[...] = value_gradient(True, k_feat_ref, grad_vf_ref, later)
 
 
 def last_kernel(
-    k_ref, v_ref, grad_kf_ref, grad_vf_ref, there_ref, own_k_ref, own_v_ref,
+    v_ref, k_feat_ref, slope_ref, grad_kf_ref, grad_vf_ref, there_ref, own_k_ref, own_v_ref,
     grad_k_hbm, grad_v_hbm, other_k_ref, other_v_ref, sems,
 ):
     core = core_index()
@@ -257,10 +264,10 @@
     ]
     copies[0].start()
     copies[1].start()
-    refs = k_ref, v_ref, grad_kf_ref, grad_vf_ref
-    later = from_pieces(there_ref[:, 0, :])
-    other_k_ref[...], other_v_ref[...] = finished(False, refs, later)
+    later = spread(from_pieces(there_ref[:, 0, :]).astype(BF16))
+    other_k_ref[...] = key_gradient(False, v_ref, slope_ref, grad_kf_ref, later)
     copies[2].start()
+    other_v_ref[...] = value_gradient(False, k_feat_ref, grad_vf_ref, later)
     copies[3].start()
     for copy in copies:
         copy.wait()
@@ -297,16 +304,17 @@
 PIECES = ((CHIPS, 1, PIECE), F32)
 WIDE = ((TOK, CORES * HALF), F32)
 WIDE_LOW = ((TOK, CORES * HALF), BF16)
+DONE = ((8, LANES), F32)
 STATE = ((HEAD_DIM, HALF), F32)
 HALF_LOW = ((TOK, HALF), BF16)
 BLOCKS = ((CORES, TOK, HALF), F32)
 
 
-def scan(pieces, backward):
-    def kernel(pieces_ref, out_ref):
-        scan_kernel(backward, pieces_ref, out_ref)
-
-    (summed,) = call(kernel, [PIECES], across_chips(pieces))
+def scan(pieces, backward, *after):
+    def kernel(*refs):
+        scan_kernel(backward, *refs)
+
+    (summed,) = call(kernel, [PIECES], across_chips(pieces), *after)
     return across_chips(summed)
 
 
@@ -319,10 +327,10 @@
         send_kernel, [((4, TOK, HALF), F32)], queries, key_input, value_input, cotangent
     )
     got = swap_cores(given)
-    (intra,) = call(
-        intra_kernel, [BLOCKS], queries, key_input, value_input, got, flops=200_000_000
-    )
-    chip = scan(mine + received, False)
+    intra, done = call(
+        intra_kernel, [BLOCKS, DONE], queries, key_input, value_input, got, flops=200_000_000
+    )
+    chip = scan(mine + received, False, done)
     raw, low, give, parts = call(
         raw_kernel,
         [BLOCKS, ((HEAD_DIM, HALF), BF16), ((TOK + HEAD_DIM, HALF), F32), ((sharers, 4, TOK), F32)],
@@ -334,16 +342,16 @@
         [PIECES, STATE, STATE],
         queries, cotangent, gain, got, raw, parts,
     )
-    attended, grad_query, grad_kf, grad_vf, here, there = call(
+    attended, grad_query, grad_kf, grad_vf, k_feat, slope, here, there = call(
         back_kernel,
-        [WIDE_LOW, WIDE_LOW, WIDE, WIDE, STATE, PIECES],
+        [WIDE_LOW, WIDE_LOW, WIDE, WIDE, WIDE_LOW, WIDE, STATE, PIECES],
         queries, key_input, value_input, cotangent, gain, raw, low, swap_cores(give), parts,
         own, other,
         flops=500_000_000,
     )
     chip = scan(total, True)
     there = swap_cores(chip + there)
-    parts = key_input, value_input, grad_kf, grad_vf
+    parts = value_input, k_feat, slope, grad_kf, grad_vf
     own = call(own_kernel, [HALF_LOW, HALF_LOW], *parts, chip, here, flops=50_000_000)
     store = [pltpu.VMEM(*HALF_LOW)] * 2 + [pltpu.SemaphoreType.DMA((4,))]
     grad_key, grad_value = call(

time: 138 us -> 139 us (level)
    all_to_all x3, waiting for transfers between devices: 34 us -> 35.7 us  [across_chips(): return lax.all_to_all(x, 'ctx', 0, 0, axis_index_groups=groups)]
  transfers between devices with their start and end apart: 7 -> 7, of which waited for: 6 -> 5; matrix products, arithmetic and copies ran while one was open for 0% -> 1% of each run, Pallas kernels for 3% -> 3%
where the time goes in v7:
time: 139 us
  starting transfers between devices  51.9 us (37%)
  blocking collectives  38.4 us (28%)
  waiting for transfers between devices  37.6 us (27%)
  Pallas kernels  7.7 us (6%)
  other arithmetic  2.12 us (2%)
    all_to_all x3, waiting for transfers between devices, across_chips(): return lax.all_to_all(x, 'ctx', 0, 0, axis_index_groups=groups)  35.7 us
    ppermute x4, starting transfers between devices, swap_cores(): return lax.ppermute(x, 'ctx', pairs)  27.5 us
    all_to_all x3, starting transfers between devices, across_chips(): return lax.all_to_all(x, 'ctx', 0, 0, axis_index_groups=groups)  24.3 us
    all_to_all x1, blocking collectives, across_chips(): return lax.all_to_all(x, 'ctx', 0, 0, axis_index_groups=groups)  20.5 us
    all_to_all x1, blocking collectives, over_heads(): return lax.all_to_all(x, ('ctx', 'head'), 0, 0, axis_index_groups=groups)  17.9 us
    pallas_call x10, Pallas kernels, call(): pl.pallas_call(kernel, out_shape=[jax.ShapeDtypeStruct(shape, kind) for s...  7.7 us
  transfers between devices with their start and end apart: 7, of which 5 were waited for; matrix products, arithmetic and copies ran while one was open for 1% of the time, Pallas kernels for 3%

profile of v7, /device:TPU:1, one launch (start us, length us, event | category | flops | bytes accessed | tf_op | source)
XLA Modules:
  0.0 138.6 jit_solution(14546026445145445520)
XLA Ops:
  0.6 0.0 copy-start.2
  0.6 0.0 copy-start.3
  0.7 1.1 pad_maximum_fusion.pair_ref
  1.8 0.0 copy-start
  1.8 0.0 copy-start.1
  1.8 0.5 shard_map.86
  2.3 16.1 %collective-permute-start.1 = (f32[64,1,640]{2,1,0:T(1,128)S(1)}, f32[64,1,640]{2,1,0:T(1,128)S(1)}, u32[]{:S(2)}, u32[]{:S(2)}) collective-permute-start(f32[64,1,640]{2,1,0:T(1,128)S(1)} %get-tuple-element.29), channel_id=1, source_target_pairs={{0,8},{8,0},{16,24},{24,16},{32,40},{40,32},{48,56},{56,48},{64,72... | collective-permute-start | bytes 491528 | tf_op jit(solution)/shard_map/ppermute | solution.py:290
  18.3 0.0 copy-done.2
  18.3 0.0 copy-done.3
  18.4 0.0 copy-done
  18.4 0.0 copy-done.1
  18.4 0.1 shard_map.84
  18.5 1.9 %collective-permute-start = (f32[4,128,384]{2,1,0:T(8,128)S(1)}, f32[4,128,384]{2,1,0:T(8,128)S(1)}, u32[]{:S(2)}, u32[]{:S(2)}) collective-permute-start(f32[4,128,384]{2,1,0:T(8,128)S(1)} %shard_map.84), channel_id=1, source_target_pairs={{0,8},{8,0},{16,24},{24,16},{32,40},{40,32},{48,56},{56,48},{64,72... | collective-permute-start | bytes 2359304 | tf_op jit(solution)/shard_map/ppermute | solution.py:290
  20.4 0.0 collective-permute-done.1.received_ref
  20.4 0.8 add.6
  21.2 9.3 %all-to-all-start = ((f32[64,1,640]{2,1,0:T(1,128)}), f32[64,1,640]{2,1,0:T(1,128)S(1)}, u32[]{:S(2)}, u32[]{:S(2)}) async-start(f32[64,1,640]{2,1,0:T(1,128)} %add.6), calls=%async_computation | async-start | bytes 327680 | tf_op jit(solution)/shard_map/all_to_all | solution.py:295
  30.5 0.0 collective-permute-done.got_ref
  30.6 0.8 shard_map.85
  31.3 14.4 %all-to-all-done.refs_0_ = f32[64,1,640]{2,1,0:T(1,128)S(1)} async-done(((f32[64,1,640]{2,1,0:T(1,128)}), f32[64,1,640]{2,1,0:T(1,128)S(1)}, u32[]{:S(2)}, u32[]{:S(2)}) %all-to-all-start) | async-done | bytes 163872 | tf_op jit(solution)/shard_map/all_to_all | solution.py:295
  45.7 0.7 shard_map.87
  46.5 0.0 copy-start.6
  46.5 7.6 %all-to-all-start.1 = ((f32[64,1,640]{2,1,0:T(1,128)}), f32[64,1,640]{2,1,0:T(1,128)S(1)}, u32[]{:S(2)}, u32[]{:S(2)}) async-start(f32[64,1,640]{2,1,0:T(1,128)} %shard_map.87), calls=%async_computation.1 | async-start | bytes 327680 | tf_op jit(solution)/shard_map/all_to_all | solution.py:295
  54.1 0.0 copy-done.6
  54.1 14.4 %all-to-all-done.1.chip_ref = f32[64,1,640]{2,1,0:T(1,128)S(1)} async-done(((f32[64,1,640]{2,1,0:T(1,128)}), f32[64,1,640]{2,1,0:T(1,128)S(1)}, u32[]{:S(2)}, u32[]{:S(2)}) %all-to-all-start.1) | async-done | bytes 163872 | tf_op jit(solution)/shard_map/all_to_all | solution.py:295
  68.5 0.5 shard_map.88
  69.0 0.0 copy-start.4
  69.0 17.9 %all_to_all.25.parts_ref = f32[16,4,128]{2,1,0:T(4,128)S(1)} all-to-all(f32[16,4,128]{2,1,0:T(4,128)S(1)} %get-tuple-element.34), channel_id=1, replica_groups={{0,1,2,3,4,5,6,7,8,9,10,11,12,13,14,15},{16,17,18,19,20,21,22,23,24,25,..., dimensions={0} | all-to-all | bytes 65536 | tf_op jit(solution)/shard_map/all_to_all | solution.py:301
  86.9 0.5 shard_map.89
  87.4 0.0 copy-done.4
  87.4 20.5 %all_to_all.26.refs_0_ = f32[64,1,640]{2,1,0:T(1,128)S(1)} all-to-all(f32[64,1,640]{2,1,0:T(1,128)S(1)} %get-tuple-element.43), channel_id=1, replica_groups={{0,16,32,48,64,80,96,112,128,144,160,176,192,208,224,240,256,272,288,30..., dimensions={0} | all-to-all | bytes 327680 | tf_op jit(solution)/shard_map/all_to_all | solution.py:295
  107.9 0.0 copy-start.5
  107.9 0.7 shard_map.91
  108.7 7.4 %all-to-all-start.4 = ((f32[64,1,640]{2,1,0:T(1,128)}), f32[64,1,640]{2,1,0:T(1,128)S(1)}, u32[]{:S(2)}, u32[]{:S(2)}) async-start(f32[64,1,640]{2,1,0:T(1,128)} %shard_map.91), calls=%async_computation.4 | async-start | bytes 327680 | tf_op jit(solution)/shard_map/all_to_all | solution.py:295
  116.1 0.0 copy-done.5
  116.1 3.6 %collective-permute-start.2 = (f32[224,384]{1,0:T(8,128)S(1)}, f32[224,384]{1,0:T(8,128)S(1)}, u32[]{:S(2)}, u32[]{:S(2)}) collective-permute-start(f32[224,384]{1,0:T(8,128)S(1)} %copy-done.5), channel_id=1, source_target_pairs={{0,8},{8,0},{16,24},{24,16},{32,40},{40,32},{48,56},{56,48},{64,72... | collective-permute-start | bytes 1032200 | tf_op jit(solution)/shard_map/ppermute | solution.py:290
  119.8 1.3 collective-permute-done.2.got_ref
  121.0 2.5 %shard_map.90 = (bf16[128,768]{1,0:T(8,128)(2,1)}, bf16[128,768]{1,0:T(8,128)(2,1)}, f32[128,768]{1,0:T(8,128)S(1)}, f32[128,768]{1,0:T(8,128)S(1)}, bf16[128,76...) custom-call(bf16[128,768]{1,0:T(8,128)(2,1)S(1)} %copy-done.1, ...), custom_call_target="tpu_custom_call" | custom-call | flops 500000000 | bytes 1000000 | tf_op jit(solution)/shard_map/pallas_call | solution.py:277
  123.5 6.9 %all-to-all-done.4.chip_ref = f32[64,1,640]{2,1,0:T(1,128)S(1)} async-done(((f32[64,1,640]{2,1,0:T(1,128)}), f32[64,1,640]{2,1,0:T(1,128)S(1)}, u32[]{:S(2)}, u32[]{:S(2)}) %all-to-all-start.4) | async-done | bytes 163872 | tf_op jit(solution)/shard_map/all_to_all | solution.py:295
  130.5 0.2 add.7
  130.6 5.9 %collective-permute-start.3 = (f32[64,1,640]{2,1,0:T(1,128)S(1)}, f32[64,1,640]{2,1,0:T(1,128)S(1)}, u32[]{:S(2)}, u32[]{:S(2)}) collective-permute-start(f32[64,1,640]{2,1,0:T(1,128)S(1)} %add.7), channel_id=1, source_target_pairs={{0,8},{8,0},{16,24},{24,16},{32,40},{40,32},{48,56},{56,48},{64,72... | collective-permute-start | bytes 491528 | tf_op jit(solution)/shard_map/ppermute | solution.py:290
  136.5 0.4 shard_map.92
  136.9 0.6 collective-permute-done.3.there_ref
  137.5 1.1 shard_map.93
  (1 shorter events, 0.0 us)
Async XLA Ops:
  0.6 17.7 %copy-start.2 = (bf16[128,768]{1,0:T(8,128)(2,1)S(1)}, bf16[128,768]{1,0:T(8,128)(2,1)}, u32[]{:S(2)}) copy-start(bf16[128,768]{1,0:T(8,128)(2,1)} %c_ref.7) | copy-start | bytes 589828
  0.6 17.7 %copy-start.3 = (bf16[128,768]{1,0:T(8,128)(2,1)S(1)}, bf16[128,768]{1,0:T(8,128)(2,1)}, u32[]{:S(2)}) copy-start(bf16[128,768]{1,0:T(8,128)(2,1)} %k_ref.5) | copy-start | bytes 589828
  1.8 16.6 %copy-start = (bf16[128,768]{1,0:T(8,128)(2,1)S(1)}, bf16[128,768]{1,0:T(8,128)(2,1)}, u32[]{:S(2)}) copy-start(bf16[128,768]{1,0:T(8,128)(2,1)} %v_ref.9) | copy-start | bytes 589828
  1.8 16.6 %copy-start.1 = (bf16[128,768]{1,0:T(8,128)(2,1)S(1)}, bf16[128,768]{1,0:T(8,128)(2,1)}, u32[]{:S(2)}) copy-start(bf16[128,768]{1,0:T(8,128)(2,1)} %q_ref.9) | copy-start | bytes 589828
  2.3 18.1 %collective-permute-start.1 = (f32[64,1,640]{2,1,0:T(1,128)S(1)}, f32[64,1,640]{2,1,0:T(1,128)S(1)}, u32[]{:S(2)}, u32[]{:S(2)}) collective-permute-start(f32[64,1,640]{2,1,0:T(1,128)S(1)} %get-tuple-element.29), channel_id=1, source_target_pairs={{0,8},{8,0},{16,24},{24,16},{32,40},{40,32},{48,56},{56,48},{64,72... | collective-permute-start | bytes 491528 | tf_op jit(solution)/shard_map/ppermute | solution.py:290
  18.5 12.1 %collective-permute-start = (f32[4,128,384]{2,1,0:T(8,128)S(1)}, f32[4,128,384]{2,1,0:T(8,128)S(1)}, u32[]{:S(2)}, u32[]{:S(2)}) collective-permute-start(f32[4,128,384]{2,1,0:T(8,128)S(1)} %shard_map.84), channel_id=1, source_target_pairs={{0,8},{8,0},{16,24},{24,16},{32,40},{40,32},{48,56},{56,48},{64,72... | collective-permute-start | bytes 2359304 | tf_op jit(solution)/shard_map/ppermute | solution.py:290
  21.2 24.5 %all-to-all-start = ((f32[64,1,640]{2,1,0:T(1,128)}), f32[64,1,640]{2,1,0:T(1,128)S(1)}, u32[]{:S(2)}, u32[]{:S(2)}) async-start(f32[64,1,640]{2,1,0:T(1,128)} %add.6), calls=%async_computation | async-start | bytes 327680 | tf_op jit(solution)/shard_map/all_to_all | solution.py:295
  46.5 7.6 %copy-start.6 = (f32[768]{0:T(1024)S(1)}, f32[768]{0:T(1024)}, u32[]{:S(2)}) copy-start(f32[768]{0:T(1024)} %param.8) | copy-start | bytes 9220
  46.5 22.0 %all-to-all-start.1 = ((f32[64,1,640]{2,1,0:T(1,128)}), f32[64,1,640]{2,1,0:T(1,128)S(1)}, u32[]{:S(2)}, u32[]{:S(2)}) async-start(f32[64,1,640]{2,1,0:T(1,128)} %shard_map.87), calls=%async_computation.1 | async-start | bytes 327680 | tf_op jit(solution)/shard_map/all_to_all | solution.py:295
  69.0 18.4 %copy-start.4 = (f32[224,384]{1,0:T(8,128)}, f32[224,384]{1,0:T(8,128)S(1)}, u32[]{:S(2)}) copy-start(f32[224,384]{1,0:T(8,128)S(1)} %get-tuple-element.33) | copy-start | bytes 1032196
  107.9 8.2 %copy-start.5 = (f32[224,384]{1,0:T(8,128)S(1)}, f32[224,384]{1,0:T(8,128)}, u32[]{:S(2)}) copy-start(f32[224,384]{1,0:T(8,128)} %copy-done.4) | copy-start | bytes 1032196
  108.7 21.8 %all-to-all-start.4 = ((f32[64,1,640]{2,1,0:T(1,128)}), f32[64,1,640]{2,1,0:T(1,128)S(1)}, u32[]{:S(2)}, u32[]{:S(2)}) async-start(f32[64,1,640]{2,1,0:T(1,128)} %shard_map.91), calls=%async_computation.4 | async-start | bytes 327680 | tf_op jit(solution)/shard_map/all_to_all | solution.py:295
  116.1 4.9 %collective-permute-start.2 = (f32[224,384]{1,0:T(8,128)S(1)}, f32[224,384]{1,0:T(8,128)S(1)}, u32[]{:S(2)}, u32[]{:S(2)}) collective-permute-start(f32[224,384]{1,0:T(8,128)S(1)} %copy-done.5), channel_id=1, source_target_pairs={{0,8},{8,0},{16,24},{24,16},{32,40},{40,32},{48,56},{56,48},{64,72... | collective-permute-start | bytes 1032200 | tf_op jit(solution)/shard_map/ppermute | solution.py:290
  130.6 6.9 %collective-permute-start.3 = (f32[64,1,640]{2,1,0:T(1,128)S(1)}, f32[64,1,640]{2,1,0:T(1,128)S(1)}, u32[]{:S(2)}, u32[]{:S(2)}) collective-permute-start(f32[64,1,640]{2,1,0:T(1,128)S(1)} %add.7), channel_id=1, source_target_pairs={{0,8},{8,0},{16,24},{24,16},{32,40},{40,32},{48,56},{56,48},{64,72... | collective-permute-start | bytes 491528 | tf_op jit(solution)/shard_map/ppermute | solution.py:290

commit v8 on v6

--- a/solution.py
+++ b/solution.py
@@ -116,23 +116,26 @@
     theirs_ref[:, 0, :] = jnp.where(low, second, first)
 
 
-def send_kernel(q_ref, k_ref, v_ref, c_ref, out_ref):
-    for i, ref in enumerate((q_ref, k_ref, v_ref, c_ref)):
-        out_ref[i] = pick(False, ref[...]).astype(F32)
+def send_kernel(after_ref, q_ref, k_ref, v_ref, c_ref, qc_ref, kv_ref):
+    for out_ref, refs in ((qc_ref, (q_ref, c_ref)), (kv_ref, (k_ref, v_ref))):
+        for i, ref in enumerate(refs):
+            out_ref[i] = pick(False, ref[...]).astype(F32)
 
 
 def attention(q_feat, k_feat):
     return jnp.where(causal4(), mm(q_feat, spread(k_feat), NT), 0.0).astype(BF16)
 
 
-def intra_kernel(q_ref, k_ref, v_ref, got_ref, intra_ref):
+def intra_kernel(q_ref, k_ref, v_ref, got_qc_ref, got_kv_ref, intra_ref):
     mine = [pick(True, ref[...]) for ref in (q_ref, k_ref, v_ref)]
-    others = [got_ref[i].astype(BF16) for i in range(3)]
+    others = [x.astype(BF16) for x in (got_qc_ref[0], got_kv_ref[0], got_kv_ref[1])]
     for i, (q, k, v) in enumerate((mine, others)):
         intra_ref[i] = mm(attention(silu_low(q), silu_low(k)), spread(v), NN)
 
 
-def scan_kernel(backward, pieces_ref, out_ref):
+def scan_kernel(backward, pieces_ref, out_ref, *done):
+    for ref in done:
+        ref[...] = jnp.zeros_like(ref)
     total = jnp.zeros((1, PIECE), F32)
     for i in range(CHIPS):
         chip = CHIPS - 1 - i if backward else i
@@ -161,7 +164,7 @@
     q, c = pick(True, q_ref[...]), pick(True, c_ref[...])
     sums = []
     for i, (q, c, state) in enumerate(
-        ((q, c, own), (got_ref[0].astype(BF16), got_ref[3], other))
+        ((q, c, own), (got_ref[0].astype(BF16), got_ref[1], other))
     ):
         raw = intra_ref[i] + mm(silu_low(q), spread(state.astype(BF16)), NN)
         raw_ref[i] = raw
@@ -196,7 +199,7 @@
     q, c = pick(True, q_ref[...]), pick(True, c_ref[...])
     states = []
     for i, (q, c, totals) in enumerate(
-        zip((q, got_ref[0].astype(BF16)), (c, got_ref[3]), own_and_other(parts_ref))
+        zip((q, got_ref[0].astype(BF16)), (c, got_ref[1]), own_and_other(parts_ref))
     ):
         d_raw = gradient(c, gain, raw_ref[i], *scales(totals))
         states.append(diagonal(mm(silu_low(q), d_raw, TN)))
@@ -303,11 +306,12 @@
 
 
 def scan(pieces, backward):
-    def kernel(pieces_ref, out_ref):
-        scan_kernel(backward, pieces_ref, out_ref)
-
-    (summed,) = call(kernel, [PIECES], across_chips(pieces))
-    return across_chips(summed)
+    def kernel(*refs):
+        scan_kernel(backward, *refs)
+
+    done = [] if backward else [((8, LANES), F32)]
+    summed, *done = call(kernel, [PIECES] + done, across_chips(pieces))
+    return across_chips(summed), *done
 
 
 def per_device(queries, key_input, value_input, norm_gain, cotangent):
@@ -315,14 +319,19 @@
     gain = norm_gain.reshape(1, -1)
     mine, theirs = call(state_kernel, [PIECES, PIECES], jnp.stack([key_input, value_input]))
     received = swap_cores(theirs)
-    (given,) = call(
-        send_kernel, [((4, TOK, HALF), F32)], queries, key_input, value_input, cotangent
-    )
-    got = swap_cores(given)
+    chip, done = scan(mine + received, False)
+    halves = call(
+        send_kernel,
+        [((2, TOK, HALF), F32)] * 2,
+        done, queries, key_input, value_input, cotangent,
+    )
+    got, got_kv = (swap_cores(x) for x in halves)
     (intra,) = call(
-        intra_kernel, [BLOCKS], queries, key_input, value_input, got, flops=200_000_000
-    )
-    chip = scan(mine + received, False)
+        intra_kernel,
+        [BLOCKS],
+        queries, key_input, value_input, got, got_kv,
+        flops=200_000_000,
+    )
     raw, low, give, parts = call(
         raw_kernel,
         [BLOCKS, ((HEAD_DIM, HALF), BF16), ((TOK + HEAD_DIM, HALF), F32), ((sharers, 4, TOK), F32)],
@@ -341,7 +350,7 @@
         own, other,
         flops=500_000_000,
     )
-    chip = scan(total, True)
+    (chip,) = scan(total, True)
     there = swap_cores(chip + there)
     parts = key_input, value_input, grad_kf, grad_vf
     own = call(own_kernel, [HALF_LOW, HALF_LOW], *parts, chip, here, flops=50_000_000)

time: 138 us -> 137 us (level)
  blocking collectives: 38.1 us -> 63.1 us
  waiting for transfers between devices: 36.9 us -> 18.4 us
  starting transfers between devices: 52.2 us -> 45.5 us
    all_to_all x1 -> x2, blocking collectives: 20.7 us -> 45.6 us  [across_chips(): return lax.all_to_all(x, 'ctx', 0, 0, axis_index_groups=groups)]
    all_to_all x3 -> x2, waiting for transfers between devices: 34 us -> 13.8 us  [across_chips(): return lax.all_to_all(x, 'ctx', 0, 0, axis_index_groups=groups)]
    all_to_all x3 -> x2, starting transfers between devices: 24 us -> 14.6 us  [across_chips(): return lax.all_to_all(x, 'ctx', 0, 0, axis_index_groups=groups)]
    ppermute x4 -> x5, starting transfers between devices: 28.1 us -> 30.9 us  [swap_cores(): return lax.ppermute(x, 'ctx', pairs)]
    ppermute x4 -> x5, waiting for transfers between devices: 2.9 us -> 4.55 us  [swap_cores(): return lax.ppermute(x, 'ctx', pairs)]
where the time goes in v8:
time: 137 us
  blocking collectives  63.1 us (46%)
  starting transfers between devices  45.5 us (33%)
  waiting for transfers between devices  18.4 us (13%)
  Pallas kernels  7.65 us (6%)
  other arithmetic  1.4 us (1%)
    all_to_all x2, blocking collectives, across_chips(): return lax.all_to_all(x, 'ctx', 0, 0, axis_index_groups=groups)  45.6 us
    ppermute x5, starting transfers between devices, swap_cores(): return lax.ppermute(x, 'ctx', pairs)  30.9 us
    all_to_all x1, blocking collectives, over_heads(): return lax.all_to_all(x, ('ctx', 'head'), 0, 0, axis_index_groups=groups)  17.5 us
    all_to_all x2, starting transfers between devices, across_chips(): return lax.all_to_all(x, 'ctx', 0, 0, axis_index_groups=groups)  14.6 us
    all_to_all x2, waiting for transfers between devices, across_chips(): return lax.all_to_all(x, 'ctx', 0, 0, axis_index_groups=groups)  13.8 us
    pallas_call x10, Pallas kernels, call(): pl.pallas_call(kernel, out_shape=[jax.ShapeDtypeStruct(shape, kind) for s...  7.65 us
    ppermute x5, waiting for transfers between devices, swap_cores(): return lax.ppermute(x, 'ctx', pairs)  4.55 us
  transfers between devices with their start and end apart: 7, of which 6 were waited for; matrix products, arithmetic and copies ran while one was open for 0% of the time, Pallas kernels for 3%

profile of v8, /device:TPU:1, one launch (start us, length us, event | category | flops | bytes accessed | tf_op | source)
XLA Modules:
  0.0 136.8 jit_solution(4558111059793297893)
XLA Ops:
  0.6 1.1 pad_maximum_fusion.pair_ref
  1.7 0.5 shard_map.84
  2.2 16.1 %collective-permute-start = (f32[64,1,640]{2,1,0:T(1,128)S(1)}, f32[64,1,640]{2,1,0:T(1,128)S(1)}, u32[]{:S(2)}, u32[]{:S(2)}) collective-permute-start(f32[64,1,640]{2,1,0:T(1,128)S(1)} %get-tuple-element.28), channel_id=1, source_target_pairs={{0,8},{8,0},{16,24},{24,16},{32,40},{40,32},{48,56},{56,48},{64,72... | collective-permute-start | bytes 491528 | tf_op jit(solution)/shard_map/ppermute | solution.py:286
  18.2 1.0 collective-permute-done.received_ref
  19.2 0.2 add.6
  19.4 0.0 copy-start.2
  19.4 0.0 copy-start.3
  19.4 25.0 %all_to_all.25.refs_0_ = f32[64,1,640]{2,1,0:T(1,128)S(1)} all-to-all(f32[64,1,640]{2,1,0:T(1,128)S(1)} %add.6), channel_id=1, replica_groups={{0,16,32,48,64,80,96,112,128,144,160,176,192,208,224,240,256,272,288,30..., dimensions={0} | all-to-all | bytes 327680 | tf_op jit(solution)/shard_map/all_to_all | solution.py:291
  44.4 0.0 copy-start.1
  44.5 0.7 shard_map.85
  45.2 0.0 copy-start
  45.2 7.1 %all-to-all-start.1 = ((f32[64,1,640]{2,1,0:T(1,128)}), f32[64,1,640]{2,1,0:T(1,128)S(1)}, u32[]{:S(2)}, u32[]{:S(2)}) async-start(f32[64,1,640]{2,1,0:T(1,128)} %get-tuple-element.32), calls=%async_computation.1 | async-start | bytes 327680 | tf_op jit(solution)/shard_map/all_to_all | solution.py:291
  52.3 0.0 copy-done.2
  52.4 0.0 copy-done.3
  52.4 0.0 copy-done.1
  52.4 0.0 copy-done
  52.4 0.0 copy-start.4
  52.4 0.1 shard_map.86
  52.5 3.4 %collective-permute-start.1 = (f32[2,128,384]{2,1,0:T(8,128)S(1)}, f32[2,128,384]{2,1,0:T(8,128)S(1)}, u32[]{:S(2)}, u32[]{:S(2)}) collective-permute-start(f32[2,128,384]{2,1,0:T(8,128)S(1)} %get-tuple-element.30), channel_id=1, source_target_pairs={{0,8},{8,0},{16,24},{24,16},{32,40},{40,32},{48,56},{56,48},{64,72... | collective-permute-start | bytes 1179656 | tf_op jit(solution)/shard_map/ppermute | solution.py:286
  55.9 1.9 %collective-permute-start.2 = (f32[2,128,384]{2,1,0:T(8,128)S(1)}, f32[2,128,384]{2,1,0:T(8,128)S(1)}, u32[]{:S(2)}, u32[]{:S(2)}) collective-permute-start(f32[2,128,384]{2,1,0:T(8,128)S(1)} %get-tuple-element.31), channel_id=1, source_target_pairs={{0,8},{8,0},{16,24},{24,16},{32,40},{40,32},{48,56},{56,48},{64,72... | collective-permute-start | bytes 1179656 | tf_op jit(solution)/shard_map/ppermute | solution.py:286
  57.8 0.0 copy-done.4
  57.8 0.0 collective-permute-done.1.got_qc_ref.got_ref
  57.8 1.7 %collective-permute-done.2.got_kv_ref = f32[2,128,384]{2,1,0:T(8,128)S(1)} collective-permute-done((f32[2,128,384]{2,1,0:T(8,128)S(1)}, f32[2,128,384]{2,1,0:T(8,128)S(1)}, u32[]{:S(2)}, u32[]{:S(2)}) %collective-permute-start.2) | collective-permute-done | bytes 393248 | tf_op jit(solution)/shard_map/ppermute | solution.py:286
  59.5 0.8 shard_map.87.intra_ref
  60.3 6.8 %all-to-all-done.1.chip_ref = f32[64,1,640]{2,1,0:T(1,128)S(1)} async-done(((f32[64,1,640]{2,1,0:T(1,128)}), f32[64,1,640]{2,1,0:T(1,128)S(1)}, u32[]{:S(2)}, u32[]{:S(2)}) %all-to-all-start.1) | async-done | bytes 163872 | tf_op jit(solution)/shard_map/all_to_all | solution.py:291
  67.0 0.5 shard_map.88
  67.6 17.5 %all_to_all.26.parts_ref = f32[16,4,128]{2,1,0:T(4,128)S(1)} all-to-all(f32[16,4,128]{2,1,0:T(4,128)S(1)} %get-tuple-element.36), channel_id=1, replica_groups={{0,1,2,3,4,5,6,7,8,9,10,11,12,13,14,15},{16,17,18,19,20,21,22,23,24,25,..., dimensions={0} | all-to-all | bytes 65536 | tf_op jit(solution)/shard_map/all_to_all | solution.py:297
  85.0 0.5 shard_map.89
  85.5 20.6 %all_to_all.27.refs_0_ = f32[64,1,640]{2,1,0:T(1,128)S(1)} all-to-all(f32[64,1,640]{2,1,0:T(1,128)S(1)} %get-tuple-element.43), channel_id=1, replica_groups={{0,16,32,48,64,80,96,112,128,144,160,176,192,208,224,240,256,272,288,30..., dimensions={0} | all-to-all | bytes 327680 | tf_op jit(solution)/shard_map/all_to_all | solution.py:291
  106.2 0.7 shard_map.91
  106.9 7.5 %all-to-all-start.4 = ((f32[64,1,640]{2,1,0:T(1,128)}), f32[64,1,640]{2,1,0:T(1,128)S(1)}, u32[]{:S(2)}, u32[]{:S(2)}) async-start(f32[64,1,640]{2,1,0:T(1,128)} %shard_map.91), calls=%async_computation.4 | async-start | bytes 327680 | tf_op jit(solution)/shard_map/all_to_all | solution.py:291
  114.4 3.6 %collective-permute-start.3 = (f32[224,384]{1,0:T(8,128)S(1)}, f32[224,384]{1,0:T(8,128)S(1)}, u32[]{:S(2)}, u32[]{:S(2)}) collective-permute-start(f32[224,384]{1,0:T(8,128)S(1)} %get-tuple-element.35), channel_id=1, source_target_pairs={{0,8},{8,0},{16,24},{24,16},{32,40},{40,32},{48,56},{56,48},{64,72... | collective-permute-start | bytes 1032200 | tf_op jit(solution)/shard_map/ppermute | solution.py:286
  118.0 1.3 collective-permute-done.3.got_ref
  119.3 2.4 %shard_map.90 = (bf16[128,768]{1,0:T(8,128)(2,1)}, bf16[128,768]{1,0:T(8,128)(2,1)}, f32[128,768]{1,0:T(8,128)S(1)}, f32[128,768]{1,0:T(8,128)S(1)}, f32[96,384]{1,0:T(8,128)S(1)}, /*index=5*/f32[64,1,640]{2,1,0:T(1,128)S(1)}) custom-call(bf16[128,768]{1,0:T(8,128)(2,1)S(1)} %copy-done.2, bf16[128,768]{1,0:T(8,128)(2,1)S(1)} %copy-done, ...), custom_call_target="tpu_custom_call" | custom-call | flops 500000000 | bytes 1000000 | tf_op jit(solution)/shard_map/pallas_call | solution.py:273
  121.7 7.0 %all-to-all-done.4.chip_ref = f32[64,1,640]{2,1,0:T(1,128)S(1)} async-done(((f32[64,1,640]{2,1,0:T(1,128)}), f32[64,1,640]{2,1,0:T(1,128)S(1)}, u32[]{:S(2)}, u32[]{:S(2)}) %all-to-all-start.4) | async-done | bytes 163872 | tf_op jit(solution)/shard_map/all_to_all | solution.py:291
  128.7 0.2 add.7
  128.9 5.9 %collective-permute-start.4 = (f32[64,1,640]{2,1,0:T(1,128)S(1)}, f32[64,1,640]{2,1,0:T(1,128)S(1)}, u32[]{:S(2)}, u32[]{:S(2)}) collective-permute-start(f32[64,1,640]{2,1,0:T(1,128)S(1)} %add.7), channel_id=1, source_target_pairs={{0,8},{8,0},{16,24},{24,16},{32,40},{40,32},{48,56},{56,48},{64,72... | collective-permute-start | bytes 491528 | tf_op jit(solution)/shard_map/ppermute | solution.py:286
  134.8 0.4 shard_map.92
  135.1 0.6 collective-permute-done.4.there_ref
  135.8 1.1 shard_map.93
  (1 shorter events, 0.0 us)
Async XLA Ops:
  2.2 17.1 %collective-permute-start = (f32[64,1,640]{2,1,0:T(1,128)S(1)}, f32[64,1,640]{2,1,0:T(1,128)S(1)}, u32[]{:S(2)}, u32[]{:S(2)}) collective-permute-start(f32[64,1,640]{2,1,0:T(1,128)S(1)} %get-tuple-element.28), channel_id=1, source_target_pairs={{0,8},{8,0},{16,24},{24,16},{32,40},{40,32},{48,56},{56,48},{64,72... | collective-permute-start | bytes 491528 | tf_op jit(solution)/shard_map/ppermute | solution.py:286
  19.4 32.9 %copy-start.2 = (bf16[128,768]{1,0:T(8,128)(2,1)S(1)}, bf16[128,768]{1,0:T(8,128)(2,1)}, u32[]{:S(2)}) copy-start(bf16[128,768]{1,0:T(8,128)(2,1)} %q_ref.9) | copy-start | bytes 589828
  19.4 32.9 %copy-start.3 = (bf16[128,768]{1,0:T(8,128)(2,1)S(1)}, bf16[128,768]{1,0:T(8,128)(2,1)}, u32[]{:S(2)}) copy-start(bf16[128,768]{1,0:T(8,128)(2,1)} %c_ref.7) | copy-start | bytes 589828
  44.4 7.9 %copy-start.1 = (bf16[128,768]{1,0:T(8,128)(2,1)S(1)}, bf16[128,768]{1,0:T(8,128)(2,1)}, u32[]{:S(2)}) copy-start(bf16[128,768]{1,0:T(8,128)(2,1)} %v_ref.9) | copy-start | bytes 589828
  45.2 7.2 %copy-start = (bf16[128,768]{1,0:T(8,128)(2,1)S(1)}, bf16[128,768]{1,0:T(8,128)(2,1)}, u32[]{:S(2)}) copy-start(bf16[128,768]{1,0:T(8,128)(2,1)} %k_ref.9) | copy-start | bytes 589828
  45.2 21.9 %all-to-all-start.1 = ((f32[64,1,640]{2,1,0:T(1,128)}), f32[64,1,640]{2,1,0:T(1,128)S(1)}, u32[]{:S(2)}, u32[]{:S(2)}) async-start(f32[64,1,640]{2,1,0:T(1,128)} %get-tuple-element.32), calls=%async_computation.1 | async-start | bytes 327680 | tf_op jit(solution)/shard_map/all_to_all | solution.py:291
  52.4 5.4 %copy-start.4 = (f32[768]{0:T(1024)S(1)}, f32[768]{0:T(1024)}, u32[]{:S(2)}) copy-start(f32[768]{0:T(1024)} %param.8) | copy-start | bytes 9220
  52.5 5.3 %collective-permute-start.1 = (f32[2,128,384]{2,1,0:T(8,128)S(1)}, f32[2,128,384]{2,1,0:T(8,128)S(1)}, u32[]{:S(2)}, u32[]{:S(2)}) collective-permute-start(f32[2,128,384]{2,1,0:T(8,128)S(1)} %get-tuple-element.30), channel_id=1, source_target_pairs={{0,8},{8,0},{16,24},{24,16},{32,40},{40,32},{48,56},{56,48},{64,72... | collective-permute-start | bytes 1179656 | tf_op jit(solution)/shard_map/ppermute | solution.py:286
  55.9 3.6 %collective-permute-start.2 = (f32[2,128,384]{2,1,0:T(8,128)S(1)}, f32[2,128,384]{2,1,0:T(8,128)S(1)}, u32[]{:S(2)}, u32[]{:S(2)}) collective-permute-start(f32[2,128,384]{2,1,0:T(8,128)S(1)} %get-tuple-element.31), channel_id=1, source_target_pairs={{0,8},{8,0},{16,24},{24,16},{32,40},{40,32},{48,56},{56,48},{64,72... | collective-permute-start | bytes 1179656 | tf_op jit(solution)/shard_map/ppermute | solution.py:286
  106.9 21.8 %all-to-all-start.4 = ((f32[64,1,640]{2,1,0:T(1,128)}), f32[64,1,640]{2,1,0:T(1,128)S(1)}, u32[]{:S(2)}, u32[]{:S(2)}) async-start(f32[64,1,640]{2,1,0:T(1,128)} %shard_map.91), calls=%async_computation.4 | async-start | bytes 327680 | tf_op jit(solution)/shard_map/all_to_all | solution.py:291
  114.4 4.9 %collective-permute-start.3 = (f32[224,384]{1,0:T(8,128)S(1)}, f32[224,384]{1,0:T(8,128)S(1)}, u32[]{:S(2)}, u32[]{:S(2)}) collective-permute-start(f32[224,384]{1,0:T(8,128)S(1)} %get-tuple-element.35), channel_id=1, source_target_pairs={{0,8},{8,0},{16,24},{24,16},{32,40},{40,32},{48,56},{56,48},{64,72... | collective-permute-start | bytes 1032200 | tf_op jit(solution)/shard_map/ppermute | solution.py:286
  128.9 6.9 %collective-permute-start.4 = (f32[64,1,640]{2,1,0:T(1,128)S(1)}, f32[64,1,640]{2,1,0:T(1,128)S(1)}, u32[]{:S(2)}, u32[]{:S(2)}) collective-permute-start(f32[64,1,640]{2,1,0:T(1,128)S(1)} %add.7), channel_id=1, source_target_pairs={{0,8},{8,0},{16,24},{24,16},{32,40},{40,32},{48,56},{56,48},{64,72... | collective-permute-start | bytes 491528 | tf_op jit(solution)/shard_map/ppermute | solution.py:286

commit v9 on v8

--- a/solution.py
+++ b/solution.py
@@ -1,3 +1,5 @@
+import functools
+
 import jax
 import jax.numpy as jnp
 from jax import lax
@@ -14,6 +16,8 @@
 CHIPS = 64
 CORES = 2
 PIECE = 640
+PARTS = 4
+PART = CHIPS // PARTS
 
 epsilon = 1e-06
 F32 = jnp.float32
@@ -106,14 +110,9 @@
     return jnp.where(first, own, other), jnp.where(first, other, own)
 
 
-def state_kernel(pair_ref, mine_ref, theirs_ref):
-    first, second = (
-        to_pieces(diagonal(mm(silu_low(pair_ref[0, :, half(g)]), pair_ref[1, :, half(g)], TN)))
-        for g in range(CORES)
-    )
-    low = core_index() == 0
-    mine_ref[:, 0, :] = jnp.where(low, first, second)
-    theirs_ref[:, 0, :] = jnp.where(low, second, first)
+def state_kernel(own, pair_ref, out_ref):
+    k, v = pick(own, pair_ref[0]), pick(own, pair_ref[1])
+    out_ref[:, 0, :] = to_pieces(diagonal(mm(silu_low(k), v, TN)))
 
 
 def send_kernel(after_ref, q_ref, k_ref, v_ref, c_ref, qc_ref, kv_ref):
@@ -133,14 +132,24 @@
         intra_ref[i] = mm(attention(silu_low(q), silu_low(k)), spread(v), NN)
 
 
-def scan_kernel(backward, pieces_ref, out_ref, *done):
+def scan_kernel(backward, pieces_ref, out_hbm, *refs):
+    *done, rows_ref, sems = refs
+    total = jnp.zeros((1, PIECE), F32)
+    copies = []
+    for part in range(PARTS):
+        first = (PARTS - 1 - part if backward else part) * PART
+        for i in range(PART):
+            chip = first + (PART - 1 - i if backward else i)
+            rows_ref[chip] = total
+            total = total + pieces_ref[chip]
+        rows = pl.ds(first, PART)
+        copy = pltpu.make_async_copy(rows_ref.at[rows], out_hbm.at[rows], sems.at[part])
+        copy.start()
+        copies.append(copy)
     for ref in done:
         ref[...] = jnp.zeros_like(ref)
-    total = jnp.zeros((1, PIECE), F32)
-    for i in range(CHIPS):
-        chip = CHIPS - 1 - i if backward else i
-        out_ref[chip] = total
-        total = total + pieces_ref[chip]
+    for copy in copies:
+        copy.wait()
 
 
 def lane_sums(x):
@@ -269,12 +278,12 @@
         copy.wait()
 
 
-def call(kernel, outs, *args, flops=0, out_space=VMEM, scratch=()):
+def call(kernel, outs, *args, flops=0, out_spaces=None, scratch=()):
     return pl.pallas_call(
         kernel,
         out_shape=[jax.ShapeDtypeStruct(shape, kind) for shape, kind in outs],
         in_specs=[VMEM] * len(args),
-        out_specs=[out_space] * len(outs),
+        out_specs=out_spaces or [VMEM] * len(outs),
         scratch_shapes=list(scratch),
         compiler_params=pltpu.CompilerParams(vmem_limit_bytes=32 * 1024 * 1024),
         cost_estimate=pl.CostEstimate(flops=flops, bytes_accessed=1_000_000, transcendentals=0),
@@ -310,15 +319,21 @@
         scan_kernel(backward, *refs)
 
     done = [] if backward else [((8, LANES), F32)]
-    summed, *done = call(kernel, [PIECES] + done, across_chips(pieces))
+    spaces = [pl.BlockSpec(memory_space=pltpu.HBM)] + [VMEM] * len(done)
+    rows = [pltpu.VMEM(*PIECES), pltpu.SemaphoreType.DMA((PARTS,))]
+    summed, *done = call(
+        kernel, [PIECES] + done, across_chips(pieces), out_spaces=spaces, scratch=rows
+    )
     return across_chips(summed), *done
 
 
 def per_device(queries, key_input, value_input, norm_gain, cotangent):
     sharers = CORES * lax.axis_size("head")
     gain = norm_gain.reshape(1, -1)
-    mine, theirs = call(state_kernel, [PIECES, PIECES], jnp.stack([key_input, value_input]))
+    pair = jnp.stack([key_input, value_input])
+    (theirs,) = call(functools.partial(state_kernel, False), [PIECES], pair)
     received = swap_cores(theirs)
+    (mine,) = call(functools.partial(state_kernel, True), [PIECES], pair)
     chip, done = scan(mine + received, False)
     halves = call(
         send_kernel,
@@ -359,7 +374,7 @@
         last_kernel,
         [WIDE_LOW, WIDE_LOW],
         *parts, there, *own,
-        out_space=pl.BlockSpec(memory_space=pltpu.HBM),
+        out_spaces=[pl.BlockSpec(memory_space=pltpu.HBM)] * 2,
         scratch=store,
     )
     return (attended, grad_query, grad_key, grad_value)

time: 137 us -> 137 us (level)
    pallas_call x10 -> x11, Pallas kernels: 7.65 us -> 7.93 us  [call(): pl.pallas_call(kernel, out_shape=[jax.ShapeDtypeStruct(shape, kind) for s...]
where the time goes in v9:
time: 137 us
  blocking collectives  63.1 us (46%)
  starting transfers between devices  45.5 us (33%)
  waiting for transfers between devices  18 us (13%)
  Pallas kernels  7.93 us (6%)
  other arithmetic  1.4 us (1%)
    all_to_all x2, blocking collectives, across_chips(): return lax.all_to_all(x, 'ctx', 0, 0, axis_index_groups=groups)  45.7 us
    ppermute x5, starting transfers between devices, swap_cores(): return lax.ppermute(x, 'ctx', pairs)  30.9 us
    all_to_all x1, blocking collectives, over_heads(): return lax.all_to_all(x, ('ctx', 'head'), 0, 0, axis_index_groups=groups)  17.5 us
    all_to_all x2, starting transfers between devices, across_chips(): return lax.all_to_all(x, 'ctx', 0, 0, axis_index_groups=groups)  14.6 us
    all_to_all x2, waiting for transfers between devices, across_chips(): return lax.all_to_all(x, 'ctx', 0, 0, axis_index_groups=groups)  13.8 us
    pallas_call x11, Pallas kernels, call(): pl.pallas_call(kernel, out_shape=[jax.ShapeDtypeStruct(shape, kind) for s...  7.93 us
    ppermute x5, waiting for transfers between devices, swap_cores(): return lax.ppermute(x, 'ctx', pairs)  4.16 us
  transfers between devices with their start and end apart: 7, of which 6 were waited for; matrix products, arithmetic and copies ran while one was open for 0% of the time, Pallas kernels for 3%

profile of v9, /device:TPU:1, one launch (start us, length us, event | category | flops | bytes accessed | tf_op | source)
XLA Modules:
  0.0 136.8 jit_solution(17366013256931731632)
XLA Ops:
  0.6 1.1 pad_maximum_fusion.pair_ref
  1.7 0.4 shard_map.85
  2.1 16.1 %collective-permute-start = (f32[64,1,640]{2,1,0:T(1,128)S(1)}, f32[64,1,640]{2,1,0:T(1,128)S(1)}, u32[]{:S(2)}, u32[]{:S(2)}) collective-permute-start(f32[64,1,640]{2,1,0:T(1,128)S(1)} %shard_map.85), channel_id=1, source_target_pairs={{0,8},{8,0},{16,24},{24,16},{32,40},{40,32},{48,56},{56,48},{64,72... | collective-permute-start | bytes 491528 | tf_op jit(solution)/shard_map/ppermute | solution.py:295
  18.2 0.4 shard_map.84.mine_ref
  18.6 0.6 collective-permute-done.received_ref
  19.2 0.2 add.6
  19.3 0.0 copy-start.2
  19.3 0.0 copy-start.3
  19.4 25.0 %all_to_all.25.refs_0_ = f32[64,1,640]{2,1,0:T(1,128)S(1)} all-to-all(f32[64,1,640]{2,1,0:T(1,128)S(1)} %add.6), channel_id=1, replica_groups={{0,16,32,48,64,80,96,112,128,144,160,176,192,208,224,240,256,272,288,30..., dimensions={0} | all-to-all | bytes 327680 | tf_op jit(solution)/shard_map/all_to_all | solution.py:300
  44.4 0.0 copy-start.1
  44.4 0.7 shard_map.86
  45.1 0.0 copy-start
  45.1 7.2 %all-to-all-start.1 = ((f32[64,1,640]{2,1,0:T(1,128)}), f32[64,1,640]{2,1,0:T(1,128)S(1)}, u32[]{:S(2)}, u32[]{:S(2)}) async-start(f32[64,1,640]{2,1,0:T(1,128)} %get-tuple-element.28), calls=%async_computation.1 | async-start | bytes 327680 | tf_op jit(solution)/shard_map/all_to_all | solution.py:300
  52.3 0.0 copy-done.2
  52.3 0.0 copy-done.3
  52.3 0.0 copy-done.1
  52.3 0.0 copy-done
  52.3 0.0 copy-start.4
  52.3 0.1 shard_map.87
  52.4 3.4 %collective-permute-start.1 = (f32[2,128,384]{2,1,0:T(8,128)S(1)}, f32[2,128,384]{2,1,0:T(8,128)S(1)}, u32[]{:S(2)}, u32[]{:S(2)}) collective-permute-start(f32[2,128,384]{2,1,0:T(8,128)S(1)} %get-tuple-element.26), channel_id=1, source_target_pairs={{0,8},{8,0},{16,24},{24,16},{32,40},{40,32},{48,56},{56,48},{64,72... | collective-permute-start | bytes 1179656 | tf_op jit(solution)/shard_map/ppermute | solution.py:295
  55.8 1.9 %collective-permute-start.2 = (f32[2,128,384]{2,1,0:T(8,128)S(1)}, f32[2,128,384]{2,1,0:T(8,128)S(1)}, u32[]{:S(2)}, u32[]{:S(2)}) collective-permute-start(f32[2,128,384]{2,1,0:T(8,128)S(1)} %get-tuple-element.27), channel_id=1, source_target_pairs={{0,8},{8,0},{16,24},{24,16},{32,40},{40,32},{48,56},{56,48},{64,72... | collective-permute-start | bytes 1179656 | tf_op jit(solution)/shard_map/ppermute | solution.py:295
  57.7 0.0 copy-done.4
  57.7 0.0 collective-permute-done.1.got_qc_ref.got_ref
  57.8 1.7 %collective-permute-done.2.got_kv_ref = f32[2,128,384]{2,1,0:T(8,128)S(1)} collective-permute-done((f32[2,128,384]{2,1,0:T(8,128)S(1)}, f32[2,128,384]{2,1,0:T(8,128)S(1)}, u32[]{:S(2)}, u32[]{:S(2)}) %collective-permute-start.2) | collective-permute-done | bytes 393248 | tf_op jit(solution)/shard_map/ppermute | solution.py:295
  59.4 0.8 shard_map.88.intra_ref
  60.2 6.8 %all-to-all-done.1.chip_ref = f32[64,1,640]{2,1,0:T(1,128)S(1)} async-done(((f32[64,1,640]{2,1,0:T(1,128)}), f32[64,1,640]{2,1,0:T(1,128)S(1)}, u32[]{:S(2)}, u32[]{:S(2)}) %all-to-all-start.1) | async-done | bytes 163872 | tf_op jit(solution)/shard_map/all_to_all | solution.py:300
  67.0 0.5 shard_map.89
  67.5 17.5 %all_to_all.26.parts_ref = f32[16,4,128]{2,1,0:T(4,128)S(1)} all-to-all(f32[16,4,128]{2,1,0:T(4,128)S(1)} %get-tuple-element.32), channel_id=1, replica_groups={{0,1,2,3,4,5,6,7,8,9,10,11,12,13,14,15},{16,17,18,19,20,21,22,23,24,25,..., dimensions={0} | all-to-all | bytes 65536 | tf_op jit(solution)/shard_map/all_to_all | solution.py:306
  85.0 0.5 shard_map.90
  85.5 20.7 %all_to_all.27.refs_0_ = f32[64,1,640]{2,1,0:T(1,128)S(1)} all-to-all(f32[64,1,640]{2,1,0:T(1,128)S(1)} %get-tuple-element.39), channel_id=1, replica_groups={{0,16,32,48,64,80,96,112,128,144,160,176,192,208,224,240,256,272,288,30..., dimensions={0} | all-to-all | bytes 327680 | tf_op jit(solution)/shard_map/all_to_all | solution.py:300
  106.1 0.7 shard_map.92
  106.9 7.4 %all-to-all-start.4 = ((f32[64,1,640]{2,1,0:T(1,128)}), f32[64,1,640]{2,1,0:T(1,128)S(1)}, u32[]{:S(2)}, u32[]{:S(2)}) async-start(f32[64,1,640]{2,1,0:T(1,128)} %shard_map.92), calls=%async_computation.4 | async-start | bytes 327680 | tf_op jit(solution)/shard_map/all_to_all | solution.py:300
  114.3 3.6 %collective-permute-start.3 = (f32[224,384]{1,0:T(8,128)S(1)}, f32[224,384]{1,0:T(8,128)S(1)}, u32[]{:S(2)}, u32[]{:S(2)}) collective-permute-start(f32[224,384]{1,0:T(8,128)S(1)} %get-tuple-element.31), channel_id=1, source_target_pairs={{0,8},{8,0},{16,24},{24,16},{32,40},{40,32},{48,56},{56,48},{64,72... | collective-permute-start | bytes 1032200 | tf_op jit(solution)/shard_map/ppermute | solution.py:295
  118.0 1.3 collective-permute-done.3.got_ref
  119.2 2.4 %shard_map.91 = (bf16[128,768]{1,0:T(8,128)(2,1)}, bf16[128,768]{1,0:T(8,128)(2,1)}, f32[128,768]{1,0:T(8,128)S(1)}, f32[128,768]{1,0:T(8,128)S(1)}, f32[96,384]{1,0:T(8,128)S(1)}, /*index=5*/f32[64,1,640]{2,1,0:T(1,128)S(1)}) custom-call(bf16[128,768]{1,0:T(8,128)(2,1)S(1)} %copy-done.2, bf16[128,768]{1,0:T(8,128)(2,1)S(1)} %copy-done, ...), custom_call_target="tpu_custom_call" | custom-call | flops 500000000 | bytes 1000000 | tf_op jit(solution)/shard_map/pallas_call | solution.py:282
  121.6 7.0 %all-to-all-done.4.chip_ref = f32[64,1,640]{2,1,0:T(1,128)S(1)} async-done(((f32[64,1,640]{2,1,0:T(1,128)}), f32[64,1,640]{2,1,0:T(1,128)S(1)}, u32[]{:S(2)}, u32[]{:S(2)}) %all-to-all-start.4) | async-done | bytes 163872 | tf_op jit(solution)/shard_map/all_to_all | solution.py:300
  128.6 0.2 add.7
  128.8 5.9 %collective-permute-start.4 = (f32[64,1,640]{2,1,0:T(1,128)S(1)}, f32[64,1,640]{2,1,0:T(1,128)S(1)}, u32[]{:S(2)}, u32[]{:S(2)}) collective-permute-start(f32[64,1,640]{2,1,0:T(1,128)S(1)} %add.7), channel_id=1, source_target_pairs={{0,8},{8,0},{16,24},{24,16},{32,40},{40,32},{48,56},{56,48},{64,72... | collective-permute-start | bytes 491528 | tf_op jit(solution)/shard_map/ppermute | solution.py:295
  134.7 0.4 shard_map.93
  135.1 0.6 collective-permute-done.4.there_ref
  135.7 1.1 shard_map.94
  (1 shorter events, 0.0 us)
Async XLA Ops:
  2.1 17.1 %collective-permute-start = (f32[64,1,640]{2,1,0:T(1,128)S(1)}, f32[64,1,640]{2,1,0:T(1,128)S(1)}, u32[]{:S(2)}, u32[]{:S(2)}) collective-permute-start(f32[64,1,640]{2,1,0:T(1,128)S(1)} %shard_map.85), channel_id=1, source_target_pairs={{0,8},{8,0},{16,24},{24,16},{32,40},{40,32},{48,56},{56,48},{64,72... | collective-permute-start | bytes 491528 | tf_op jit(solution)/shard_map/ppermute | solution.py:295
  19.3 32.9 %copy-start.2 = (bf16[128,768]{1,0:T(8,128)(2,1)S(1)}, bf16[128,768]{1,0:T(8,128)(2,1)}, u32[]{:S(2)}) copy-start(bf16[128,768]{1,0:T(8,128)(2,1)} %q_ref.9) | copy-start | bytes 589828
  19.3 32.9 %copy-start.3 = (bf16[128,768]{1,0:T(8,128)(2,1)S(1)}, bf16[128,768]{1,0:T(8,128)(2,1)}, u32[]{:S(2)}) copy-start(bf16[128,768]{1,0:T(8,128)(2,1)} %c_ref.7) | copy-start | bytes 589828
  44.4 7.9 %copy-start.1 = (bf16[128,768]{1,0:T(8,128)(2,1)S(1)}, bf16[128,768]{1,0:T(8,128)(2,1)}, u32[]{:S(2)}) copy-start(bf16[128,768]{1,0:T(8,128)(2,1)} %v_ref.9) | copy-start | bytes 589828
  45.1 7.2 %copy-start = (bf16[128,768]{1,0:T(8,128)(2,1)S(1)}, bf16[128,768]{1,0:T(8,128)(2,1)}, u32[]{:S(2)}) copy-start(bf16[128,768]{1,0:T(8,128)(2,1)} %k_ref.9) | copy-start | bytes 589828
  45.1 21.9 %all-to-all-start.1 = ((f32[64,1,640]{2,1,0:T(1,128)}), f32[64,1,640]{2,1,0:T(1,128)S(1)}, u32[]{:S(2)}, u32[]{:S(2)}) async-start(f32[64,1,640]{2,1,0:T(1,128)} %get-tuple-element.28), calls=%async_computation.1 | async-start | bytes 327680 | tf_op jit(solution)/shard_map/all_to_all | solution.py:300
  52.3 5.4 %copy-start.4 = (f32[768]{0:T(1024)S(1)}, f32[768]{0:T(1024)}, u32[]{:S(2)}) copy-start(f32[768]{0:T(1024)} %param.8) | copy-start | bytes 9220
  52.4 5.3 %collective-permute-start.1 = (f32[2,128,384]{2,1,0:T(8,128)S(1)}, f32[2,128,384]{2,1,0:T(8,128)S(1)}, u32[]{:S(2)}, u32[]{:S(2)}) collective-permute-start(f32[2,128,384]{2,1,0:T(8,128)S(1)} %get-tuple-element.26), channel_id=1, source_target_pairs={{0,8},{8,0},{16,24},{24,16},{32,40},{40,32},{48,56},{56,48},{64,72... | collective-permute-start | bytes 1179656 | tf_op jit(solution)/shard_map/ppermute | solution.py:295
  55.8 3.6 %collective-permute-start.2 = (f32[2,128,384]{2,1,0:T(8,128)S(1)}, f32[2,128,384]{2,1,0:T(8,128)S(1)}, u32[]{:S(2)}, u32[]{:S(2)}) collective-permute-start(f32[2,128,384]{2,1,0:T(8,128)S(1)} %get-tuple-element.27), channel_id=1, source_target_pairs={{0,8},{8,0},{16,24},{24,16},{32,40},{40,32},{48,56},{56,48},{64,72... | collective-permute-start | bytes 1179656 | tf_op jit(solution)/shard_map/ppermute | solution.py:295
  106.9 21.8 %all-to-all-start.4 = ((f32[64,1,640]{2,1,0:T(1,128)}), f32[64,1,640]{2,1,0:T(1,128)S(1)}, u32[]{:S(2)}, u32[]{:S(2)}) async-start(f32[64,1,640]{2,1,0:T(1,128)} %shard_map.92), calls=%async_computation.4 | async-start | bytes 327680 | tf_op jit(solution)/shard_map/all_to_all | solution.py:300
  114.3 4.9 %collective-permute-start.3 = (f32[224,384]{1,0:T(8,128)S(1)}, f32[224,384]{1,0:T(8,128)S(1)}, u32[]{:S(2)}, u32[]{:S(2)}) collective-permute-start(f32[224,384]{1,0:T(8,128)S(1)} %get-tuple-element.31), channel_id=1, source_target_pairs={{0,8},{8,0},{16,24},{24,16},{32,40},{40,32},{48,56},{56,48},{64,72... | collective-permute-start | bytes 1032200 | tf_op jit(solution)/shard_map/ppermute | solution.py:295
  128.8 6.9 %collective-permute-start.4 = (f32[64,1,640]{2,1,0:T(1,128)S(1)}, f32[64,1,640]{2,1,0:T(1,128)S(1)}, u32[]{:S(2)}, u32[]{:S(2)}) collective-permute-start(f32[64,1,640]{2,1,0:T(1,128)S(1)} %add.7), channel_id=1, source_target_pairs={{0,8},{8,0},{16,24},{24,16},{32,40},{40,32},{48,56},{56,48},{64,72... | collective-permute-start | bytes 491528 | tf_op jit(solution)/shard_map/ppermute | solution.py:295

commit v10 on v9

--- a/solution.py
+++ b/solution.py
@@ -202,27 +202,30 @@
 
 
 def grad_state_kernel(
-    q_ref, c_ref, gain_ref, got_ref, raw_ref, parts_ref, sum_ref, own_ref, other_ref
+    q_ref, c_ref, gain_ref, got_ref, raw_ref, parts_ref, sum_ref, late_q_ref, late_d_ref
 ):
     gain = pick(True, gain_ref[...])
     q, c = pick(True, q_ref[...]), pick(True, c_ref[...])
-    states = []
+    features, gradients = [], []
     for i, (q, c, totals) in enumerate(
         zip((q, got_ref[0].astype(BF16)), (c, got_ref[1]), own_and_other(parts_ref))
     ):
-        d_raw = gradient(c, gain, raw_ref[i], *scales(totals))
-        states.append(diagonal(mm(silu_low(q), d_raw, TN)))
-    own_ref[...], other_ref[...] = states
-    sum_ref[:, 0, :] = to_pieces(states[0] + states[1])
+        features.append(silu_low(q))
+        gradients.append(gradient(c, gain, raw_ref[i], *scales(totals)))
+    late_q_ref[...] = in_order(*features)[1]
+    late_d_ref[...] = in_order(*gradients)[1]
+    both = [jnp.concatenate(x, axis=0) for x in (features, gradients)]
+    sum_ref[:, 0, :] = to_pieces(diagonal(mm(*both, TN)))
 
 
 def back_kernel(
-    q_ref, k_ref, v_ref, c_ref, gain_ref, raw_ref, low_ref, got_ref, parts_ref, own_ref, other_ref,
+    q_ref, k_ref, v_ref, c_ref, gain_ref, raw_ref, low_ref, got_ref, parts_ref, late_q_ref, late_d_ref,
     attended_ref, grad_q_ref, grad_kf_ref, grad_vf_ref, here_ref, there_ref,
 ):
     core = core_index()
-    here_ref[...] = jnp.where(core == 0, other_ref[...], 0.0)
-    there_ref[:, 0, :] = to_pieces(jnp.where(core == 1, own_ref[...], 0.0))
+    late = diagonal(mm(late_q_ref[...], late_d_ref[...], TN))
+    here_ref[...] = jnp.where(core == 0, late, 0.0)
+    there_ref[:, 0, :] = to_pieces(jnp.where(core == 1, late, 0.0))
     keep = causal4()
     inverse, pull = scales(own_and_other(parts_ref)[0])
     raws = in_order(raw_ref[0], got_ref[0:TOK])
@@ -353,16 +356,16 @@
         queries, cotangent, gain, got, intra, chip, mine, received,
     )
     parts = over_heads(parts)
-    total, own, other = call(
+    total, late_q, late_d = call(
         grad_state_kernel,
-        [PIECES, STATE, STATE],
+        [PIECES, HALF_LOW, HALF_LOW],
         queries, cotangent, gain, got, raw, parts,
     )
     attended, grad_query, grad_kf, grad_vf, here, there = call(
         back_kernel,
         [WIDE_LOW, WIDE_LOW, WIDE, WIDE, STATE, PIECES],
         queries, key_input, value_input, cotangent, gain, raw, low, swap_cores(give), parts,
-        own, other,
+        late_q, late_d,
         flops=500_000_000,
     )
     (chip,) = scan(total, True)

time: 137 us -> 137 us (level)
  no operation moved by 1% of the time
where the time goes in v10:
time: 137 us
  blocking collectives  63.1 us (46%)
  starting transfers between devices  45.5 us (33%)
  waiting for transfers between devices  18 us (13%)
  Pallas kernels  7.94 us (6%)
  other arithmetic  1.4 us (1%)
    all_to_all x2, blocking collectives, across_chips(): return lax.all_to_all(x, 'ctx', 0, 0, axis_index_groups=groups)  45.6 us
    ppermute x5, starting transfers between devices, swap_cores(): return lax.ppermute(x, 'ctx', pairs)  30.9 us
    all_to_all x1, blocking collectives, over_heads(): return lax.all_to_all(x, ('ctx', 'head'), 0, 0, axis_index_groups=groups)  17.5 us
    all_to_all x2, starting transfers between devices, across_chips(): return lax.all_to_all(x, 'ctx', 0, 0, axis_index_groups=groups)  14.6 us
    all_to_all x2, waiting for transfers between devices, across_chips(): return lax.all_to_all(x, 'ctx', 0, 0, axis_index_groups=groups)  13.8 us
    pallas_call x11, Pallas kernels, call(): pl.pallas_call(kernel, out_shape=[jax.ShapeDtypeStruct(shape, kind) for s...  7.94 us
    ppermute x5, waiting for transfers between devices, swap_cores(): return lax.ppermute(x, 'ctx', pairs)  4.16 us
  transfers between devices with their start and end apart: 7, of which 6 were waited for; matrix products, arithmetic and copies ran while one was open for 0% of the time, Pallas kernels for 3%

profile of v10, /device:TPU:1, one launch (start us, length us, event | category | flops | bytes accessed | tf_op | source)
XLA Modules:
  0.0 136.8 jit_solution(13966138983815663051)
XLA Ops:
  0.6 1.1 pad_maximum_fusion.pair_ref
  1.7 0.4 shard_map.85
  2.1 16.1 %collective-permute-start = (f32[64,1,640]{2,1,0:T(1,128)S(1)}, f32[64,1,640]{2,1,0:T(1,128)S(1)}, u32[]{:S(2)}, u32[]{:S(2)}) collective-permute-start(f32[64,1,640]{2,1,0:T(1,128)S(1)} %shard_map.85), channel_id=1, source_target_pairs={{0,8},{8,0},{16,24},{24,16},{32,40},{40,32},{48,56},{56,48},{64,72... | collective-permute-start | bytes 491528 | tf_op jit(solution)/shard_map/ppermute | solution.py:298
  18.2 0.4 shard_map.84.mine_ref
  18.6 0.6 collective-permute-done.received_ref
  19.2 0.2 add.6
  19.3 0.0 copy-start.2
  19.3 0.0 copy-start.3
  19.4 25.0 %all_to_all.25.refs_0_ = f32[64,1,640]{2,1,0:T(1,128)S(1)} all-to-all(f32[64,1,640]{2,1,0:T(1,128)S(1)} %add.6), channel_id=1, replica_groups={{0,16,32,48,64,80,96,112,128,144,160,176,192,208,224,240,256,272,288,30..., dimensions={0} | all-to-all | bytes 327680 | tf_op jit(solution)/shard_map/all_to_all | solution.py:303
  44.4 0.0 copy-start.1
  44.4 0.7 shard_map.86
  45.1 0.0 copy-start
  45.1 7.2 %all-to-all-start.1 = ((f32[64,1,640]{2,1,0:T(1,128)}), f32[64,1,640]{2,1,0:T(1,128)S(1)}, u32[]{:S(2)}, u32[]{:S(2)}) async-start(f32[64,1,640]{2,1,0:T(1,128)} %get-tuple-element.28), calls=%async_computation.1 | async-start | bytes 327680 | tf_op jit(solution)/shard_map/all_to_all | solution.py:303
  52.3 0.0 copy-done.2
  52.3 0.0 copy-done.3
  52.3 0.0 copy-done.1
  52.3 0.0 copy-done
  52.3 0.0 copy-start.4
  52.3 0.1 shard_map.87
  52.4 3.4 %collective-permute-start.1 = (f32[2,128,384]{2,1,0:T(8,128)S(1)}, f32[2,128,384]{2,1,0:T(8,128)S(1)}, u32[]{:S(2)}, u32[]{:S(2)}) collective-permute-start(f32[2,128,384]{2,1,0:T(8,128)S(1)} %get-tuple-element.26), channel_id=1, source_target_pairs={{0,8},{8,0},{16,24},{24,16},{32,40},{40,32},{48,56},{56,48},{64,72... | collective-permute-start | bytes 1179656 | tf_op jit(solution)/shard_map/ppermute | solution.py:298
  55.8 1.9 %collective-permute-start.2 = (f32[2,128,384]{2,1,0:T(8,128)S(1)}, f32[2,128,384]{2,1,0:T(8,128)S(1)}, u32[]{:S(2)}, u32[]{:S(2)}) collective-permute-start(f32[2,128,384]{2,1,0:T(8,128)S(1)} %get-tuple-element.27), channel_id=1, source_target_pairs={{0,8},{8,0},{16,24},{24,16},{32,40},{40,32},{48,56},{56,48},{64,72... | collective-permute-start | bytes 1179656 | tf_op jit(solution)/shard_map/ppermute | solution.py:298
  57.7 0.0 copy-done.4
  57.7 0.0 collective-permute-done.1.got_qc_ref.got_ref
  57.8 1.7 %collective-permute-done.2.got_kv_ref = f32[2,128,384]{2,1,0:T(8,128)S(1)} collective-permute-done((f32[2,128,384]{2,1,0:T(8,128)S(1)}, f32[2,128,384]{2,1,0:T(8,128)S(1)}, u32[]{:S(2)}, u32[]{:S(2)}) %collective-permute-start.2) | collective-permute-done | bytes 393248 | tf_op jit(solution)/shard_map/ppermute | solution.py:298
  59.4 0.8 shard_map.88.intra_ref
  60.2 6.8 %all-to-all-done.1.chip_ref = f32[64,1,640]{2,1,0:T(1,128)S(1)} async-done(((f32[64,1,640]{2,1,0:T(1,128)}), f32[64,1,640]{2,1,0:T(1,128)S(1)}, u32[]{:S(2)}, u32[]{:S(2)}) %all-to-all-start.1) | async-done | bytes 163872 | tf_op jit(solution)/shard_map/all_to_all | solution.py:303
  67.0 0.5 shard_map.89
  67.5 17.5 %all_to_all.26.parts_ref = f32[16,4,128]{2,1,0:T(4,128)S(1)} all-to-all(f32[16,4,128]{2,1,0:T(4,128)S(1)} %get-tuple-element.32), channel_id=1, replica_groups={{0,1,2,3,4,5,6,7,8,9,10,11,12,13,14,15},{16,17,18,19,20,21,22,23,24,25,..., dimensions={0} | all-to-all | bytes 65536 | tf_op jit(solution)/shard_map/all_to_all | solution.py:309
  85.0 0.5 shard_map.90
  85.5 20.6 %all_to_all.27.refs_0_ = f32[64,1,640]{2,1,0:T(1,128)S(1)} all-to-all(f32[64,1,640]{2,1,0:T(1,128)S(1)} %get-tuple-element.39), channel_id=1, replica_groups={{0,16,32,48,64,80,96,112,128,144,160,176,192,208,224,240,256,272,288,30..., dimensions={0} | all-to-all | bytes 327680 | tf_op jit(solution)/shard_map/all_to_all | solution.py:303
  106.1 0.7 shard_map.92
  106.8 7.5 %all-to-all-start.4 = ((f32[64,1,640]{2,1,0:T(1,128)}), f32[64,1,640]{2,1,0:T(1,128)S(1)}, u32[]{:S(2)}, u32[]{:S(2)}) async-start(f32[64,1,640]{2,1,0:T(1,128)} %shard_map.92), calls=%async_computation.4 | async-start | bytes 327680 | tf_op jit(solution)/shard_map/all_to_all | solution.py:303
  114.3 3.6 %collective-permute-start.3 = (f32[224,384]{1,0:T(8,128)S(1)}, f32[224,384]{1,0:T(8,128)S(1)}, u32[]{:S(2)}, u32[]{:S(2)}) collective-permute-start(f32[224,384]{1,0:T(8,128)S(1)} %get-tuple-element.31), channel_id=1, source_target_pairs={{0,8},{8,0},{16,24},{24,16},{32,40},{40,32},{48,56},{56,48},{64,72... | collective-permute-start | bytes 1032200 | tf_op jit(solution)/shard_map/ppermute | solution.py:298
  118.0 1.3 collective-permute-done.3.got_ref
  119.2 2.4 %shard_map.91 = (bf16[128,768]{1,0:T(8,128)(2,1)}, bf16[128,768]{1,0:T(8,128)(2,1)}, f32[128,768]{1,0:T(8,128)S(1)}, f32[128,768]{1,0:T(8,128)S(1)}, f32[96,384]{1,0:T(8,128)S(1)}, /*index=5*/f32[64,1,640]{2,1,0:T(1,128)S(1)}) custom-call(bf16[128,768]{1,0:T(8,128)(2,1)S(1)} %copy-done.2, bf16[128,768]{1,0:T(8,128)(2,1)S(1)} %copy-done, ...), custom_call_target="tpu_custom_call" | custom-call | flops 500000000 | bytes 1000000 | tf_op jit(solution)/shard_map/pallas_call | solution.py:285
  121.6 7.0 %all-to-all-done.4.chip_ref = f32[64,1,640]{2,1,0:T(1,128)S(1)} async-done(((f32[64,1,640]{2,1,0:T(1,128)}), f32[64,1,640]{2,1,0:T(1,128)S(1)}, u32[]{:S(2)}, u32[]{:S(2)}) %all-to-all-start.4) | async-done | bytes 163872 | tf_op jit(solution)/shard_map/all_to_all | solution.py:303
  128.7 0.2 add.7
  128.8 5.9 %collective-permute-start.4 = (f32[64,1,640]{2,1,0:T(1,128)S(1)}, f32[64,1,640]{2,1,0:T(1,128)S(1)}, u32[]{:S(2)}, u32[]{:S(2)}) collective-permute-start(f32[64,1,640]{2,1,0:T(1,128)S(1)} %add.7), channel_id=1, source_target_pairs={{0,8},{8,0},{16,24},{24,16},{32,40},{40,32},{48,56},{56,48},{64,72... | collective-permute-start | bytes 491528 | tf_op jit(solution)/shard_map/ppermute | solution.py:298
  134.7 0.4 shard_map.93
  135.1 0.6 collective-permute-done.4.there_ref
  135.7 1.1 shard_map.94
  (1 shorter events, 0.0 us)
Async XLA Ops:
  2.1 17.1 %collective-permute-start = (f32[64,1,640]{2,1,0:T(1,128)S(1)}, f32[64,1,640]{2,1,0:T(1,128)S(1)}, u32[]{:S(2)}, u32[]{:S(2)}) collective-permute-start(f32[64,1,640]{2,1,0:T(1,128)S(1)} %shard_map.85), channel_id=1, source_target_pairs={{0,8},{8,0},{16,24},{24,16},{32,40},{40,32},{48,56},{56,48},{64,72... | collective-permute-start | bytes 491528 | tf_op jit(solution)/shard_map/ppermute | solution.py:298
  19.3 32.9 %copy-start.2 = (bf16[128,768]{1,0:T(8,128)(2,1)S(1)}, bf16[128,768]{1,0:T(8,128)(2,1)}, u32[]{:S(2)}) copy-start(bf16[128,768]{1,0:T(8,128)(2,1)} %q_ref.9) | copy-start | bytes 589828
  19.3 32.9 %copy-start.3 = (bf16[128,768]{1,0:T(8,128)(2,1)S(1)}, bf16[128,768]{1,0:T(8,128)(2,1)}, u32[]{:S(2)}) copy-start(bf16[128,768]{1,0:T(8,128)(2,1)} %c_ref.7) | copy-start | bytes 589828
  44.4 7.9 %copy-start.1 = (bf16[128,768]{1,0:T(8,128)(2,1)S(1)}, bf16[128,768]{1,0:T(8,128)(2,1)}, u32[]{:S(2)}) copy-start(bf16[128,768]{1,0:T(8,128)(2,1)} %v_ref.9) | copy-start | bytes 589828
  45.1 7.2 %copy-start = (bf16[128,768]{1,0:T(8,128)(2,1)S(1)}, bf16[128,768]{1,0:T(8,128)(2,1)}, u32[]{:S(2)}) copy-start(bf16[128,768]{1,0:T(8,128)(2,1)} %k_ref.9) | copy-start | bytes 589828
  45.1 21.9 %all-to-all-start.1 = ((f32[64,1,640]{2,1,0:T(1,128)}), f32[64,1,640]{2,1,0:T(1,128)S(1)}, u32[]{:S(2)}, u32[]{:S(2)}) async-start(f32[64,1,640]{2,1,0:T(1,128)} %get-tuple-element.28), calls=%async_computation.1 | async-start | bytes 327680 | tf_op jit(solution)/shard_map/all_to_all | solution.py:303
  52.3 5.4 %copy-start.4 = (f32[768]{0:T(1024)S(1)}, f32[768]{0:T(1024)}, u32[]{:S(2)}) copy-start(f32[768]{0:T(1024)} %param.8) | copy-start | bytes 9220
  52.4 5.3 %collective-permute-start.1 = (f32[2,128,384]{2,1,0:T(8,128)S(1)}, f32[2,128,384]{2,1,0:T(8,128)S(1)}, u32[]{:S(2)}, u32[]{:S(2)}) collective-permute-start(f32[2,128,384]{2,1,0:T(8,128)S(1)} %get-tuple-element.26), channel_id=1, source_target_pairs={{0,8},{8,0},{16,24},{24,16},{32,40},{40,32},{48,56},{56,48},{64,72... | collective-permute-start | bytes 1179656 | tf_op jit(solution)/shard_map/ppermute | solution.py:298
  55.8 3.6 %collective-permute-start.2 = (f32[2,128,384]{2,1,0:T(8,128)S(1)}, f32[2,128,384]{2,1,0:T(8,128)S(1)}, u32[]{:S(2)}, u32[]{:S(2)}) collective-permute-start(f32[2,128,384]{2,1,0:T(8,128)S(1)} %get-tuple-element.27), channel_id=1, source_target_pairs={{0,8},{8,0},{16,24},{24,16},{32,40},{40,32},{48,56},{56,48},{64,72... | collective-permute-start | bytes 1179656 | tf_op jit(solution)/shard_map/ppermute | solution.py:298
  106.8 21.8 %all-to-all-start.4 = ((f32[64,1,640]{2,1,0:T(1,128)}), f32[64,1,640]{2,1,0:T(1,128)S(1)}, u32[]{:S(2)}, u32[]{:S(2)}) async-start(f32[64,1,640]{2,1,0:T(1,128)} %shard_map.92), calls=%async_computation.4 | async-start | bytes 327680 | tf_op jit(solution)/shard_map/all_to_all | solution.py:303
  114.3 4.9 %collective-permute-start.3 = (f32[224,384]{1,0:T(8,128)S(1)}, f32[224,384]{1,0:T(8,128)S(1)}, u32[]{:S(2)}, u32[]{:S(2)}) collective-permute-start(f32[224,384]{1,0:T(8,128)S(1)} %get-tuple-element.31), channel_id=1, source_target_pairs={{0,8},{8,0},{16,24},{24,16},{32,40},{40,32},{48,56},{56,48},{64,72... | collective-permute-start | bytes 1032200 | tf_op jit(solution)/shard_map/ppermute | solution.py:298
  128.8 6.9 %collective-permute-start.4 = (f32[64,1,640]{2,1,0:T(1,128)S(1)}, f32[64,1,640]{2,1,0:T(1,128)S(1)}, u32[]{:S(2)}, u32[]{:S(2)}) collective-permute-start(f32[64,1,640]{2,1,0:T(1,128)S(1)} %add.7), channel_id=1, source_target_pairs={{0,8},{8,0},{16,24},{24,16},{32,40},{40,32},{48,56},{56,48},{64,72... | collective-permute-start | bytes 491528 | tf_op jit(solution)/shard_map/ppermute | solution.py:298

commit v11 on v9

--- a/solution.py
+++ b/solution.py
@@ -301,8 +301,11 @@
 
 
 def over_heads(x):
-    size = CORES * lax.axis_size("head")
-    groups = [[chip * size + i for i in range(size)] for chip in range(CHIPS)]
+    size = lax.axis_size("head")
+    groups = [
+        [(chip * CORES + core) * size + i for i in range(size) for core in range(CORES)]
+        for chip in range(CHIPS)
+    ]
     return lax.all_to_all(x, ("ctx", "head"), 0, 0, axis_index_groups=groups)
 
 

time: 137 us -> 138 us (level)
  no operation moved by 1% of the time
where the time goes in v11:
time: 138 us; the launch traced here: 137 us
  blocking collectives  64.2 us (47%)
  starting transfers between devices  44.3 us (32%)
  waiting for transfers between devices  18.6 us (13%)
  Pallas kernels  7.94 us (6%)
  other arithmetic  1.4 us (1%)
    all_to_all x2, blocking collectives, across_chips(): return lax.all_to_all(x, 'ctx', 0, 0, axis_index_groups=groups)  46.4 us
    ppermute x5, starting transfers between devices, swap_cores(): return lax.ppermute(x, 'ctx', pairs)  30.1 us
    all_to_all x1, blocking collectives, over_heads(): return lax.all_to_all(x, ('ctx', 'head'), 0, 0, axis_index_groups=groups)  17.8 us
    all_to_all x2, waiting for transfers between devices, across_chips(): return lax.all_to_all(x, 'ctx', 0, 0, axis_index_groups=groups)  14.4 us
    all_to_all x2, starting transfers between devices, across_chips(): return lax.all_to_all(x, 'ctx', 0, 0, axis_index_groups=groups)  14.2 us
    pallas_call x11, Pallas kernels, call(): pl.pallas_call(kernel, out_shape=[jax.ShapeDtypeStruct(shape, kind) for s...  7.94 us
    ppermute x5, waiting for transfers between devices, swap_cores(): return lax.ppermute(x, 'ctx', pairs)  4.15 us
  transfers between devices with their start and end apart: 7, of which 6 were waited for; matrix products, arithmetic and copies ran while one was open for 0% of the time, Pallas kernels for 3%

profile of v11, /device:TPU:1, one launch (start us, length us, event | category | flops | bytes accessed | tf_op | source)
XLA Modules:
  0.0 137.3 jit_solution(14990392802546543295)
XLA Ops:
  0.6 1.1 pad_maximum_fusion.pair_ref
  1.7 0.4 shard_map.85
  2.1 16.1 %collective-permute-start = (f32[64,1,640]{2,1,0:T(1,128)S(1)}, f32[64,1,640]{2,1,0:T(1,128)S(1)}, u32[]{:S(2)}, u32[]{:S(2)}) collective-permute-start(f32[64,1,640]{2,1,0:T(1,128)S(1)} %shard_map.85), channel_id=1, source_target_pairs={{0,8},{8,0},{16,24},{24,16},{32,40},{40,32},{48,56},{56,48},{64,72... | collective-permute-start | bytes 491528 | tf_op jit(solution)/shard_map/ppermute | solution.py:295
  18.2 0.4 shard_map.84.mine_ref
  18.6 0.6 collective-permute-done.received_ref
  19.2 0.2 add.6
  19.3 0.0 copy-start.2
  19.3 0.0 copy-start.3
  19.4 25.0 %all_to_all.25.refs_0_ = f32[64,1,640]{2,1,0:T(1,128)S(1)} all-to-all(f32[64,1,640]{2,1,0:T(1,128)S(1)} %add.6), channel_id=1, replica_groups={{0,16,32,48,64,80,96,112,128,144,160,176,192,208,224,240,256,272,288,30..., dimensions={0} | all-to-all | bytes 327680 | tf_op jit(solution)/shard_map/all_to_all | solution.py:300
  44.4 0.0 copy-start.1
  44.4 0.7 shard_map.86
  45.1 0.0 copy-start
  45.1 7.2 %all-to-all-start.1 = ((f32[64,1,640]{2,1,0:T(1,128)}), f32[64,1,640]{2,1,0:T(1,128)S(1)}, u32[]{:S(2)}, u32[]{:S(2)}) async-start(f32[64,1,640]{2,1,0:T(1,128)} %get-tuple-element.28), calls=%async_computation.1 | async-start | bytes 327680 | tf_op jit(solution)/shard_map/all_to_all | solution.py:300
  52.3 0.0 copy-done.2
  52.3 0.0 copy-done.3
  52.3 0.0 copy-done.1
  52.3 0.0 copy-done
  52.3 0.0 copy-start.4
  52.3 0.1 shard_map.87
  52.4 3.4 %collective-permute-start.1 = (f32[2,128,384]{2,1,0:T(8,128)S(1)}, f32[2,128,384]{2,1,0:T(8,128)S(1)}, u32[]{:S(2)}, u32[]{:S(2)}) collective-permute-start(f32[2,128,384]{2,1,0:T(8,128)S(1)} %get-tuple-element.26), channel_id=1, source_target_pairs={{0,8},{8,0},{16,24},{24,16},{32,40},{40,32},{48,56},{56,48},{64,72... | collective-permute-start | bytes 1179656 | tf_op jit(solution)/shard_map/ppermute | solution.py:295
  55.8 1.9 %collective-permute-start.2 = (f32[2,128,384]{2,1,0:T(8,128)S(1)}, f32[2,128,384]{2,1,0:T(8,128)S(1)}, u32[]{:S(2)}, u32[]{:S(2)}) collective-permute-start(f32[2,128,384]{2,1,0:T(8,128)S(1)} %get-tuple-element.27), channel_id=1, source_target_pairs={{0,8},{8,0},{16,24},{24,16},{32,40},{40,32},{48,56},{56,48},{64,72... | collective-permute-start | bytes 1179656 | tf_op jit(solution)/shard_map/ppermute | solution.py:295
  57.7 0.0 copy-done.4
  57.7 0.0 collective-permute-done.1.got_qc_ref.got_ref
  57.8 1.7 %collective-permute-done.2.got_kv_ref = f32[2,128,384]{2,1,0:T(8,128)S(1)} collective-permute-done((f32[2,128,384]{2,1,0:T(8,128)S(1)}, f32[2,128,384]{2,1,0:T(8,128)S(1)}, u32[]{:S(2)}, u32[]{:S(2)}) %collective-permute-start.2) | collective-permute-done | bytes 393248 | tf_op jit(solution)/shard_map/ppermute | solution.py:295
  59.4 0.8 shard_map.88.intra_ref
  60.2 6.8 %all-to-all-done.1.chip_ref = f32[64,1,640]{2,1,0:T(1,128)S(1)} async-done(((f32[64,1,640]{2,1,0:T(1,128)}), f32[64,1,640]{2,1,0:T(1,128)S(1)}, u32[]{:S(2)}, u32[]{:S(2)}) %all-to-all-start.1) | async-done | bytes 163872 | tf_op jit(solution)/shard_map/all_to_all | solution.py:300
  67.0 0.5 shard_map.89
  67.5 17.8 %all_to_all.26.parts_ref = f32[16,4,128]{2,1,0:T(4,128)S(1)} all-to-all(f32[16,4,128]{2,1,0:T(4,128)S(1)} %get-tuple-element.32), channel_id=1, replica_groups={{0,8,1,9,2,10,3,11,4,12,5,13,6,14,7,15},{16,24,17,25,18,26,19,27,20,28,..., dimensions={0} | all-to-all | bytes 65536 | tf_op jit(solution)/shard_map/all_to_all | solution.py:309
  85.3 0.5 shard_map.90
  85.8 21.4 %all_to_all.27.refs_0_ = f32[64,1,640]{2,1,0:T(1,128)S(1)} all-to-all(f32[64,1,640]{2,1,0:T(1,128)S(1)} %get-tuple-element.39), channel_id=1, replica_groups={{0,16,32,48,64,80,96,112,128,144,160,176,192,208,224,240,256,272,288,30..., dimensions={0} | all-to-all | bytes 327680 | tf_op jit(solution)/shard_map/all_to_all | solution.py:300
  107.2 0.7 shard_map.92
  107.9 7.0 %all-to-all-start.4 = ((f32[64,1,640]{2,1,0:T(1,128)}), f32[64,1,640]{2,1,0:T(1,128)S(1)}, u32[]{:S(2)}, u32[]{:S(2)}) async-start(f32[64,1,640]{2,1,0:T(1,128)} %shard_map.92), calls=%async_computation.4 | async-start | bytes 327680 | tf_op jit(solution)/shard_map/all_to_all | solution.py:300
  114.9 3.4 %collective-permute-start.3 = (f32[224,384]{1,0:T(8,128)S(1)}, f32[224,384]{1,0:T(8,128)S(1)}, u32[]{:S(2)}, u32[]{:S(2)}) collective-permute-start(f32[224,384]{1,0:T(8,128)S(1)} %get-tuple-element.31), channel_id=1, source_target_pairs={{0,8},{8,0},{16,24},{24,16},{32,40},{40,32},{48,56},{56,48},{64,72... | collective-permute-start | bytes 1032200 | tf_op jit(solution)/shard_map/ppermute | solution.py:295
  118.3 1.3 collective-permute-done.3.got_ref
  119.6 2.4 %shard_map.91 = (bf16[128,768]{1,0:T(8,128)(2,1)}, bf16[128,768]{1,0:T(8,128)(2,1)}, f32[128,768]{1,0:T(8,128)S(1)}, f32[128,768]{1,0:T(8,128)S(1)}, f32[96,384]{1,0:T(8,128)S(1)}, /*index=5*/f32[64,1,640]{2,1,0:T(1,128)S(1)}) custom-call(bf16[128,768]{1,0:T(8,128)(2,1)S(1)} %copy-done.2, bf16[128,768]{1,0:T(8,128)(2,1)S(1)} %copy-done, ...), custom_call_target="tpu_custom_call" | custom-call | flops 500000000 | bytes 1000000 | tf_op jit(solution)/shard_map/pallas_call | solution.py:282
  122.0 7.7 %all-to-all-done.4.chip_ref = f32[64,1,640]{2,1,0:T(1,128)S(1)} async-done(((f32[64,1,640]{2,1,0:T(1,128)}), f32[64,1,640]{2,1,0:T(1,128)S(1)}, u32[]{:S(2)}, u32[]{:S(2)}) %all-to-all-start.4) | async-done | bytes 163872 | tf_op jit(solution)/shard_map/all_to_all | solution.py:300
  129.6 0.2 add.7
  129.8 5.4 %collective-permute-start.4 = (f32[64,1,640]{2,1,0:T(1,128)S(1)}, f32[64,1,640]{2,1,0:T(1,128)S(1)}, u32[]{:S(2)}, u32[]{:S(2)}) collective-permute-start(f32[64,1,640]{2,1,0:T(1,128)S(1)} %add.7), channel_id=1, source_target_pairs={{0,8},{8,0},{16,24},{24,16},{32,40},{40,32},{48,56},{56,48},{64,72... | collective-permute-start | bytes 491528 | tf_op jit(solution)/shard_map/ppermute | solution.py:295
  135.2 0.4 shard_map.93
  135.6 0.6 collective-permute-done.4.there_ref
  136.2 1.1 shard_map.94
  (1 shorter events, 0.0 us)
Async XLA Ops:
  2.1 17.1 %collective-permute-start = (f32[64,1,640]{2,1,0:T(1,128)S(1)}, f32[64,1,640]{2,1,0:T(1,128)S(1)}, u32[]{:S(2)}, u32[]{:S(2)}) collective-permute-start(f32[64,1,640]{2,1,0:T(1,128)S(1)} %shard_map.85), channel_id=1, source_target_pairs={{0,8},{8,0},{16,24},{24,16},{32,40},{40,32},{48,56},{56,48},{64,72... | collective-permute-start | bytes 491528 | tf_op jit(solution)/shard_map/ppermute | solution.py:295
  19.3 32.9 %copy-start.2 = (bf16[128,768]{1,0:T(8,128)(2,1)S(1)}, bf16[128,768]{1,0:T(8,128)(2,1)}, u32[]{:S(2)}) copy-start(bf16[128,768]{1,0:T(8,128)(2,1)} %q_ref.9) | copy-start | bytes 589828
  19.3 32.9 %copy-start.3 = (bf16[128,768]{1,0:T(8,128)(2,1)S(1)}, bf16[128,768]{1,0:T(8,128)(2,1)}, u32[]{:S(2)}) copy-start(bf16[128,768]{1,0:T(8,128)(2,1)} %c_ref.7) | copy-start | bytes 589828
  44.4 7.9 %copy-start.1 = (bf16[128,768]{1,0:T(8,128)(2,1)S(1)}, bf16[128,768]{1,0:T(8,128)(2,1)}, u32[]{:S(2)}) copy-start(bf16[128,768]{1,0:T(8,128)(2,1)} %v_ref.9) | copy-start | bytes 589828
  45.1 7.2 %copy-start = (bf16[128,768]{1,0:T(8,128)(2,1)S(1)}, bf16[128,768]{1,0:T(8,128)(2,1)}, u32[]{:S(2)}) copy-start(bf16[128,768]{1,0:T(8,128)(2,1)} %k_ref.9) | copy-start | bytes 589828
  45.1 21.9 %all-to-all-start.1 = ((f32[64,1,640]{2,1,0:T(1,128)}), f32[64,1,640]{2,1,0:T(1,128)S(1)}, u32[]{:S(2)}, u32[]{:S(2)}) async-start(f32[64,1,640]{2,1,0:T(1,128)} %get-tuple-element.28), calls=%async_computation.1 | async-start | bytes 327680 | tf_op jit(solution)/shard_map/all_to_all | solution.py:300
  52.3 5.4 %copy-start.4 = (f32[768]{0:T(1024)S(1)}, f32[768]{0:T(1024)}, u32[]{:S(2)}) copy-start(f32[768]{0:T(1024)} %param.8) | copy-start | bytes 9220
  52.4 5.3 %collective-permute-start.1 = (f32[2,128,384]{2,1,0:T(8,128)S(1)}, f32[2,128,384]{2,1,0:T(8,128)S(1)}, u32[]{:S(2)}, u32[]{:S(2)}) collective-permute-start(f32[2,128,384]{2,1,0:T(8,128)S(1)} %get-tuple-element.26), channel_id=1, source_target_pairs={{0,8},{8,0},{16,24},{24,16},{32,40},{40,32},{48,56},{56,48},{64,72... | collective-permute-start | bytes 1179656 | tf_op jit(solution)/shard_map/ppermute | solution.py:295
  55.8 3.6 %collective-permute-start.2 = (f32[2,128,384]{2,1,0:T(8,128)S(1)}, f32[2,128,384]{2,1,0:T(8,128)S(1)}, u32[]{:S(2)}, u32[]{:S(2)}) collective-permute-start(f32[2,128,384]{2,1,0:T(8,128)S(1)} %get-tuple-element.27), channel_id=1, source_target_pairs={{0,8},{8,0},{16,24},{24,16},{32,40},{40,32},{48,56},{56,48},{64,72... | collective-permute-start | bytes 1179656 | tf_op jit(solution)/shard_map/ppermute | solution.py:295
  107.9 21.7 %all-to-all-start.4 = ((f32[64,1,640]{2,1,0:T(1,128)}), f32[64,1,640]{2,1,0:T(1,128)S(1)}, u32[]{:S(2)}, u32[]{:S(2)}) async-start(f32[64,1,640]{2,1,0:T(1,128)} %shard_map.92), calls=%async_computation.4 | async-start | bytes 327680 | tf_op jit(solution)/shard_map/all_to_all | solution.py:300
  114.9 4.6 %collective-permute-start.3 = (f32[224,384]{1,0:T(8,128)S(1)}, f32[224,384]{1,0:T(8,128)S(1)}, u32[]{:S(2)}, u32[]{:S(2)}) collective-permute-start(f32[224,384]{1,0:T(8,128)S(1)} %get-tuple-element.31), channel_id=1, source_target_pairs={{0,8},{8,0},{16,24},{24,16},{32,40},{40,32},{48,56},{56,48},{64,72... | collective-permute-start | bytes 1032200 | tf_op jit(solution)/shard_map/ppermute | solution.py:295
  129.8 6.4 %collective-permute-start.4 = (f32[64,1,640]{2,1,0:T(1,128)S(1)}, f32[64,1,640]{2,1,0:T(1,128)S(1)}, u32[]{:S(2)}, u32[]{:S(2)}) collective-permute-start(f32[64,1,640]{2,1,0:T(1,128)S(1)} %add.7), channel_id=1, source_target_pairs={{0,8},{8,0},{16,24},{24,16},{32,40},{40,32},{48,56},{56,48},{64,72... | collective-permute-start | bytes 491528 | tf_op jit(solution)/shard_map/ppermute | solution.py:295
